TPU v7x, 32 devices: a whole 2x2x4 slice. The times are simulated.
32 devices in a mesh: groups: 2 (over y), ctx: 4 (over z), dp: 2 (over x), head: 2 (over core).
Axes of the slice: x: 2, y: 2, z: 4, core: 2. Of those that a mesh axis runs over, the one named last changes fastest.
Arguments:
- queries: bfloat16 [4, 1024, 2048], P(('groups', 'dp'), 'ctx', 'head'), parts along dimension 0, may hold values from -6.2 to 6.2
- keys: bfloat16 [4, 1024, 512], P(('groups', 'dp'), 'ctx', 'head'), parts along dimension 0, may hold values from -6.2 to 6.2
- values: bfloat16 [4, 1024, 512], P(('groups', 'dp'), 'ctx', 'head'), parts along dimension 0, may hold values from -6 to 6
- tok_ids: int32 [4, 1024], P(('groups', 'dp'), 'ctx'), parts along dimension 0, may hold values from 0 to 15, never falling along the last dimension, each value on 1 to 128 neighbouring positions
- vis_start: int32 [4, 4], P(('groups', 'dp'), 'ctx'), parts along dimension 0, may hold values from 0 to 3, as said below
- out_weight: bfloat16 [4096, 2048], P('dp', 'head'), may hold values from -0.125 to 0.125
- grad_out: bfloat16 [4, 1024, 4096], P(('groups', 'dp'), 'ctx'), parts along dimension 0, may hold values from -6 to 6
Outputs:
- grad_q: bfloat16 [4, 1024, 2048], P(('groups', 'dp'), 'ctx', 'head'), parts along dimension 0
- key_gradient: bfloat16 [4, 1024, 512], P(('groups', 'dp'), 'ctx', 'head'), parts along dimension 0
- value_gradient: bfloat16 [4, 1024, 512], P(('groups', 'dp'), 'ctx', 'head'), parts along dimension 0
- weight_grad: bfloat16 [8192, 2048], P(('groups', 'dp'), 'head'), parts along dimension 0
There are 2 independent parts, one for each index of `groups`. A program takes and returns all parts, laid end to end along the dimension named above; an argument that names none is the same for every part. Nothing has to cross between parts.
Inputs may be any that keep to these rules, and one draw needn't show every extreme that they name: vis_start[b, j] lies between 0 and j, and vis_start[b, 0] is 0.
All inputs are finite; a program needn't handle non-finite values.
Results may differ from a plain program's by a relative error of at most 0.011.
Values may be sent and summed in bfloat16 or wider, within the bound.
No kernel may reach another device: no remote copies, remote signals or barrier semaphores. Data moves between devices by JAX's collectives and lax.ppermute only.
A program may use at most 128 MiB of HBM per device.

v0:
```python
import jax
import jax.numpy as jnp
from jax import lax
from jax.sharding import PartitionSpec as P

HEAD_SIZE = 128
SUMMARY_TOKENS = 64


NEG_FILL = -1e30


def one_head(inputs, allowed):
    q_head, k_head, v_head, d_head = inputs
    scale = HEAD_SIZE ** (-0.5)
    scores = jnp.einsum("sgd,kd->gsk", q_head, k_head, preferred_element_type=jnp.float32) * scale
    scores = jnp.where(allowed[None], scores, NEG_FILL)
    top = jnp.max(scores, axis=-1, keepdims=True)
    expo = jnp.exp(scores - top)
    prob = expo / jnp.sum(expo, axis=-1, keepdims=True)
    probs_b = prob.astype(jnp.bfloat16)
    attn = jnp.einsum("gsk,kd->sgd", probs_b, v_head, preferred_element_type=jnp.float32).astype(
        jnp.bfloat16
    )
    delta = jnp.sum(d_head.astype(jnp.float32) * attn.astype(jnp.float32), axis=-1)
    dprob = jnp.einsum("sgd,kd->gsk", d_head, v_head, preferred_element_type=jnp.float32)
    dscore = prob * (dprob - jnp.transpose(delta)[:, :, None])
    ds_b = dscore.astype(jnp.bfloat16)
    grad_q = (
        scale * jnp.einsum("gsk,kd->sgd", ds_b, k_head, preferred_element_type=jnp.float32)
    ).astype(jnp.bfloat16)
    key_gradient = scale * jnp.einsum(
        "gsk,sgd->kd", ds_b, q_head, preferred_element_type=jnp.float32
    )
    value_gradient = jnp.einsum("gsk,sgd->kd", probs_b, d_head, preferred_element_type=jnp.float32)
    return (attn, grad_q, key_gradient, value_gradient)


def shards(queries, keys, values, tok_ids, vis_start, out_weight, grad_out):
    seg_len = queries.shape[1]
    q_width = queries.shape[2]
    kv_width = keys.shape[2]
    kv_heads = kv_width // HEAD_SIZE
    head_groups = q_width // kv_width
    d_model = grad_out.shape[2]
    n_ctx = lax.axis_size("ctx")
    n_dp = lax.axis_size("dp")
    place = lax.axis_index("ctx")
    grad_rows = grad_out[0]
    columns = grad_rows
    d_attn = jnp.dot(
        columns,
        lax.all_gather(out_weight, "dp", axis=0, tiled=True),
        preferred_element_type=jnp.float32,
    ).astype(jnp.bfloat16)
    summ_keys, summ_vals = (
        lax.all_gather(keys[0, seg_len - SUMMARY_TOKENS :], "ctx", axis=0, tiled=True),
        lax.all_gather(values[0, seg_len - SUMMARY_TOKENS :], "ctx", axis=0, tiled=True),
    )
    n_summ = summ_keys.shape[0]
    all_keys = jnp.concatenate([keys[0], summ_keys], 0)
    all_vals = jnp.concatenate([values[0], summ_vals], 0)
    token_ids = tok_ids[0]
    positions = jnp.arange(seg_len, dtype=jnp.int32)
    own = (positions[:, None] >= positions[None, :]) & (token_ids[:, None] == token_ids[None, :])
    summ_seg = jnp.arange(n_summ, dtype=jnp.int32) // SUMMARY_TOKENS
    seen = (summ_seg >= vis_start[0, 0]) & (summ_seg < place)
    allowed = jnp.concatenate([own, jnp.broadcast_to(seen[None, :], (seg_len, n_summ))], axis=1)
    query_head_count = (
        queries[0].reshape(seg_len, kv_heads, head_groups, HEAD_SIZE).transpose(1, 0, 2, 3)
    )
    head_dimension = d_attn.reshape(seg_len, kv_heads, head_groups, HEAD_SIZE).transpose(1, 0, 2, 3)
    key_head_count = all_keys.reshape(-1, kv_heads, HEAD_SIZE).transpose(1, 0, 2)
    value_head_count = all_vals.reshape(-1, kv_heads, HEAD_SIZE).transpose(1, 0, 2)
    attn, grad_q, key_gradient, value_gradient = lax.map(
        lambda inputs: one_head(inputs, allowed),
        (query_head_count, key_head_count, value_head_count, head_dimension),
    )
    attn_rows = attn.transpose(1, 0, 2, 3).reshape(seg_len, q_width)
    grad_q = grad_q.transpose(1, 0, 2, 3).reshape(seg_len, q_width)
    key_gradient = key_gradient.transpose(1, 0, 2).reshape(-1, kv_width)
    value_gradient = value_gradient.transpose(1, 0, 2).reshape(-1, kv_width)
    far_k = key_gradient[seg_len:]
    far_v = value_gradient[seg_len:]
    back_k, back_v = (
        lax.psum_scatter(far_k, "ctx", scatter_dimension=0, tiled=True),
        lax.psum_scatter(far_v, "ctx", scatter_dimension=0, tiled=True),
    )
    cut = seg_len - SUMMARY_TOKENS
    out_k = jnp.concatenate([key_gradient[:cut], key_gradient[cut:seg_len] + back_k], 0).astype(
        jnp.bfloat16
    )
    out_v = jnp.concatenate([value_gradient[:cut], value_gradient[cut:seg_len] + back_v], 0).astype(
        jnp.bfloat16
    )
    block = d_model // (n_ctx * n_dp)
    reordered = (
        grad_rows.reshape(seg_len, n_dp, n_ctx, block)
        .transpose(0, 2, 1, 3)
        .reshape(seg_len, d_model)
    )
    columns = reordered
    shard = lax.psum_scatter(
        jnp.einsum("sd,se->de", columns, attn_rows, preferred_element_type=jnp.float32),
        ("ctx", "dp"),
        scatter_dimension=0,
        tiled=True,
    ).astype(jnp.bfloat16)
    weight_grad = lax.all_gather(shard, "ctx", axis=0, tiled=True)
    return (grad_q[None], out_k[None], out_v[None], weight_grad)


def solution(mesh):
    placed = (
        P(("groups", "dp"), "ctx", "head"),
        P(("groups", "dp"), "ctx", "head"),
        P(("groups", "dp"), "ctx", "head"),
        P(("groups", "dp"), "ctx"),
        P(("groups", "dp"), "ctx"),
        P("dp", "head"),
        P(("groups", "dp"), "ctx", None),
    )
    return jax.shard_map(
        shards,
        mesh=mesh,
        in_specs=placed,
        out_specs=(
            P(("groups", "dp"), "ctx", "head"),
            P(("groups", "dp"), "ctx", "head"),
            P(("groups", "dp"), "ctx", "head"),
            P(("groups", "dp"), "head"),
        ),
        check_vma=False,
    )
```

profile of v0, /device:TPU:0, one launch (start us, length us, event | category | flops | bytes accessed | tf_op | source)
XLA Modules:
  0.0 564.7 jit_solution(15795330385928336685)
XLA Ops:
  7.3 0.7 all-gather.5.cloned.1.call-update
  9.1 15.1 %all-gather = bf16[1,256,256]{2,1,0:T(8,128)(2,1)S(1)} all-gather(bf16[1,64,256]{2,1,0:T(8,128)(2,1)S(1)} %slice-done.1), channel_id=2, replica_groups=mesh['groups'=2,'ctx'=4,'dp'=2,'head'=2] {'ctx'}, dimensions={1}, use_global_device_ids=true | all-gather | bytes 163840 | tf_op jit(solution)/shard_map/all_gather | solution.py:58
  24.2 13.5 %all-gather.1 = bf16[1,256,256]{2,1,0:T(8,128)(2,1)S(1)} all-gather(bf16[1,64,256]{2,1,0:T(8,128)(2,1)S(1)} %slice-done), channel_id=3, replica_groups=mesh['groups'=2,'ctx'=4,'dp'=2,'head'=2] {'ctx'}, dimensions={1}, use_global_device_ids=true | all-gather | bytes 163840 | tf_op jit(solution)/shard_map/all_gather | solution.py:57
  38.1 3.3 copy.95
  41.4 1.5 copy.96
  42.9 0.7 maximum_bitcast_fusion
  43.9 72.5 %all-gather.5.cloned.1.call-done = bf16[4096,1024]{1,0:T(8,128)(2,1)} async-done(((bf16[2048,1024]{1,0:T(8,128)(2,1)}), bf16[4096,1024]{1,0:T(8,128)(2,1)}) %all-gather.5.cloned.1.call-update) | async-done | bytes 8388624 | tf_op jit(solution)/shard_map/all_gather | solution.py:53
  116.3 6.3 %fusion.56 = bf16[256,1024]{1,0:T(8,128)(2,1)S(1)} fusion(bf16[4096,1024]{1,0:T(8,128)(2,1)} %all-gather.5.cloned.1.call-done, bf16[1,256,4096]{2,1,0:T(8,128)(2,1)} %param.15), kind=kOutput, calls=%fused_computation.56 | convolution fusion | flops 2147745792 | bytes 11010048 | tf_op jit(solution)/shard_map/dot_general | solution.py:51
  122.9 13.8 %while.16 = (s32[]{:T(128)}, bf16[2,256,4,128]{1,3,2,0:T(8,128)(2,1)}, bf16[2,256,4,128]{1,3,2,0:T(8,128)(2,1)}, f32[2,512,128]{2,1,0:T(8,128)}, f32[2,512,128]{...) while((s32[]{:T(128)}, ...), condition=%wide.region_4.5_spmd, body=%wide.region_0.4_spmd.sunk | while | flops 811531776 | bytes 33974644 | solution.py:75
  122.9 1.8 fusion.104
  124.9 0.8 copy-done.7
  126.6 0.5 fusion.106
  129.0 0.8 copy-done.5
  129.8 1.8 fusion.104
  131.8 0.8 copy-done.7
  133.5 0.5 fusion.106
  135.9 0.8 copy-done.5
  136.7 9.9 %convolution_bitcast_fusion.2 = f32[4096,1024]{0,1:T(8,128)} fusion(bf16[256,1024]{0,1:T(8,128)(2,1)} %bitcast.213, bf16[256,4096]{0,1:T(8,128)(2,1)} %bitcast.210), kind=kOutput, calls=%fused_computation.53 | convolution fusion | flops 2147483648 | bytes 19398656 | tf_op jit(solution)/shard_map/sd,se->de/dot_general | solution.py:104
  146.7 1.0 copy-done.9
  147.6 0.7 copy_bitcast_fusion
  148.4 0.7 copy_bitcast_fusion.1
  149.2 280.3 %reduce-scatter.8.cloned.1.call-done = f32[512,1024]{0,1:T(8,128)} async-done(((f32[4096,1024]{0,1:T(8,128)}), f32[512,1024]{0,1:T(8,128)}) %reduce-scatter.8.cloned.1.call-update) | async-done | bytes 2097168 | tf_op jit(solution)/shard_map/reduce_scatter | solution.py:103
  429.5 2.7 convert_element_type.47
  432.7 1.0 copy.107
  433.7 16.9 %reduce-scatter.6.cloned.1.call-done = f32[64,256]{1,0:T(8,128)} async-done(((f32[256,256]{1,0:T(8,128)}), f32[64,256]{1,0:T(8,128)}) %reduce-scatter.6.cloned.1.call-update) | async-done | bytes 65552 | tf_op jit(solution)/shard_map/reduce_scatter | solution.py:87
  450.5 0.8 fusion.63
  451.4 0.7 pad_maximum_fusion.1
  452.0 18.6 %reduce-scatter.4.cloned.1.call-done = f32[64,256]{1,0:T(8,128)} async-done(((f32[256,256]{1,0:T(8,128)}), f32[64,256]{1,0:T(8,128)}) %reduce-scatter.4.cloned.1.call-update) | async-done | bytes 65552 | tf_op jit(solution)/shard_map/reduce_scatter | solution.py:86
  470.6 0.8 fusion.62
  471.5 0.7 pad_maximum_fusion
  472.2 79.6 %all-gather.7.cloned.1.call-done = bf16[2048,1024]{0,1:T(8,128)(2,1)} async-done(((bf16[512,1024]{0,1:T(8,128)(2,1)}), bf16[2048,1024]{0,1:T(8,128)(2,1)}) %all-gather.7.cloned.1.call-update) | async-done | bytes 4194320 | tf_op jit(solution)/shard_map/all_gather | solution.py:109
  551.7 6.4 %copy.97 = bf16[2048,1024]{1,0:T(8,128)(2,1)} copy(bf16[2048,1024]{0,1:T(8,128)(2,1)} %all-gather.7.cloned.1.call-done) | data formatting | bytes 8388608
  (90 shorter events, 7.6 us)
Async XLA Ops:
  7.2 1.0 copy-start.13
  7.2 17.0 %slice-start = ((bf16[1,256,256]{2,1,0:T(8,128)(2,1)}), bf16[1,64,256]{2,1,0:T(8,128)(2,1)S(1)}, s32[]{:S(2)}) async-start(bf16[1,256,256]{2,1,0:T(8,128)(2,1)} %param.10), calls=%async_computation.8 | async-start | bytes 65536 | tf_op jit(solution)/shard_map/slice | solution.py:57
  7.2 1.1 copy-start.14
  7.2 1.9 slice-start.1
  7.2 30.7 %copy-start.3 = (bf16[1,256,1024]{2,1,0:T(8,128)(2,1)S(1)}, bf16[1,256,1024]{2,1,0:T(8,128)(2,1)}, u32[]{:S(2)}) copy-start(bf16[1,256,1024]{2,1,0:T(8,128)(2,1)} %param.9) | copy-start | bytes 1572868
  7.2 109.1 %all-gather.5.cloned.1.call-start = ((), (), s32[]{:S(2)}) async-start(), calls=%async_computation.3 | async-start | bytes 12582912 | tf_op jit(solution)/shard_map/all_gather | solution.py:53
  8.0 421.6 %reduce-scatter.8.cloned.1.call-start = ((), (), s32[]{:S(2)}) async-start(), calls=%async_computation.6 | async-start | bytes 18874368 | tf_op jit(solution)/shard_map/reduce_scatter | solution.py:103
  41.4 2.2 copy-start.15
  124.7 1.0 copy-start.7
  124.7 1.5 copy-start.1
  126.2 0.9 copy-start.8
  126.5 0.8 copy-start.2
  126.6 1.1 copy-start.10
  126.6 1.6 copy-start
  126.6 1.6 copy-start.4
  128.2 0.8 copy-start.11
  129.0 0.8 copy-start.5
  131.6 1.0 copy-start.7
  131.6 1.5 copy-start.1
  133.1 0.9 copy-start.8
  133.4 0.8 copy-start.2
  133.5 1.1 copy-start.10
  133.5 1.6 copy-start
  133.5 1.6 copy-start.4
  135.1 0.8 copy-start.11
  135.9 0.8 copy-start.5
  146.6 1.0 copy-start.9
  146.6 1.8 copy-start.12
  146.6 303.9 %reduce-scatter.6.cloned.1.call-start = ((), (), s32[]{:S(2)}) async-start(), calls=%async_computation.5 | async-start | bytes 327680 | tf_op jit(solution)/shard_map/reduce_scatter | solution.py:87
  148.4 322.3 %reduce-scatter.4.cloned.1.call-start = ((), (), s32[]{:S(2)}) async-start(), calls=%async_computation.4 | async-start | bytes 327680 | tf_op jit(solution)/shard_map/reduce_scatter | solution.py:86
  149.2 283.5 %copy-start.6 = (bf16[2,256,4,128]{1,3,2,0:T(8,128)(2,1)S(1)}, bf16[2,256,4,128]{1,3,2,0:T(8,128)(2,1)}, u32[]{:S(2)}) copy-start(bf16[2,256,4,128]{1,3,2,0:T(8,128)(2,1)} %get-tuple-element.59) | copy-start | bytes 1572868
  149.2 402.6 %all-gather.7.cloned.1.call-start = ((), (), s32[]{:S(2)}) async-start(), calls=%async_computation.7 | async-start | bytes 5242880 | tf_op jit(solution)/shard_map/all_gather | solution.py:109
Sparse Core Ops, SparseCore 0:
  9.6 106.6 all-gather.4
  146.7 282.7 reduce-scatter.7
  431.9 18.6 reduce-scatter.5
  452.6 17.9 reduce-scatter.3
  472.7 78.9 all-gather.6
where the time goes:
time: 565 us
  waiting for transfers between devices  469 us (83%)
  blocking collectives  28.6 us (5%)
  matrix products  23.7 us (4%)
  local copies, waits for them, and re-layouts  21.4 us (4%)
  between operations  14.7 us (3%)
  other arithmetic  7.24 us (1%)
    reduce_scatter x1, waiting for transfers between devices, shards(): lax.psum_scatter(jnp.einsum('sd,se->de', columns, attn_rows, preferred_el...  280 us
    all_gather x1, waiting for transfers between devices, shards(): weight_grad = lax.all_gather(shard, 'ctx', axis=0, tiled=True)  79.6 us
    all_gather x1, waiting for transfers between devices, shards(): lax.all_gather(out_weight, 'dp', axis=0, tiled=True)  72.5 us
    reduce_scatter x1, waiting for transfers between devices, shards(): lax.psum_scatter(far_k, 'ctx', scatter_dimension=0, tiled=True)  18.6 us
    reduce_scatter x1, waiting for transfers between devices, shards(): lax.psum_scatter(far_v, 'ctx', scatter_dimension=0, tiled=True)  16.9 us
    all_gather x1, blocking collectives, shards(): lax.all_gather(values[0, seg_len - SUMMARY_TOKENS:], 'ctx', axis=0, tiled...  15.1 us
    all_gather x1, blocking collectives, shards(): lax.all_gather(keys[0, seg_len - SUMMARY_TOKENS:], 'ctx', axis=0, tiled=T...  13.5 us
  transfers between devices with their start and end apart: 5, of which 5 were waited for; matrix products, arithmetic and copies ran while one was open for 3% of the time, Pallas kernels for 0%

commit v1 on v0

v1 whole, which is shorter than its diff:
```python
import functools

import jax
import jax.numpy as jnp
from jax import lax
from jax.experimental import pallas as pl
from jax.experimental.pallas import tpu as pltpu
from jax.sharding import PartitionSpec as P

HEAD_SIZE = 128
SUMMARY_TOKENS = 64
SCALE = HEAD_SIZE ** (-0.5)
NEG_FILL = -1e30
VMEM_LIMIT = 48 * 1024 * 1024

VMEM = pltpu.MemorySpace.VMEM
SMEM = pltpu.MemorySpace.SMEM


def dot(a, b, contract):
    return lax.dot_general(a, b, (contract, ((), ())), preferred_element_type=jnp.float32)


def mask_bias(count_ref, id_column_ref, id_row_ref, shape, seg_len):
    rows = lax.broadcasted_iota(jnp.int32, shape, 0)
    cols = lax.broadcasted_iota(jnp.int32, shape, 1)
    own = (rows >= cols) & (id_column_ref[...] == id_row_ref[...])
    far = (cols >= seg_len) & (cols < seg_len + SUMMARY_TOKENS * count_ref[0, 0])
    return jnp.where(own | far, 0.0, NEG_FILL).astype(jnp.float32)


def softmax_rows(q_head, k_head, bias):
    scores = dot(q_head, k_head, ((1,), (1,))) * SCALE + bias
    top = jnp.max(scores, axis=-1, keepdims=True)
    expo = jnp.exp(scores - top)
    return expo / jnp.sum(expo, axis=-1, keepdims=True)


def forward_kernel(count_ref, idc_ref, idr_ref, q_ref, k_ref, v_ref, attn_ref, bias_ref):
    seg_len, q_width = q_ref.shape
    kv_heads = k_ref.shape[1] // HEAD_SIZE
    group = q_width // k_ref.shape[1]
    bias_ref[...] = mask_bias(count_ref, idc_ref, idr_ref, bias_ref.shape, seg_len)
    for kv in range(kv_heads):
        kv_cols = slice(kv * HEAD_SIZE, (kv + 1) * HEAD_SIZE)
        for g in range(group):
            h = kv * group + g
            cols = slice(h * HEAD_SIZE, (h + 1) * HEAD_SIZE)
            probs_b = softmax_rows(q_ref[:, cols], k_ref[:, kv_cols], bias_ref[...]).astype(jnp.bfloat16)
            attn_ref[:, cols] = dot(probs_b, v_ref[:, kv_cols], ((1,), (0,))).astype(jnp.bfloat16)


def backward_kernel(count_ref, idc_ref, idr_ref, q_ref, k_ref, v_ref, attn_ref, d_mine_ref, d_part_ref,
                    gq_ref, gkv_ref, bias_ref):
    seg_len, q_width = q_ref.shape
    kv_width = k_ref.shape[1]
    kv_heads = kv_width // HEAD_SIZE
    group = q_width // kv_width
    bias_ref[...] = mask_bias(count_ref, idc_ref, idr_ref, bias_ref.shape, seg_len)
    for kv in range(kv_heads):
        kv_cols = slice(kv * HEAD_SIZE, (kv + 1) * HEAD_SIZE)
        k_head = k_ref[:, kv_cols]
        v_head = v_ref[:, kv_cols]
        grad_k = jnp.zeros((k_ref.shape[0], HEAD_SIZE), jnp.float32)
        grad_v = jnp.zeros((k_ref.shape[0], HEAD_SIZE), jnp.float32)
        for g in range(group):
            h = kv * group + g
            cols = slice(h * HEAD_SIZE, (h + 1) * HEAD_SIZE)
            q_head = q_ref[:, cols]
            d_sum = d_mine_ref[:, cols]
            for part in range(d_part_ref.shape[0]):
                d_sum = d_sum + d_part_ref[part, :, cols].astype(jnp.float32)
            d_head = d_sum.astype(jnp.bfloat16)
            prob = softmax_rows(q_head, k_head, bias_ref[...])
            probs_b = prob.astype(jnp.bfloat16)
            delta = jnp.sum(
                d_head.astype(jnp.float32) * attn_ref[:, cols].astype(jnp.float32), axis=-1, keepdims=True
            )
            dprob = dot(d_head, v_head, ((1,), (1,)))
            ds_b = (prob * (dprob - delta)).astype(jnp.bfloat16)
            gq_ref[:, cols] = (SCALE * dot(ds_b, k_head, ((1,), (0,)))).astype(jnp.bfloat16)
            grad_k += dot(ds_b, q_head, ((0,), (0,)))
            grad_v += dot(probs_b, d_head, ((0,), (0,)))
        gkv_ref[:, kv_cols] = SCALE * grad_k
        gkv_ref[:, kv_width + kv * HEAD_SIZE : kv_width + (kv + 1) * HEAD_SIZE] = grad_v


def call_attention(kernel, out_shape, operands, bias_shape, flops):
    return pl.pallas_call(
        kernel,
        out_shape=out_shape,
        in_specs=[pl.BlockSpec(memory_space=SMEM)] + [pl.BlockSpec(memory_space=VMEM)] * (len(operands) - 1),
        out_specs=jax.tree.map(lambda _: pl.BlockSpec(memory_space=VMEM), out_shape),
        scratch_shapes=[pltpu.VMEM(bias_shape, jnp.float32)],
        compiler_params=pltpu.CompilerParams(vmem_limit_bytes=VMEM_LIMIT),
        cost_estimate=pl.CostEstimate(flops=flops, bytes_accessed=4 << 20, transcendentals=1 << 20),
    )(*operands)


def weight_kernel(blocks, has_acc, info_ref, *refs):
    ins, out_ref = refs[:-1], refs[-1]
    acc_ref = None
    if has_acc:
        acc_ref, ins = ins[0], ins[1:]
    core = info_ref[0]
    total = jnp.zeros(out_ref.shape, jnp.float32) if acc_ref is None else acc_ref[...]
    at = 0
    for whole in blocks:
        if whole:
            rows = ins[at][...]
            attn = ins[at + 1][...]
            at += 2
        else:
            mine, other, attn = ins[at][...], ins[at + 1][...], ins[at + 2][...]
            low = jnp.where(core == 0, mine, other)
            high = jnp.where(core == 0, other, mine)
            rows = jnp.concatenate([low, high], 0)
            at += 3
        total += dot(rows, attn, ((0,), (0,)))
    out_ref[...] = total.astype(out_ref.dtype)


def weight_stage(info, acc, blocks, out_dtype, tile):
    operands = [] if acc is None else [acc]
    width = blocks[0][-1].shape[1]
    height = blocks[0][0].shape[1]
    in_specs = [] if acc is None else [pl.BlockSpec((tile, width), lambda i, s: (i, 0))]
    flops = 0
    moved = (0 if acc is None else acc.size * 4) + height * width * jnp.dtype(out_dtype).itemsize
    for block in blocks:
        for part in block[:-1]:
            operands.append(part)
            in_specs.append(pl.BlockSpec((part.shape[0], tile), lambda i, s: (0, i)))
            moved += part.size * 2
        operands.append(block[-1])
        in_specs.append(pl.BlockSpec(block[-1].shape, lambda i, s: (0, 0)))
        flops += 2 * block[-1].size * height
        moved += block[-1].size * 2
    return pl.pallas_call(
        functools.partial(weight_kernel, [len(b) == 2 for b in blocks], acc is not None),
        out_shape=jax.ShapeDtypeStruct((height, width), out_dtype),
        grid_spec=pltpu.PrefetchScalarGridSpec(
            num_scalar_prefetch=1,
            grid=(height // tile,),
            in_specs=in_specs,
            out_specs=pl.BlockSpec((tile, width), lambda i, s: (i, 0)),
        ),
        compiler_params=pltpu.CompilerParams(vmem_limit_bytes=VMEM_LIMIT),
        cost_estimate=pl.CostEstimate(flops=flops, bytes_accessed=moved, transcendentals=0),
    )(info, *operands)


def turn(x, axis, step):
    n = lax.axis_size(axis)
    return lax.ppermute(x, axis, [(i, (i + step) % n) for i in range(n)])


def line_pairs(n, step):
    return [(i, i + step) for i in range(n) if 0 <= i + step < n]


def spread(x):
    right = lax.ppermute(x, "ctx", line_pairs(4, 1))
    left = lax.ppermute(x, "ctx", line_pairs(4, -1))
    two = lax.ppermute(x, "ctx", [(0, 2), (1, 3), (2, 0), (3, 1)])
    three = lax.ppermute(two, "ctx", [(1, 0), (2, 3)])
    return [right, left, two, three]


def after(x, *others):
    return lax.optimization_barrier((x, *others))[0]


def shards(queries, keys, values, tok_ids, vis_start, out_weight, grad_out):
    seg_len = queries.shape[1]
    kv_width = keys.shape[2]
    d_model = grad_out.shape[2]
    part_rows = out_weight.shape[0]
    n_ctx = lax.axis_size("ctx")
    n_dp = lax.axis_size("dp")
    n_head = lax.axis_size("head")
    place = lax.axis_index("ctx")
    me_dp = lax.axis_index("dp")
    me_head = lax.axis_index("head")
    half = seg_len // n_head
    cut = seg_len - SUMMARY_TOKENS

    tail = jnp.concatenate([keys[0, cut:], values[0, cut:]], axis=1)
    far = [lax.ppermute(tail, "ctx", line_pairs(n_ctx, s)) for s in range(1, n_ctx)]
    far_len = -(-(n_ctx - 1) * SUMMARY_TOKENS // HEAD_SIZE) * HEAD_SIZE
    far.append(jnp.zeros((far_len - (n_ctx - 1) * SUMMARY_TOKENS, 2 * kv_width), keys.dtype))
    far = jnp.concatenate(far, axis=0)
    all_keys = jnp.concatenate([keys[0], far[:, :kv_width]], axis=0)
    all_vals = jnp.concatenate([values[0], far[:, kv_width:]], axis=0)
    n_keys = seg_len + far_len

    rows_half = lax.dynamic_slice(grad_out[0], (me_head * half, 0), (half, d_model))
    own_rows = lax.dynamic_slice(grad_out[0], (0, me_dp * part_rows), (seg_len, part_rows))
    own_half = lax.dynamic_slice(rows_half, (0, me_dp * part_rows), (half, part_rows))
    peer_half = []
    for s in range(1, n_dp):
        to = lax.rem(me_dp + s, n_dp)
        peer_half.append(turn(lax.dynamic_slice(rows_half, (0, to * part_rows), (half, part_rows)), "dp", s))
    peer_other = [turn(x, "head", 1) for x in peer_half]

    wide = n_ctx != 4
    if not wide:
        own_z = spread(own_half)

    count = (place - vis_start[0, 0]).reshape(1, 1).astype(jnp.int32)
    id_column = tok_ids[0].reshape(seg_len, 1)
    id_row = jnp.pad(tok_ids, ((0, 0), (0, far_len)), constant_values=-1)
    pair_flops = 2 * seg_len * n_keys * queries.shape[2]
    attn = call_attention(
        forward_kernel,
        jax.ShapeDtypeStruct(queries.shape[1:], jnp.bfloat16),
        (count, id_column, id_row, queries[0], all_keys, all_vals),
        (seg_len, n_keys),
        2 * pair_flops,
    )
    if not wide:
        attn_z = [attn] + spread(attn)
        attn_x = []
        for s in range(1, n_dp):
            attn_x.append([turn(x, "dp", s) for x in attn_z])

    first_core = me_head == 0
    back = []
    for s in range(1, n_dp):
        mine, other = peer_half[s - 1], peer_other[s - 1]
        rows = jnp.concatenate([jnp.where(first_core, mine, other), jnp.where(first_core, other, mine)], 0)
        part = jnp.dot(rows, out_weight, preferred_element_type=jnp.float32).astype(jnp.bfloat16)
        back.append(turn(part, "dp", -s))
    d_mine = jnp.dot(own_rows, out_weight, preferred_element_type=jnp.float32)
    d_part = jnp.stack(back)

    grad_q, grad_kv = call_attention(
        backward_kernel,
        (
            jax.ShapeDtypeStruct(queries.shape[1:], jnp.bfloat16),
            jax.ShapeDtypeStruct((n_keys, 2 * kv_width), jnp.float32),
        ),
        (count, id_column, id_row, queries[0], all_keys, all_vals, attn, d_mine, d_part),
        (seg_len, n_keys),
        5 * pair_flops,
    )
    home = grad_kv[cut:seg_len]
    for s in range(1, n_ctx):
        begin = seg_len + (s - 1) * SUMMARY_TOKENS
        home = home + lax.ppermute(grad_kv[begin : begin + SUMMARY_TOKENS], "ctx", line_pairs(n_ctx, -s))
    out_kv = jnp.concatenate([grad_kv[:cut], home], 0).astype(jnp.bfloat16)
    out_k, out_v = out_kv[:, :kv_width], out_kv[:, kv_width:]

    if wide:
        block = d_model // (n_ctx * n_dp)
        columns = (
            grad_out[0].reshape(seg_len, n_dp, n_ctx, block).transpose(0, 2, 1, 3).reshape(seg_len, d_model)
        )
        shard = lax.psum_scatter(
            jnp.einsum("sd,se->de", columns, attn, preferred_element_type=jnp.float32),
            ("ctx", "dp"),
            scatter_dimension=0,
            tiled=True,
        ).astype(jnp.bfloat16)
        weight_grad = lax.all_gather(shard, "ctx", axis=0, tiled=True)
    else:
        info = me_head.reshape(1).astype(jnp.int32)
        own_other = [turn(x, "head", 1) for x in own_z]
        acc = weight_stage(
            info,
            None,
            [(own_rows, attn)] + list(zip(own_z, own_other, attn_z[1:])),
            jnp.float32,
            256,
        )
        for s in range(1, n_dp):
            start = after(peer_half[s - 1], *own_z)
            peer_z = spread(start)
            other_z = [turn(x, "head", 1) for x in peer_z]
            acc = weight_stage(
                info,
                acc,
                list(zip([start] + peer_z, [peer_other[s - 1]] + other_z, attn_x[s - 1])),
                jnp.bfloat16 if s == n_dp - 1 else jnp.float32,
                256,
            )
        weight_grad = acc
    return (grad_q[None], out_k[None], out_v[None], weight_grad)


def solution(mesh):
    placed = (
        P(("groups", "dp"), "ctx", "head"),
        P(("groups", "dp"), "ctx", "head"),
        P(("groups", "dp"), "ctx", "head"),
        P(("groups", "dp"), "ctx"),
        P(("groups", "dp"), "ctx"),
        P("dp", "head"),
        P(("groups", "dp"), "ctx", None),
    )
    return jax.shard_map(
        shards,
        mesh=mesh,
        in_specs=placed,
        out_specs=(
            P(("groups", "dp"), "ctx", "head"),
            P(("groups", "dp"), "ctx", "head"),
            P(("groups", "dp"), "ctx", "head"),
            P(("groups", "dp"), "head"),
        ),
        check_vma=False,
    )
```

time: 565 us -> 179 us (0.32)
  waiting for transfers between devices: 469 us -> 82.2 us
  starting transfers between devices: 0.2 us -> 46 us
  Pallas kernels: 0 us -> 33.9 us
  blocking collectives: 28.6 us -> 0 us
  matrix products: 23.7 us -> 4.87 us
  local copies, waits for them, and re-layouts: 21.4 us -> 6.95 us
  between operations: 14.7 us -> 1.69 us
    reduce_scatter x3 -> x0, waiting for transfers between devices: 316 us -> none  [the longest x1 280 us: shards(): lax.psum_scatter(jnp.einsum('sd,se->de', columns, attn_rows, preferred_el...]
    all_gather x2 -> x0, waiting for transfers between devices: 152 us -> none  [the longest x1 79.6 us: shards(): weight_grad = lax.all_gather(shard, 'ctx', axis=0, tiled=True)]
    ppermute x0 -> x34, waiting for transfers between devices: none -> 82.2 us  [the longest x3 31.7 us: spread(): two = lax.ppermute(x, 'ctx', [(0, 2), (1, 3), (2, 0), (3, 1)])]
    ppermute x0 -> x34, starting transfers between devices: none -> 46 us  [the longest x16 10.8 us: turn(): return lax.ppermute(x, axis, [(i, (i + step) % n) for i in range(n)])]
    pallas_call x0 -> x4, Pallas kernels: none -> 33.9 us  [the longest x2 22.7 us: weight_stage(): pl.pallas_call(functools.partial(weight_kernel, [len(b) == 2 for b in blo...]
    all_gather x2 -> x0, blocking collectives: 28.6 us -> none  [the longest x1 15.1 us: shards(): lax.all_gather(values[0, seg_len - SUMMARY_TOKENS:], 'ctx', axis=0, tiled...]
    dot_general x12 -> x2, matrix products: 20.1 us -> 4.87 us  [the longest x1 3.59 us: shards(): jnp.dot(rows, out_weight, preferred_element_type=jnp.float32)]
    unnamed x19 -> x18, local copies, waits for them, and re-layouts: 11.2 us -> 1.62 us
  transfers between devices with their start and end apart: 5 -> 34, of which waited for: 5 -> 11; matrix products, arithmetic and copies ran while one was open for 3% -> 7% of each run, Pallas kernels for 0% -> 13%
where the time goes in v1:
time: 179 us; the launch traced here: 178 us
  waiting for transfers between devices  82.2 us (46%)
  starting transfers between devices  46 us (26%)
  Pallas kernels  33.9 us (19%)
  local copies, waits for them, and re-layouts  6.95 us (4%)
  matrix products  4.87 us (3%)
  other arithmetic  2.79 us (2%)
    ppermute x3, waiting for transfers between devices, spread(): two = lax.ppermute(x, 'ctx', [(0, 2), (1, 3), (2, 0), (3, 1)])  31.7 us
    pallas_call x2, Pallas kernels, weight_stage(): pl.pallas_call(functools.partial(weight_kernel, [len(b) == 2 for b in blo...  22.7 us
    ppermute x3, waiting for transfers between devices, spread(): three = lax.ppermute(two, 'ctx', [(1, 0), (2, 3)])  19.1 us
    ppermute x16, waiting for transfers between devices, turn(): return lax.ppermute(x, axis, [(i, (i + step) % n) for i in range(n)])  17.6 us
    pallas_call x2, Pallas kernels, call_attention(): pl.pallas_call(kernel, out_shape=out_shape, in_specs=[pl.BlockSpec(memory...  11.1 us
    ppermute x16, starting transfers between devices, turn(): return lax.ppermute(x, axis, [(i, (i + step) % n) for i in range(n)])  10.8 us
    ppermute x3, starting transfers between devices, shards(): lax.ppermute(tail, 'ctx', line_pairs(n_ctx, s))  10.7 us
    ppermute x3, waiting for transfers between devices, shards(): lax.ppermute(grad_kv[begin:begin + SUMMARY_TOKENS], 'ctx', line_pairs(n_c...  10.6 us
  transfers between devices with their start and end apart: 34, of which 11 were waited for; matrix products, arithmetic and copies ran while one was open for 7% of the time, Pallas kernels for 13%

profile of v1, /device:TPU:0, one launch (start us, length us, event | category | flops | bytes accessed | tf_op | source)
XLA Modules:
  0.0 178.4 jit_solution(15910436241713690611)
XLA Ops:
  1.5 7.0 %collective-permute-start.2 = (bf16[64,512]{1,0:T(8,128)(2,1)S(1)}, bf16[64,512]{1,0:T(8,128)(2,1)S(1)}, u32[]{:S(2)}, u32[]{:S(2)}) collective-permute-start(bf16[64,512]{1,0:T(8,128)(2,1)S(1)} %pad_maximum_fusion.3), channel_id=1, source_target_pairs={{0,12},{1,13},{2,14},{3,15},{16,28},{17,29},{18,30},{19,31}} | collective-permute-start | bytes 196616 | tf_op jit(solution)/shard_map/ppermute | solution.py:189
  8.5 1.3 collective-permute-start.1
  9.8 2.5 %collective-permute-start = (bf16[64,512]{1,0:T(8,128)(2,1)S(1)}, bf16[64,512]{1,0:T(8,128)(2,1)S(1)}, u32[]{:S(2)}, u32[]{:S(2)}) collective-permute-start(bf16[64,512]{1,0:T(8,128)(2,1)S(1)} %pad_maximum_fusion.3), channel_id=1, source_target_pairs={{0,4},{4,8},{8,12},{1,5},{5,9},{9,13},{2,6},{6,10},{10,14},{3,7},{... | collective-permute-start | bytes 196616 | tf_op jit(solution)/shard_map/ppermute | solution.py:189
  12.3 2.7 %dynamic-slice_bitcast_fusion.1 = (bf16[128,2048]{1,0:T(8,128)(2,1)}, bf16[128,2048]{1,0:T(8,128)(2,1)}) fusion(bf16[1,256,4096]{2,1,0:T(8,128)(2,1)} %param.13, s32[]{:T(128)S(6)} %select_n.31, s32[]{:T(128)S(6)} %select_n.36, s32[]{:T(128)S(6)} %select_n.33), kind=kLoop, calls=%fused_computation.5 | loop fusion | bytes 2097164 | tf_op jit(solution)/shard_map/dynamic_slice | solution.py:199
  15.0 1.9 %collective-permute-start.9 = (bf16[128,2048]{1,0:T(8,128)(2,1)}, bf16[128,2048]{1,0:T(8,128)(2,1)S(1)}, u32[]{:S(2)}, u32[]{:S(2)}) collective-permute-start(bf16[128,2048]{1,0:T(8,128)(2,1)} %get-tuple-element.10), channel_id=1, source_target_pairs={{0,4},{4,8},{8,12},{1,5},{5,9},{9,13},{2,6},{6,10},{10,14},{3,7},{... | collective-permute-start | bytes 1572872 | tf_op jit(solution)/shard_map/ppermute | solution.py:163
  16.9 1.3 collective-permute-start.12
  20.5 2.1 %collective-permute-start.15 = (bf16[128,2048]{1,0:T(8,128)(2,1)}, bf16[128,2048]{1,0:T(8,128)(2,1)}, u32[]{:S(2)}, u32[]{:S(2)}) collective-permute-start(bf16[128,2048]{1,0:T(8,128)(2,1)} %get-tuple-element.10), channel_id=1, source_target_pairs={{0,8},{4,12},{8,0},{12,4},{1,9},{5,13},{9,1},{13,5},{2,10},{6,14},... | collective-permute-start | bytes 1572872 | tf_op jit(solution)/shard_map/ppermute | solution.py:165
  22.6 1.5 collective-permute-start.3
  26.1 4.4 %shard_map.102.attn_ref.refs_1_ = bf16[256,1024]{1,0:T(8,128)(2,1)} custom-call(s32[1,1]{1,0:T(1,128)} %bitcast.1.count_ref, s32[256,1]{1,0:T(8,128)S(1)} %copy.12.idc_ref, s32[1,512]{1,0:T(1,128)S(1)} %pad.4.idr_ref, bf16[256,1024]{1,0:T(8,128)(2,1)S(1)} %bitcast.27, bf16[512,256]{1,0:T(8,128)(2,1)S(1)} %pad_maximum_fusion.k_ref, ...), custom_call_target="tpu_custom_call" | custom-call | flops 536870912 | bytes 4194304 | tf_op jit(solution)/shard_map/pallas_call | solution.py:89
  30.4 3.4 %collective-permute-start.11 = (bf16[256,1024]{1,0:T(8,128)(2,1)}, bf16[256,1024]{1,0:T(8,128)(2,1)}, u32[]{:S(2)}, u32[]{:S(2)}) collective-permute-start(bf16[256,1024]{1,0:T(8,128)(2,1)} %shard_map.102.attn_ref.refs_1_), channel_id=1, source_target_pairs={{0,4},{4,8},{8,12},{1,5},{5,9},{9,13},{2,6},{6,10},{10,14},{3,7},{... | collective-permute-start | bytes 1572872 | tf_op jit(solution)/shard_map/ppermute | solution.py:163
  33.8 1.8 collective-permute-done.3.refs_1_
  36.9 19.0 %collective-permute-done.15.refs_8_ = bf16[128,2048]{1,0:T(8,128)(2,1)} collective-permute-done((bf16[128,2048]{1,0:T(8,128)(2,1)}, bf16[128,2048]{1,0:T(8,128)(2,1)}, u32[]{:S(2)}, u32[]{:S(2)}) %collective-permute-start.15) | collective-permute-done | bytes 524320 | tf_op jit(solution)/shard_map/ppermute | solution.py:165
  58.2 1.5 collective-permute-start.21
  59.7 3.2 %collective-permute-done.14.refs_7_ = bf16[256,1024]{1,0:T(8,128)(2,1)} collective-permute-done((bf16[256,1024]{1,0:T(8,128)(2,1)}, bf16[256,1024]{1,0:T(8,128)(2,1)}, u32[]{:S(2)}, u32[]{:S(2)}) %collective-permute-start.14) | collective-permute-done | bytes 524320 | tf_op jit(solution)/shard_map/ppermute | solution.py:164
  63.4 8.3 %collective-permute-done.18.refs_11_ = bf16[128,2048]{1,0:T(8,128)(2,1)} collective-permute-done((bf16[128,2048]{1,0:T(8,128)(2,1)}, bf16[128,2048]{1,0:T(8,128)(2,1)}, u32[]{:S(2)}, u32[]{:S(2)}) %collective-permute-start.18) | collective-permute-done | bytes 524320 | tf_op jit(solution)/shard_map/ppermute | solution.py:166
  71.7 3.6 %convolution_convert_fusion = bf16[256,1024]{1,0:T(8,128)(2,1)S(1)} fusion(bf16[2048,1024]{1,0:T(8,128)(2,1)} %param.12, bf16[128,2048]{1,0:T(8,128)(2,1)S(1)} %get-tuple-element.16, bf16[128,2048]{1,0:T(8,128)(2,1)S(1)} %get-tuple-element.15), kind=kOutput, calls=%fused_computation | convolution fusion | flops 1076101120 | bytes 5767168 | tf_op jit(solution)/shard_map/dot_general | solution.py:232
  75.3 12.7 %collective-permute-done.17.refs_10_ = bf16[256,1024]{1,0:T(8,128)(2,1)S(1)} collective-permute-done((bf16[256,1024]{1,0:T(8,128)(2,1)}, bf16[256,1024]{1,0:T(8,128)(2,1)S(1)}, u32[]{:S(2)}, u32[]{:S(2)}) %collective-permute-start.17) | collective-permute-done | bytes 524320 | tf_op jit(solution)/shard_map/ppermute | solution.py:165
  89.4 1.6 collective-permute-start.24
  91.5 1.5 collective-permute-start.5
  94.3 10.8 %collective-permute-done.20.refs_13_ = bf16[256,1024]{1,0:T(8,128)(2,1)} collective-permute-done((bf16[256,1024]{1,0:T(8,128)(2,1)S(1)}, bf16[256,1024]{1,0:T(8,128)(2,1)}, u32[]{:S(2)}, u32[]{:S(2)}) %collective-permute-start.20) | collective-permute-done | bytes 524320 | tf_op jit(solution)/shard_map/ppermute | solution.py:166
  105.1 1.5 collective-permute-start.30
  106.6 3.2 %collective-permute-start.22 = (bf16[128,2048]{1,0:T(8,128)(2,1)S(1)}, bf16[128,2048]{1,0:T(8,128)(2,1)S(1)}, u32[]{:S(2)}, u32[]{:S(2)}) collective-permute-start(bf16[128,2048]{1,0:T(8,128)(2,1)S(1)} %collective-permute-done.3.refs_1_), channel_id=1, source_target_pairs={{0,4},{4,8},{8,12},{1,5},{5,9},{9,13},{2,6},{6,10},{10,14},{3,7},{... | collective-permute-start | bytes 1572872 | tf_op jit(solution)/shard_map/ppermute | solution.py:163
  109.8 5.9 %collective-permute-done.27.refs_9_ = bf16[256,1024]{1,0:T(8,128)(2,1)S(1)} collective-permute-done((bf16[256,1024]{1,0:T(8,128)(2,1)}, bf16[256,1024]{1,0:T(8,128)(2,1)S(1)}, u32[]{:S(2)}, u32[]{:S(2)}) %collective-permute-start.27) | collective-permute-done | bytes 524320 | tf_op jit(solution)/shard_map/ppermute | solution.py:155
  117.0 9.9 %collective-permute-done.5 = bf16[256,1024]{1,0:T(8,128)(2,1)S(1)} collective-permute-done((bf16[256,1024]{1,0:T(8,128)(2,1)S(1)}, bf16[256,1024]{1,0:T(8,128)(2,1)S(1)}, u32[]{:S(2)}, u32[]{:S(2)}) %collective-permute-start.5) | collective-permute-done | bytes 524320 | tf_op jit(solution)/shard_map/ppermute | solution.py:155
  127.0 1.5 collective-permute-start.31
  129.7 6.7 %shard_map.103 = (bf16[256,1024]{1,0:T(8,128)(2,1)}, f32[512,512]{1,0:T(8,128)S(1)}) custom-call(s32[1,1]{1,0:T(1,128)} %bitcast.1.count_ref, s32[256,1]{1,0:T(8,128)S(1)} %copy.12.idc_ref, s32[1,512]{1,0:T(1,128)S(1)} %pad.4.idr_ref, bf16[256,1024]{1,0:T(8,128)(2,1)S(1)} %bitcast.28, bf16[512,256]{1,0:T(8,128)(2,1)S(1)} %pad_maximum_fusion.k_ref, ...), custom_call_target="tpu_custom_call" | custom-call | flops 1342177280 | bytes 4194304 | tf_op jit(solution)/shard_map/pallas_call | solution.py:89
  136.5 1.3 collective-permute-start.8
  140.5 1.6 collective-permute-start.33
  142.0 4.4 %collective-permute-done.8 = f32[64,512]{1,0:T(8,128)S(1)} collective-permute-done((f32[64,512]{1,0:T(8,128)S(1)}, f32[64,512]{1,0:T(8,128)S(1)}, u32[]{:S(2)}, u32[]{:S(2)}) %collective-permute-start.8) | collective-permute-done | bytes 131104 | tf_op jit(solution)/shard_map/ppermute | solution.py:250
  146.5 5.4 %collective-permute-done.7 = f32[64,512]{1,0:T(8,128)S(1)} collective-permute-done((f32[64,512]{1,0:T(8,128)S(1)}, f32[64,512]{1,0:T(8,128)S(1)}, u32[]{:S(2)}, u32[]{:S(2)}) %collective-permute-start.7) | collective-permute-done | bytes 131104 | tf_op jit(solution)/shard_map/ppermute | solution.py:250
  153.2 11.3 %shard_map.104.refs_0_ = f32[2048,1024]{1,0:T(8,128)} custom-call(s32[1]{0:T(128)} %bitcast.14.info_ref, bf16[256,2048]{1,0:T(8,128)(2,1)} %copy-done.2, bf16[256,1024]{1,0:T(8,128)(2,1)} %shard_map.102.attn_ref.refs_1_, bf16[128,2048]{1,0:T(8,128)(2,1)S(1)} %collective-permute-done.9.refs_2_, bf16[128,2048]{1,0:T(8,128)(2,1)S(1)} %collective-permute-done.10.refs_3_, ...), custom_call_target="tpu_custom_call" | custom-call | flops 5368709120 | bytes 16252928 | tf_op jit(solution)/shard_map/pallas_call | solution.py:139
  166.9 11.4 %shard_map.105 = bf16[2048,1024]{1,0:T(8,128)(2,1)} custom-call(s32[1]{0:T(128)} %bitcast.14.info_ref, f32[2048,1024]{1,0:T(8,128)} %shard_map.104.refs_0_, bf16[128,2048]{1,0:T(8,128)(2,1)S(1)} %collective-permute-done.3.refs_1_, bf16[128,2048]{1,0:T(8,128)(2,1)S(1)} %collective-permute-done.4.refs_2_, ...), custom_call_target="tpu_custom_call" | custom-call | flops 5368709120 | bytes 20447232 | tf_op jit(solution)/shard_map/pallas_call | solution.py:139
  (77 shorter events, 20.6 us)
Async XLA Ops:
  1.5 19.0 %collective-permute-start.2 = (bf16[64,512]{1,0:T(8,128)(2,1)S(1)}, bf16[64,512]{1,0:T(8,128)(2,1)S(1)}, u32[]{:S(2)}, u32[]{:S(2)}) collective-permute-start(bf16[64,512]{1,0:T(8,128)(2,1)S(1)} %pad_maximum_fusion.3), channel_id=1, source_target_pairs={{0,12},{1,13},{2,14},{3,15},{16,28},{17,29},{18,30},{19,31}} | collective-permute-start | bytes 196616 | tf_op jit(solution)/shard_map/ppermute | solution.py:189
  8.5 14.1 %collective-permute-start.1 = (bf16[64,512]{1,0:T(8,128)(2,1)S(1)}, bf16[64,512]{1,0:T(8,128)(2,1)S(1)}, u32[]{:S(2)}, u32[]{:S(2)}) collective-permute-start(bf16[64,512]{1,0:T(8,128)(2,1)S(1)} %pad_maximum_fusion.3), channel_id=1, source_target_pairs={{0,8},{4,12},{1,9},{5,13},{2,10},{6,14},{3,11},{7,15},{16,24},{20,... | collective-permute-start | bytes 196616 | tf_op jit(solution)/shard_map/ppermute | solution.py:189
  9.8 14.3 %collective-permute-start = (bf16[64,512]{1,0:T(8,128)(2,1)S(1)}, bf16[64,512]{1,0:T(8,128)(2,1)S(1)}, u32[]{:S(2)}, u32[]{:S(2)}) collective-permute-start(bf16[64,512]{1,0:T(8,128)(2,1)S(1)} %pad_maximum_fusion.3), channel_id=1, source_target_pairs={{0,4},{4,8},{8,12},{1,5},{5,9},{9,13},{2,6},{6,10},{10,14},{3,7},{... | collective-permute-start | bytes 196616 | tf_op jit(solution)/shard_map/ppermute | solution.py:189
  15.0 21.9 %collective-permute-start.9 = (bf16[128,2048]{1,0:T(8,128)(2,1)}, bf16[128,2048]{1,0:T(8,128)(2,1)S(1)}, u32[]{:S(2)}, u32[]{:S(2)}) collective-permute-start(bf16[128,2048]{1,0:T(8,128)(2,1)} %get-tuple-element.10), channel_id=1, source_target_pairs={{0,4},{4,8},{8,12},{1,5},{5,9},{9,13},{2,6},{6,10},{10,14},{3,7},{... | collective-permute-start | bytes 1572872 | tf_op jit(solution)/shard_map/ppermute | solution.py:163
  16.9 40.3 %collective-permute-start.12 = (bf16[128,2048]{1,0:T(8,128)(2,1)}, bf16[128,2048]{1,0:T(8,128)(2,1)S(1)}, u32[]{:S(2)}, u32[]{:S(2)}) collective-permute-start(bf16[128,2048]{1,0:T(8,128)(2,1)} %get-tuple-element.10), channel_id=1, source_target_pairs={{4,0},{8,4},{12,8},{5,1},{9,5},{13,9},{6,2},{10,6},{14,10},{7,3},{... | collective-permute-start | bytes 1572872 | tf_op jit(solution)/shard_map/ppermute | solution.py:164
  20.5 35.5 %collective-permute-start.15 = (bf16[128,2048]{1,0:T(8,128)(2,1)}, bf16[128,2048]{1,0:T(8,128)(2,1)}, u32[]{:S(2)}, u32[]{:S(2)}) collective-permute-start(bf16[128,2048]{1,0:T(8,128)(2,1)} %get-tuple-element.10), channel_id=1, source_target_pairs={{0,8},{4,12},{8,0},{12,4},{1,9},{5,13},{9,1},{13,5},{2,10},{6,14},... | collective-permute-start | bytes 1572872 | tf_op jit(solution)/shard_map/ppermute | solution.py:165
  22.6 13.0 %collective-permute-start.3 = (bf16[128,2048]{1,0:T(8,128)(2,1)}, bf16[128,2048]{1,0:T(8,128)(2,1)S(1)}, u32[]{:S(2)}, u32[]{:S(2)}) collective-permute-start(bf16[128,2048]{1,0:T(8,128)(2,1)} %get-tuple-element.11), channel_id=1, source_target_pairs={{0,2},{2,0},{1,3},{3,1},{4,6},{6,4},{5,7},{7,5},{8,10},{10,8},{9,1... | collective-permute-start | bytes 1572872 | tf_op jit(solution)/shard_map/ppermute | solution.py:155
  30.4 27.7 %collective-permute-start.11 = (bf16[256,1024]{1,0:T(8,128)(2,1)}, bf16[256,1024]{1,0:T(8,128)(2,1)}, u32[]{:S(2)}, u32[]{:S(2)}) collective-permute-start(bf16[256,1024]{1,0:T(8,128)(2,1)} %shard_map.102.attn_ref.refs_1_), channel_id=1, source_target_pairs={{0,4},{4,8},{8,12},{1,5},{5,9},{9,13},{2,6},{6,10},{10,14},{3,7},{... | collective-permute-start | bytes 1572872 | tf_op jit(solution)/shard_map/ppermute | solution.py:163
  35.6 27.3 %collective-permute-start.14 = (bf16[256,1024]{1,0:T(8,128)(2,1)}, bf16[256,1024]{1,0:T(8,128)(2,1)}, u32[]{:S(2)}, u32[]{:S(2)}) collective-permute-start(bf16[256,1024]{1,0:T(8,128)(2,1)} %shard_map.102.attn_ref.refs_1_), channel_id=1, source_target_pairs={{4,0},{8,4},{12,8},{5,1},{9,5},{13,9},{6,2},{10,6},{14,10},{7,3},{... | collective-permute-start | bytes 1572872 | tf_op jit(solution)/shard_map/ppermute | solution.py:164
  36.9 26.0 %collective-permute-start.4 = (bf16[128,2048]{1,0:T(8,128)(2,1)S(1)}, bf16[128,2048]{1,0:T(8,128)(2,1)S(1)}, u32[]{:S(2)}, u32[]{:S(2)}) collective-permute-start(bf16[128,2048]{1,0:T(8,128)(2,1)S(1)} %collective-permute-done.3.refs_1_), channel_id=1, source_target_pairs={{0,1},{1,0},{2,3},{3,2},{4,5},{5,4},{6,7},{7,6},{8,9},{9,8},{10,11... | collective-permute-start | bytes 1572872 | tf_op jit(solution)/shard_map/ppermute | solution.py:155
  56.0 15.7 %collective-permute-start.18 = (bf16[128,2048]{1,0:T(8,128)(2,1)}, bf16[128,2048]{1,0:T(8,128)(2,1)}, u32[]{:S(2)}, u32[]{:S(2)}) collective-permute-start(bf16[128,2048]{1,0:T(8,128)(2,1)} %collective-permute-done.15.refs_8_), channel_id=1, source_target_pairs={{4,0},{8,12},{5,1},{9,13},{6,2},{10,14},{7,3},{11,15},{20,16},{24,... | collective-permute-start | bytes 1572872 | tf_op jit(solution)/shard_map/ppermute | solution.py:166
  57.3 30.8 %collective-permute-start.17 = (bf16[256,1024]{1,0:T(8,128)(2,1)}, bf16[256,1024]{1,0:T(8,128)(2,1)S(1)}, u32[]{:S(2)}, u32[]{:S(2)}) collective-permute-start(bf16[256,1024]{1,0:T(8,128)(2,1)} %shard_map.102.attn_ref.refs_1_), channel_id=1, source_target_pairs={{0,8},{4,12},{8,0},{12,4},{1,9},{5,13},{9,1},{13,5},{2,10},{6,14},... | collective-permute-start | bytes 1572872 | tf_op jit(solution)/shard_map/ppermute | solution.py:165
  58.2 31.1 %collective-permute-start.21 = (bf16[256,1024]{1,0:T(8,128)(2,1)}, bf16[256,1024]{1,0:T(8,128)(2,1)S(1)}, u32[]{:S(2)}, u32[]{:S(2)}) collective-permute-start(bf16[256,1024]{1,0:T(8,128)(2,1)} %shard_map.102.attn_ref.refs_1_), channel_id=1, source_target_pairs={{0,2},{2,0},{1,3},{3,1},{4,6},{6,4},{5,7},{7,5},{8,10},{10,8},{9,1... | collective-permute-start | bytes 1572872 | tf_op jit(solution)/shard_map/ppermute | solution.py:155
  62.9 30.1 %collective-permute-start.16 = (bf16[128,2048]{1,0:T(8,128)(2,1)}, bf16[128,2048]{1,0:T(8,128)(2,1)S(1)}, u32[]{:S(2)}, u32[]{:S(2)}) collective-permute-start(bf16[128,2048]{1,0:T(8,128)(2,1)} %collective-permute-done.15.refs_8_), channel_id=1, source_target_pairs={{0,1},{1,0},{2,3},{3,2},{4,5},{5,4},{6,7},{7,6},{8,9},{9,8},{10,11... | collective-permute-start | bytes 1572872 | tf_op jit(solution)/shard_map/ppermute | solution.py:155
  62.9 28.1 %collective-permute-start.10 = (bf16[128,2048]{1,0:T(8,128)(2,1)S(1)}, bf16[128,2048]{1,0:T(8,128)(2,1)S(1)}, u32[]{:S(2)}, u32[]{:S(2)}) collective-permute-start(bf16[128,2048]{1,0:T(8,128)(2,1)S(1)} %collective-permute-done.9.refs_2_), channel_id=1, source_target_pairs={{0,1},{1,0},{2,3},{3,2},{4,5},{5,4},{6,7},{7,6},{8,9},{9,8},{10,11... | collective-permute-start | bytes 1572872 | tf_op jit(solution)/shard_map/ppermute | solution.py:155
  71.6 19.8 %collective-permute-start.13 = (bf16[128,2048]{1,0:T(8,128)(2,1)S(1)}, bf16[128,2048]{1,0:T(8,128)(2,1)S(1)}, u32[]{:S(2)}, u32[]{:S(2)}) collective-permute-start(bf16[128,2048]{1,0:T(8,128)(2,1)S(1)} %collective-permute-done.12.refs_5_), channel_id=1, source_target_pairs={{0,1},{1,0},{2,3},{3,2},{4,5},{5,4},{6,7},{7,6},{8,9},{9,8},{10,11... | collective-permute-start | bytes 1572872 | tf_op jit(solution)/shard_map/ppermute | solution.py:155
  88.1 17.0 %collective-permute-start.20 = (bf16[256,1024]{1,0:T(8,128)(2,1)S(1)}, bf16[256,1024]{1,0:T(8,128)(2,1)}, u32[]{:S(2)}, u32[]{:S(2)}) collective-permute-start(bf16[256,1024]{1,0:T(8,128)(2,1)S(1)} %collective-permute-done.17.refs_10_), channel_id=1, source_target_pairs={{4,0},{8,12},{5,1},{9,13},{6,2},{10,14},{7,3},{11,15},{20,16},{24,... | collective-permute-start | bytes 1572872 | tf_op jit(solution)/shard_map/ppermute | solution.py:166
  89.4 17.2 %collective-permute-start.24 = (bf16[256,1024]{1,0:T(8,128)(2,1)}, bf16[256,1024]{1,0:T(8,128)(2,1)S(1)}, u32[]{:S(2)}, u32[]{:S(2)}) collective-permute-start(bf16[256,1024]{1,0:T(8,128)(2,1)} %collective-permute-done.11.refs_4_), channel_id=1, source_target_pairs={{0,2},{2,0},{1,3},{3,1},{4,6},{6,4},{5,7},{7,5},{8,10},{10,8},{9,1... | collective-permute-start | bytes 1572872 | tf_op jit(solution)/shard_map/ppermute | solution.py:155
  90.9 24.8 %collective-permute-start.27 = (bf16[256,1024]{1,0:T(8,128)(2,1)}, bf16[256,1024]{1,0:T(8,128)(2,1)S(1)}, u32[]{:S(2)}, u32[]{:S(2)}) collective-permute-start(bf16[256,1024]{1,0:T(8,128)(2,1)} %collective-permute-done.14.refs_7_), channel_id=1, source_target_pairs={{0,2},{2,0},{1,3},{3,1},{4,6},{6,4},{5,7},{7,5},{8,10},{10,8},{9,1... | collective-permute-start | bytes 1572872 | tf_op jit(solution)/shard_map/ppermute | solution.py:155
  91.5 35.5 %collective-permute-start.5 = (bf16[256,1024]{1,0:T(8,128)(2,1)S(1)}, bf16[256,1024]{1,0:T(8,128)(2,1)S(1)}, u32[]{:S(2)}, u32[]{:S(2)}) collective-permute-start(bf16[256,1024]{1,0:T(8,128)(2,1)S(1)} %convolution_convert_fusion), channel_id=1, source_target_pairs={{0,2},{2,0},{1,3},{3,1},{4,6},{6,4},{5,7},{7,5},{8,10},{10,8},{9,1... | collective-permute-start | bytes 1572872 | tf_op jit(solution)/shard_map/ppermute | solution.py:155
  92.9 34.0 %collective-permute-start.28 = (bf16[128,2048]{1,0:T(8,128)(2,1)S(1)}, bf16[128,2048]{1,0:T(8,128)(2,1)S(1)}, u32[]{:S(2)}, u32[]{:S(2)}) collective-permute-start(bf16[128,2048]{1,0:T(8,128)(2,1)S(1)} %collective-permute-done.3.refs_1_), channel_id=1, source_target_pairs={{0,8},{4,12},{8,0},{12,4},{1,9},{5,13},{9,1},{13,5},{2,10},{6,14},... | collective-permute-start | bytes 1572872 | tf_op jit(solution)/shard_map/ppermute | solution.py:165
  105.1 31.4 %collective-permute-start.30 = (bf16[256,1024]{1,0:T(8,128)(2,1)S(1)}, bf16[256,1024]{1,0:T(8,128)(2,1)S(1)}, u32[]{:S(2)}, u32[]{:S(2)}) collective-permute-start(bf16[256,1024]{1,0:T(8,128)(2,1)S(1)} %collective-permute-done.17.refs_10_), channel_id=1, source_target_pairs={{0,2},{2,0},{1,3},{3,1},{4,6},{6,4},{5,7},{7,5},{8,10},{10,8},{9,1... | collective-permute-start | bytes 1572872 | tf_op jit(solution)/shard_map/ppermute | solution.py:155
  106.6 32.6 %collective-permute-start.22 = (bf16[128,2048]{1,0:T(8,128)(2,1)S(1)}, bf16[128,2048]{1,0:T(8,128)(2,1)S(1)}, u32[]{:S(2)}, u32[]{:S(2)}) collective-permute-start(bf16[128,2048]{1,0:T(8,128)(2,1)S(1)} %collective-permute-done.3.refs_1_), channel_id=1, source_target_pairs={{0,4},{4,8},{8,12},{1,5},{5,9},{9,13},{2,6},{6,10},{10,14},{3,7},{... | collective-permute-start | bytes 1572872 | tf_op jit(solution)/shard_map/ppermute | solution.py:163
  115.7 24.7 %collective-permute-start.25 = (bf16[128,2048]{1,0:T(8,128)(2,1)S(1)}, bf16[128,2048]{1,0:T(8,128)(2,1)S(1)}, u32[]{:S(2)}, u32[]{:S(2)}) collective-permute-start(bf16[128,2048]{1,0:T(8,128)(2,1)S(1)} %collective-permute-done.3.refs_1_), channel_id=1, source_target_pairs={{4,0},{8,4},{12,8},{5,1},{9,5},{13,9},{6,2},{10,6},{14,10},{7,3},{... | collective-permute-start | bytes 1572872 | tf_op jit(solution)/shard_map/ppermute | solution.py:164
  127.0 25.7 %collective-permute-start.31 = (bf16[128,2048]{1,0:T(8,128)(2,1)S(1)}, bf16[128,2048]{1,0:T(8,128)(2,1)S(1)}, u32[]{:S(2)}, u32[]{:S(2)}) collective-permute-start(bf16[128,2048]{1,0:T(8,128)(2,1)S(1)} %collective-permute-done.28.refs_10_), channel_id=1, source_target_pairs={{4,0},{8,12},{5,1},{9,13},{6,2},{10,14},{7,3},{11,15},{20,16},{24,... | collective-permute-start | bytes 1572872 | tf_op jit(solution)/shard_map/ppermute | solution.py:166
  137.9 14.1 %collective-permute-start.7 = (f32[64,512]{1,0:T(8,128)S(1)}, f32[64,512]{1,0:T(8,128)S(1)}, u32[]{:S(2)}, u32[]{:S(2)}) collective-permute-start(f32[64,512]{1,0:T(8,128)S(1)} %get-tuple-element.14), channel_id=1, source_target_pairs={{8,0},{12,4},{9,1},{13,5},{10,2},{14,6},{11,3},{15,7},{24,16},{28,... | collective-permute-start | bytes 393224 | tf_op jit(solution)/shard_map/ppermute | solution.py:250
  139.2 13.5 %collective-permute-start.6 = (f32[64,512]{1,0:T(8,128)S(1)}, f32[64,512]{1,0:T(8,128)S(1)}, u32[]{:S(2)}, u32[]{:S(2)}) collective-permute-start(f32[64,512]{1,0:T(8,128)S(1)} %get-tuple-element.12), channel_id=1, source_target_pairs={{4,0},{8,4},{12,8},{5,1},{9,5},{13,9},{6,2},{10,6},{14,10},{7,3},{... | collective-permute-start | bytes 393224 | tf_op jit(solution)/shard_map/ppermute | solution.py:250
  140.5 24.9 %collective-permute-start.33 = (bf16[256,1024]{1,0:T(8,128)(2,1)}, bf16[256,1024]{1,0:T(8,128)(2,1)S(1)}, u32[]{:S(2)}, u32[]{:S(2)}) collective-permute-start(bf16[256,1024]{1,0:T(8,128)(2,1)} %collective-permute-done.20.refs_13_), channel_id=1, source_target_pairs={{0,2},{2,0},{1,3},{3,1},{4,6},{6,4},{5,7},{7,5},{8,10},{10,8},{9,1... | collective-permute-start | bytes 1572872 | tf_op jit(solution)/shard_map/ppermute | solution.py:155
  146.5 18.9 %collective-permute-start.29 = (bf16[128,2048]{1,0:T(8,128)(2,1)S(1)}, bf16[128,2048]{1,0:T(8,128)(2,1)S(1)}, u32[]{:S(2)}, u32[]{:S(2)}) collective-permute-start(bf16[128,2048]{1,0:T(8,128)(2,1)S(1)} %collective-permute-done.28.refs_10_), channel_id=1, source_target_pairs={{0,1},{1,0},{2,3},{3,2},{4,5},{5,4},{6,7},{7,6},{8,9},{9,8},{10,11... | collective-permute-start | bytes 1572872 | tf_op jit(solution)/shard_map/ppermute | solution.py:155
  151.9 13.4 %collective-permute-start.23 = (bf16[128,2048]{1,0:T(8,128)(2,1)S(1)}, bf16[128,2048]{1,0:T(8,128)(2,1)S(1)}, u32[]{:S(2)}, u32[]{:S(2)}) collective-permute-start(bf16[128,2048]{1,0:T(8,128)(2,1)S(1)} %collective-permute-done.22.refs_4_), channel_id=1, source_target_pairs={{0,1},{1,0},{2,3},{3,2},{4,5},{5,4},{6,7},{7,6},{8,9},{9,8},{10,11... | collective-permute-start | bytes 1572872 | tf_op jit(solution)/shard_map/ppermute | solution.py:155
  152.6 12.7 %collective-permute-start.26 = (bf16[128,2048]{1,0:T(8,128)(2,1)S(1)}, bf16[128,2048]{1,0:T(8,128)(2,1)S(1)}, u32[]{:S(2)}, u32[]{:S(2)}) collective-permute-start(bf16[128,2048]{1,0:T(8,128)(2,1)S(1)} %collective-permute-done.25.refs_7_), channel_id=1, source_target_pairs={{0,1},{1,0},{2,3},{3,2},{4,5},{5,4},{6,7},{7,6},{8,9},{9,8},{10,11... | collective-permute-start | bytes 1572872 | tf_op jit(solution)/shard_map/ppermute | solution.py:155
  152.7 12.7 %collective-permute-start.32 = (bf16[128,2048]{1,0:T(8,128)(2,1)S(1)}, bf16[128,2048]{1,0:T(8,128)(2,1)S(1)}, u32[]{:S(2)}, u32[]{:S(2)}) collective-permute-start(bf16[128,2048]{1,0:T(8,128)(2,1)S(1)} %collective-permute-done.31.refs_13_), channel_id=1, source_target_pairs={{0,1},{1,0},{2,3},{3,2},{4,5},{5,4},{6,7},{7,6},{8,9},{9,8},{10,11... | collective-permute-start | bytes 1572872 | tf_op jit(solution)/shard_map/ppermute | solution.py:155
  (11 other events, 223.9 us)

commit v2 on v1

v2 whole, which is shorter than its diff:
```python
import functools

import jax
import jax.numpy as jnp
from jax import lax
from jax.experimental import pallas as pl
from jax.experimental.pallas import tpu as pltpu
from jax.sharding import PartitionSpec as P

HEAD_SIZE = 128
SUMMARY_TOKENS = 64
SCALE = HEAD_SIZE ** (-0.5)
NEG_FILL = -1e30
MARK = 20_000_000_000
VMEM_LIMIT = 48 * 1024 * 1024

VMEM = pltpu.MemorySpace.VMEM
SMEM = pltpu.MemorySpace.SMEM


def dot(a, b, contract):
    return lax.dot_general(a, b, (contract, ((), ())), preferred_element_type=jnp.float32)


def mask_bias(count_ref, id_column_ref, id_row_ref, shape, seg_len):
    rows = lax.broadcasted_iota(jnp.int32, shape, 0)
    cols = lax.broadcasted_iota(jnp.int32, shape, 1)
    own = (rows >= cols) & (id_column_ref[...] == id_row_ref[...])
    far = (cols >= seg_len) & (cols < seg_len + SUMMARY_TOKENS * count_ref[0, 0])
    return jnp.where(own | far, 0.0, NEG_FILL).astype(jnp.float32)


def softmax_rows(q_head, k_head, bias):
    scores = dot(q_head, k_head, ((1,), (1,))) * SCALE + bias
    top = jnp.max(scores, axis=-1, keepdims=True)
    expo = jnp.exp(scores - top)
    return expo / jnp.sum(expo, axis=-1, keepdims=True)


def forward_kernel(n_head, count_ref, idc_ref, idr_ref, q_ref, k_ref, v_ref, attn_ref, turned_ref, bias_ref):
    seg_len, q_width = q_ref.shape
    kv_heads = k_ref.shape[1] // HEAD_SIZE
    group = q_width // k_ref.shape[1]
    share = seg_len // n_head
    bias_ref[...] = mask_bias(count_ref, idc_ref, idr_ref, bias_ref.shape, seg_len)
    for kv in range(kv_heads):
        kv_cols = slice(kv * HEAD_SIZE, (kv + 1) * HEAD_SIZE)
        for g in range(group):
            h = kv * group + g
            cols = slice(h * HEAD_SIZE, (h + 1) * HEAD_SIZE)
            probs_b = softmax_rows(q_ref[:, cols], k_ref[:, kv_cols], bias_ref[...]).astype(jnp.bfloat16)
            attn = dot(probs_b, v_ref[:, kv_cols], ((1,), (0,))).astype(jnp.bfloat16)
            attn_ref[:, cols] = attn
            for core in range(n_head):
                to = lax.rem(core + n_head - count_ref[0, 1], n_head) * share
                turned_ref[pl.ds(pl.multiple_of(to, share), share), cols] = attn[core * share : (core + 1) * share]


def backward_kernel(count_ref, idc_ref, idr_ref, q_ref, k_ref, v_ref, attn_ref, d_mine_ref, d_part_ref, token_ref,
                    gq_ref, gkv_ref, bias_ref):
    seg_len, q_width = q_ref.shape
    kv_width = k_ref.shape[1]
    kv_heads = kv_width // HEAD_SIZE
    group = q_width // kv_width
    bias_ref[...] = mask_bias(count_ref, idc_ref, idr_ref, bias_ref.shape, seg_len)
    for kv in range(kv_heads):
        kv_cols = slice(kv * HEAD_SIZE, (kv + 1) * HEAD_SIZE)
        k_head = k_ref[:, kv_cols]
        v_head = v_ref[:, kv_cols]
        grad_k = jnp.zeros((k_ref.shape[0], HEAD_SIZE), jnp.float32)
        grad_v = jnp.zeros((k_ref.shape[0], HEAD_SIZE), jnp.float32)
        for g in range(group):
            h = kv * group + g
            cols = slice(h * HEAD_SIZE, (h + 1) * HEAD_SIZE)
            q_head = q_ref[:, cols]
            d_sum = d_mine_ref[:, cols]
            for part in range(d_part_ref.shape[0]):
                d_sum = d_sum + d_part_ref[part, :, cols].astype(jnp.float32)
            d_head = d_sum.astype(jnp.bfloat16)
            prob = softmax_rows(q_head, k_head, bias_ref[...])
            probs_b = prob.astype(jnp.bfloat16)
            delta = jnp.sum(
                d_head.astype(jnp.float32) * attn_ref[:, cols].astype(jnp.float32), axis=-1, keepdims=True
            )
            dprob = dot(d_head, v_head, ((1,), (1,)))
            ds_b = (prob * (dprob - delta)).astype(jnp.bfloat16)
            gq_ref[:, cols] = (SCALE * dot(ds_b, k_head, ((1,), (0,)))).astype(jnp.bfloat16)
            grad_k += dot(ds_b, q_head, ((0,), (0,)))
            grad_v += dot(probs_b, d_head, ((0,), (0,)))
        gkv_ref[:, kv_cols] = SCALE * grad_k
        gkv_ref[:, kv_width + kv * HEAD_SIZE : kv_width + (kv + 1) * HEAD_SIZE] = grad_v


def call_attention(kernel, out_shape, operands, bias_shape, flops):
    return pl.pallas_call(
        kernel,
        out_shape=out_shape,
        in_specs=[pl.BlockSpec(memory_space=SMEM)] + [pl.BlockSpec(memory_space=VMEM)] * (len(operands) - 1),
        out_specs=jax.tree.map(lambda _: pl.BlockSpec(memory_space=VMEM), out_shape),
        scratch_shapes=[pltpu.VMEM(bias_shape, jnp.float32)],
        compiler_params=pltpu.CompilerParams(vmem_limit_bytes=VMEM_LIMIT),
        cost_estimate=pl.CostEstimate(flops=flops, bytes_accessed=4 << 20, transcendentals=1 << 20),
    )(*operands)


def mark_kernel(*refs):
    refs[-1][...] = refs[0][...]


def mark(token, *done):
    return pl.pallas_call(
        mark_kernel,
        out_shape=jax.ShapeDtypeStruct(token.shape, token.dtype),
        in_specs=[pl.BlockSpec(memory_space=VMEM)] + [pl.BlockSpec(memory_space=pl.ANY)] * len(done),
        out_specs=pl.BlockSpec(memory_space=VMEM),
        cost_estimate=pl.CostEstimate(flops=MARK, bytes_accessed=0, transcendentals=0),
    )(token, *done)


def outer(rows, attn):
    contract = tuple(range(rows.ndim - 1))
    return dot(rows, attn, (contract, contract))


def turn(x, axis, step, name):
    n = lax.axis_size(axis)
    with jax.named_scope(name):
        return lax.ppermute(x, axis, [(i, (i + step) % n) for i in range(n)])


def line_pairs(n, step):
    return [(i, i + step) for i in range(n) if 0 <= i + step < n]


def pairs(x, name):
    with jax.named_scope(name + "_pairs"):
        return lax.ppermute(x, "ctx", [(0, 1), (1, 0), (2, 3), (3, 2)])


def middle(x, name):
    with jax.named_scope(name + "_middle"):
        return lax.ppermute(x, "ctx", [(1, 2), (2, 1)])


def two_away(x, name):
    with jax.named_scope(name + "_two"):
        return lax.ppermute(x, "ctx", [(0, 2), (1, 3), (2, 0), (3, 1)])


def ends(x, name):
    with jax.named_scope(name + "_ends"):
        return lax.ppermute(x, "ctx", [(1, 0), (2, 3)])


def gate(arrays, *done):
    out = lax.optimization_barrier((*arrays, *done))
    return list(out[: len(arrays)]), list(out[len(arrays) :])


def shards(queries, keys, values, tok_ids, vis_start, out_weight, grad_out):
    seg_len = queries.shape[1]
    kv_width = keys.shape[2]
    d_model = grad_out.shape[2]
    part_rows = out_weight.shape[0]
    n_ctx = lax.axis_size("ctx")
    n_dp = lax.axis_size("dp")
    n_head = lax.axis_size("head")
    place = lax.axis_index("ctx")
    me_dp = lax.axis_index("dp")
    me_head = lax.axis_index("head")
    half = seg_len // n_head
    cut = seg_len - SUMMARY_TOKENS

    tail = jnp.concatenate([keys[0, cut:], values[0, cut:]], axis=1)
    far = [lax.ppermute(tail, "ctx", line_pairs(n_ctx, s)) for s in range(1, n_ctx)]
    far_len = -(-(n_ctx - 1) * SUMMARY_TOKENS // HEAD_SIZE) * HEAD_SIZE
    far.append(jnp.zeros((far_len - (n_ctx - 1) * SUMMARY_TOKENS, 2 * kv_width), keys.dtype))
    far = jnp.concatenate(far, axis=0)
    all_keys = jnp.concatenate([keys[0], far[:, :kv_width]], axis=0)
    all_vals = jnp.concatenate([values[0], far[:, kv_width:]], axis=0)
    n_keys = seg_len + far_len

    wide = n_ctx != 4
    token = jnp.zeros((8, 128), jnp.float32)

    def rows_of(core, dp):
        return lax.dynamic_slice(grad_out[0], (core * half, dp * part_rows), (half, part_rows))

    own = rows_of(me_head, me_dp)
    peer, peer_other = [], []
    for s in range(1, n_dp):
        to = lax.rem(me_dp + s, n_dp)
        peer.append(turn(rows_of(me_head, to), "dp", s, "peer_in"))

    count = jnp.stack([place - vis_start[0, 0], me_head]).reshape(1, 2).astype(jnp.int32)
    id_column = tok_ids[0].reshape(seg_len, 1)
    id_row = jnp.pad(tok_ids, ((0, 0), (0, far_len)), constant_values=-1)
    pair_flops = 2 * seg_len * n_keys * queries.shape[2]
    attn, turned = call_attention(
        functools.partial(forward_kernel, n_head),
        (jax.ShapeDtypeStruct(queries.shape[1:], jnp.bfloat16),) * 2,
        (count, id_column, id_row, queries[0], all_keys, all_vals),
        (seg_len, n_keys),
        2 * pair_flops,
    )

    peer, (attn,) = gate(peer, attn)
    peer_other = [turn(x, "head", 1, "peer_s") for x in peer]
    first_core = me_head == 0
    parts = []
    for s in range(1, n_dp):
        mine, other = peer[s - 1], peer_other[s - 1]
        rows = jnp.concatenate([jnp.where(first_core, mine, other), jnp.where(first_core, other, mine)], 0)
        parts.append(jnp.dot(rows, out_weight, preferred_element_type=jnp.float32).astype(jnp.bfloat16))
    back = [turn(part, "dp", -s, "back") for s, part in zip(range(1, n_dp), parts)]
    own_rows = lax.dynamic_slice(grad_out[0], (0, me_dp * part_rows), (seg_len, part_rows))
    d_mine = jnp.dot(own_rows, out_weight, preferred_element_type=jnp.float32)
    d_part = jnp.stack(back)

    def backward(d_part):
        return call_attention(
            backward_kernel,
            (
                jax.ShapeDtypeStruct(queries.shape[1:], jnp.bfloat16),
                jax.ShapeDtypeStruct((n_keys, 2 * kv_width), jnp.float32),
            ),
            (count, id_column, id_row, queries[0], all_keys, all_vals, attn, d_mine, d_part, token),
            (seg_len, n_keys),
            5 * pair_flops,
        )


    def send_home(grad_kv):
        sent = []
        for s in range(1, n_ctx):
            begin = seg_len + (s - 1) * SUMMARY_TOKENS
            with jax.named_scope("grads"):
                sent.append(lax.ppermute(grad_kv[begin : begin + SUMMARY_TOKENS], "ctx", line_pairs(n_ctx, -s)))
        return sent

    def add_home(grad_kv, sent):
        home = sum(sent, grad_kv[cut:seg_len])
        return jnp.concatenate([grad_kv[:cut], home], 0).astype(jnp.bfloat16)

    if wide:
        grad_q, grad_kv = backward(d_part)
        out_kv = add_home(grad_kv, send_home(grad_kv))
        block = d_model // (n_ctx * n_dp)
        columns = (
            grad_out[0].reshape(seg_len, n_dp, n_ctx, block).transpose(0, 2, 1, 3).reshape(seg_len, d_model)
        )
        shard = lax.psum_scatter(
            jnp.einsum("sd,se->de", columns, attn, preferred_element_type=jnp.float32),
            ("ctx", "dp"),
            scatter_dimension=0,
            tiled=True,
        ).astype(jnp.bfloat16)
        weight_grad = lax.all_gather(shard, "ctx", axis=0, tiled=True)
    else:
        steps = range(1, n_dp)
        at_end = (place == 0) | (place == n_ctx - 1)

        def swap(x, name):
            return turn(x, "head", 1, name)

        own_1 = pairs(own, "own")
        own_2 = two_away(own, "own")
        own_mid = middle(own, "own")
        attn_1 = pairs(turned, "attn")
        attn_x0 = [turn(turned, "dp", s, "attn_x0") for s in steps]
        token = mark(token, own_1, own_2, own_mid)
        (attn_0, own_2, *peer), (token,) = gate([turned, own_2, *peer], token)
        own_end = ends(own_2, "own")
        peer_1 = [pairs(x, "peer") for x in peer]
        attn_mid_a = middle(attn_0, "attn_a")
        token = mark(token)
        (attn_1,), (token,) = gate([attn_1], token)
        attn_mid_b = middle(attn_1, "attn_b")
        attn_end_a = ends(attn_mid_a, "attn_a")
        attn_x1 = [turn(attn_1, "dp", s, "attn_x1") for s in steps]
        peer_pair = [jnp.stack([a, b]) for a, b in zip(peer, peer_1)]
        peer_pair, (attn_mid_b, own_end, d_part) = gate(peer_pair, attn_mid_b, own_end, d_part)
        attn_end_b = ends(attn_mid_b, "attn_b")
        peer_mid = [middle(x, "peer") for x in peer_pair]
        attn_a = jnp.where(at_end, attn_end_a, attn_mid_a)
        attn_b = jnp.where(at_end, attn_end_b, attn_mid_b)
        attn_xa = [turn(attn_a, "dp", s, "attn_xa") for s in steps]
        attn_xb = [turn(attn_b, "dp", s, "attn_xb") for s in steps]
        own_all = jnp.stack([own_1, own_2, jnp.where(at_end, own_end, own_mid)])
        own_all_s = swap(own_all, "own_s")
        peer_1s = [swap(x, "peer_1s") for x in peer_1]
        grad_q, grad_kv = backward(d_part)
        peer_send, (own_all_s, grad_kv, *rest) = gate(peer_mid, own_all_s, grad_kv, *peer_1s, *attn_x1)
        peer_1s, attn_x1 = rest[: n_dp - 1], rest[n_dp - 1 :]
        peer_end = [ends(x, "peer") for x in peer_send]
        peer_mid_s = [swap(x, "peer_mid_s") for x in peer_send]
        attn_all = jnp.stack([attn_1, jnp.where(at_end, attn_a, attn_b), jnp.where(at_end, attn_b, attn_a)])
        share = own_all.shape[0] * half
        rows = jnp.concatenate([own_rows, own_all.reshape(share, -1), own_all_s.reshape(share, -1)], 0)
        cols = [attn, attn_all[:, :half].reshape(share, -1), attn_all[:, half:].reshape(share, -1)]
        total = outer(rows, jnp.concatenate(cols, 0))
        for s in steps:
            rows = [peer[s - 1], peer_other[s - 1], peer_1[s - 1], peer_1s[s - 1]]
            total += outer(jnp.concatenate(rows, 0), jnp.concatenate([attn_x0[s - 1], attn_x1[s - 1]], 0))
        sent = send_home(grad_kv)
        peer_end, (total, *rest) = gate(peer_end, total, *attn_xa, *attn_xb)
        attn_xa, attn_xb = rest[: n_dp - 1], rest[n_dp - 1 :]
        for part, mid, end in ((0, peer_mid, peer_end), (1, peer_mid_s, [swap(x, "peer_end_s") for x in peer_end])):
            for s in steps:
                rows = lax.optimization_barrier(jnp.where(at_end, end[s - 1], mid[s - 1]))
                cols = [x[s - 1][part * half : (part + 1) * half] for x in (attn_xa, attn_xb)]
                total += outer(rows.reshape(2 * half, -1), jnp.concatenate(cols, 0))
        weight_grad = total.astype(jnp.bfloat16)
        sent, (weight_grad,) = gate(sent, weight_grad)
        out_kv = add_home(grad_kv, sent)
    out_k, out_v = out_kv[:, :kv_width], out_kv[:, kv_width:]
    return (grad_q[None], out_k[None], out_v[None], weight_grad)


def solution(mesh):
    placed = (
        P(("groups", "dp"), "ctx", "head"),
        P(("groups", "dp"), "ctx", "head"),
        P(("groups", "dp"), "ctx", "head"),
        P(("groups", "dp"), "ctx"),
        P(("groups", "dp"), "ctx"),
        P("dp", "head"),
        P(("groups", "dp"), "ctx", None),
    )
    return jax.shard_map(
        shards,
        mesh=mesh,
        in_specs=placed,
        out_specs=(
            P(("groups", "dp"), "ctx", "head"),
            P(("groups", "dp"), "ctx", "head"),
            P(("groups", "dp"), "ctx", "head"),
            P(("groups", "dp"), "head"),
        ),
        check_vma=False,
    )
```

time: 179 us -> 150 us (0.84)
  waiting for transfers between devices: 82.2 us -> 43.8 us
  matrix products: 4.87 us -> 25.8 us
  Pallas kernels: 33.9 us -> 13 us
  other arithmetic: 2.79 us -> 9.62 us
  starting transfers between devices: 46 us -> 48.7 us
    ppermute x15, waiting for transfers between devices: 64.6 us -> 39.3 us  [the longest x4 26.5 us: ends(): return lax.ppermute(x, 'ctx', [(1, 0), (2, 3)])]
    dot_general x0 -> x4, matrix products: none -> 20.3 us  [dot(): lax.dot_general(a, b, (contract, ((), ())), preferred_element_type=jnp.fl...]
    pallas_call x2, Pallas kernels: 22.7 us -> 2.56 us  [mark(): pl.pallas_call(mark_kernel, out_shape=jax.ShapeDtypeStruct(token.shape, t...]
    ppermute x16 -> x11, waiting for transfers between devices: 17.6 us -> 4.47 us  [turn(): return lax.ppermute(x, axis, [(i, (i + step) % n) for i in range(n)])]
    another operation x1 -> x7, other arithmetic: 0.04 us -> 5.32 us  [the longest x2 2.48 us: shards(): own_all = jnp.stack([own_1, own_2, jnp.where(at_end, own_end, own_mid)])]
    ppermute x15, starting transfers between devices: 24.5 us -> 29.7 us  [the longest x3 14.8 us: pairs(): return lax.ppermute(x, 'ctx', [(0, 1), (1, 0), (2, 3), (3, 2)])]
    ppermute x16 -> x11, starting transfers between devices: 10.8 us -> 8.27 us  [turn(): return lax.ppermute(x, axis, [(i, (i + step) % n) for i in range(n)])]
  transfers between devices with their start and end apart: 34 -> 29, of which waited for: 11 -> 11; matrix products, arithmetic and copies ran while one was open for 7% -> 27% of each run, Pallas kernels for 13% -> 9%
where the time goes in v2:
time: 150 us; the launch traced here: 149 us
  starting transfers between devices  48.7 us (32%)
  waiting for transfers between devices  43.8 us (29%)
  matrix products  25.8 us (17%)
  Pallas kernels  13 us (9%)
  other arithmetic  9.62 us (6%)
  local copies, waits for them, and re-layouts  6.91 us (5%)
  between operations  1.67 us (1%)
    ppermute x4, waiting for transfers between devices, ends(): return lax.ppermute(x, 'ctx', [(1, 0), (2, 3)])  26.5 us
    dot_general x4, matrix products, dot(): lax.dot_general(a, b, (contract, ((), ())), preferred_element_type=jnp.fl...  20.3 us
    ppermute x3, starting transfers between devices, pairs(): return lax.ppermute(x, 'ctx', [(0, 1), (1, 0), (2, 3), (3, 2)])  14.8 us
    ppermute x3, starting transfers between devices, shards(): lax.ppermute(tail, 'ctx', line_pairs(n_ctx, s))  10.7 us
    pallas_call x2, Pallas kernels, call_attention(): pl.pallas_call(kernel, out_shape=out_shape, in_specs=[pl.BlockSpec(memory...  10.4 us
    ppermute x11, starting transfers between devices, turn(): return lax.ppermute(x, axis, [(i, (i + step) % n) for i in range(n)])  8.27 us
    ppermute x1, waiting for transfers between devices, two_away(): return lax.ppermute(x, 'ctx', [(0, 2), (1, 3), (2, 0), (3, 1)])  7.25 us
    ppermute x4, starting transfers between devices, middle(): return lax.ppermute(x, 'ctx', [(1, 2), (2, 1)])  5.43 us
  transfers between devices with their start and end apart: 29, of which 11 were waited for; matrix products, arithmetic and copies ran while one was open for 27% of the time, Pallas kernels for 9%

profile of v2, /device:TPU:0, one launch (start us, length us, event | category | flops | bytes accessed | tf_op | source)
XLA Modules:
  0.0 149.4 jit_solution(14153824554430921469)
XLA Ops:
  1.5 4.9 %collective-permute-start = (bf16[64,512]{1,0:T(8,128)(2,1)S(1)}, bf16[64,512]{1,0:T(8,128)(2,1)S(1)}, u32[]{:S(2)}, u32[]{:S(2)}) collective-permute-start(bf16[64,512]{1,0:T(8,128)(2,1)S(1)} %pad_maximum_fusion.6), channel_id=1, source_target_pairs={{0,4},{4,8},{8,12},{1,5},{5,9},{9,13},{2,6},{6,10},{10,14},{3,7},{... | collective-permute-start | bytes 196616 | tf_op jit(solution)/shard_map/ppermute | solution.py:175
  6.4 4.5 %collective-permute-start.1 = (bf16[64,512]{1,0:T(8,128)(2,1)S(1)}, bf16[64,512]{1,0:T(8,128)(2,1)S(1)}, u32[]{:S(2)}, u32[]{:S(2)}) collective-permute-start(bf16[64,512]{1,0:T(8,128)(2,1)S(1)} %pad_maximum_fusion.6), channel_id=1, source_target_pairs={{0,8},{4,12},{1,9},{5,13},{2,10},{6,14},{3,11},{7,15},{16,24},{20,... | collective-permute-start | bytes 196616 | tf_op jit(solution)/shard_map/ppermute | solution.py:175
  12.2 2.1 %dynamic-slice_bitcast_fusion.1 = (bf16[128,2048]{1,0:T(8,128)(2,1)}, bf16[128,2048]{1,0:T(8,128)(2,1)S(1)}) fusion(bf16[1,256,4096]{2,1,0:T(8,128)(2,1)} %param.13, s32[]{:T(128)S(6)} %select_n.61, s32[]{:T(128)S(6)} %select_n.63, s32[]{:T(128)S(6)} %select_n.62), kind=kLoop, calls=%fused_computation.45 | loop fusion | bytes 2097164 | tf_op jit(solution)/shard_map/dynamic_slice | solution.py:187
  16.7 1.5 collective-permute-start.6
  18.1 1.5 collective-permute-start.3
  21.6 4.1 %shard_map.102 = (bf16[256,1024]{1,0:T(8,128)(2,1)S(1)}, bf16[256,1024]{1,0:T(8,128)(2,1)S(1)}) custom-call(s32[1,2]{1,0:T(1,128)S(1)} %add_bitcast_fusion.count_ref, s32[256,1]{1,0:T(8,128)S(1)} %copy.12.idc_ref, s32[1,512]{1,0:T(1,128)S(1)} %pad.4.idr_ref, bf16[256,1024]{1,0:T(8,128)(2,1)S(1)} %bitcast.48, bf16[512,256]{1,0:T(8,128)(2,1)S(1)} %pad_maximum_fusion.3.k_ref, ...), custom_call_target="tpu_custom_call" | custom-call | flops 536870912 | bytes 4194304 | tf_op jit(solution)/shard_map/pallas_call | solution.py:95
  25.8 4.1 %collective-permute-start.8 = (bf16[256,1024]{1,0:T(8,128)(2,1)S(1)}, bf16[256,1024]{1,0:T(8,128)(2,1)}, u32[]{:S(2)}, u32[]{:S(2)}) collective-permute-start(bf16[256,1024]{1,0:T(8,128)(2,1)S(1)} %get-tuple-element.50), channel_id=1, source_target_pairs={{0,4},{4,0},{8,12},{12,8},{1,5},{5,1},{9,13},{13,9},{2,6},{6,2},{1... | collective-permute-start | bytes 1572872 | tf_op jit(solution)/shard_map/attn_pairs/ppermute | solution.py:137
  29.8 1.4 collective-permute-done.3
  31.3 7.3 %collective-permute-done.4.refs_2_ = bf16[128,2048]{1,0:T(8,128)(2,1)} collective-permute-done((bf16[128,2048]{1,0:T(8,128)(2,1)}, bf16[128,2048]{1,0:T(8,128)(2,1)}, u32[]{:S(2)}, u32[]{:S(2)}) %collective-permute-start.4) | collective-permute-done | bytes 524320 | tf_op jit(solution)/shard_map/own_two/ppermute | solution.py:147
  42.6 10.7 %collective-permute-start.7 = (bf16[128,2048]{1,0:T(8,128)(2,1)S(1)}, bf16[128,2048]{1,0:T(8,128)(2,1)}, u32[]{:S(2)}, u32[]{:S(2)}) collective-permute-start(bf16[128,2048]{1,0:T(8,128)(2,1)S(1)} %collective-permute-done.3), channel_id=1, source_target_pairs={{0,4},{4,0},{8,12},{12,8},{1,5},{5,1},{9,13},{13,9},{2,6},{6,2},{1... | collective-permute-start | bytes 1572872 | tf_op jit(solution)/shard_map/peer_pairs/ppermute | solution.py:137
  54.7 1.5 %collective-permute-start.9 = (bf16[256,1024]{1,0:T(8,128)(2,1)}, bf16[256,1024]{1,0:T(8,128)(2,1)}, u32[]{:S(2)}, u32[]{:S(2)}) collective-permute-start(bf16[256,1024]{1,0:T(8,128)(2,1)} %collective-permute-done.8), channel_id=1, source_target_pairs={{4,8},{8,4},{5,9},{9,5},{6,10},{10,6},{7,11},{11,7},{20,24},{24,20... | collective-permute-start | bytes 1572872 | tf_op jit(solution)/shard_map/attn_b_middle/ppermute | solution.py:142
  57.0 4.3 %convolution_convert_fusion = bf16[256,1024]{1,0:T(8,128)(2,1)} fusion(bf16[2048,1024]{1,0:T(8,128)(2,1)} %param.12, bf16[128,2048]{1,0:T(8,128)(2,1)S(1)} %get-tuple-element.73, bf16[128,2048]{1,0:T(8,128)(2,1)S(1)} %get-tuple-element.72), kind=kOutput, calls=%fused_computation.23 | convolution fusion | flops 1076101120 | bytes 5767168 | tf_op jit(solution)/shard_map/dot_general | solution.py:214
  61.2 1.5 collective-permute-start.12
  63.6 2.6 %collective-permute-done.7 = bf16[128,2048]{1,0:T(8,128)(2,1)} collective-permute-done((bf16[128,2048]{1,0:T(8,128)(2,1)S(1)}, bf16[128,2048]{1,0:T(8,128)(2,1)}, u32[]{:S(2)}, u32[]{:S(2)}) %collective-permute-start.7) | collective-permute-done | bytes 524320 | tf_op jit(solution)/shard_map/peer_pairs/ppermute | solution.py:137
  67.5 9.3 %collective-permute-done.10 = bf16[128,2048]{1,0:T(8,128)(2,1)} collective-permute-done((bf16[128,2048]{1,0:T(8,128)(2,1)}, bf16[128,2048]{1,0:T(8,128)(2,1)}, u32[]{:S(2)}, u32[]{:S(2)}) %collective-permute-start.10) | collective-permute-done | bytes 524320 | tf_op jit(solution)/shard_map/own_ends/ppermute | solution.py:152
  77.9 1.4 pad_maximum_fusion
  79.5 1.4 collective-permute-start.22
  83.5 1.6 %collective-permute-start.24 = (bf16[256,1024]{1,0:T(8,128)(2,1)S(1)}, bf16[256,1024]{1,0:T(8,128)(2,1)S(1)}, u32[]{:S(2)}, u32[]{:S(2)}) collective-permute-start(bf16[256,1024]{1,0:T(8,128)(2,1)S(1)} %get-tuple-element.50), channel_id=1, source_target_pairs={{0,2},{2,0},{1,3},{3,1},{4,6},{6,4},{5,7},{7,5},{8,10},{10,8},{9,1... | collective-permute-start | bytes 1572872 | tf_op jit(solution)/shard_map/attn_x0/ppermute | solution.py:128
  85.1 1.6 %collective-permute-start.13 = (bf16[2,128,2048]{2,1,0:T(8,128)(2,1)S(1)}, bf16[2,128,2048]{2,1,0:T(8,128)(2,1)}, u32[]{:S(2)}, u32[]{:S(2)}) collective-permute-start(bf16[2,128,2048]{2,1,0:T(8,128)(2,1)S(1)} %pad_maximum_fusion.2), channel_id=1, source_target_pairs={{4,8},{8,4},{5,9},{9,5},{6,10},{10,6},{7,11},{11,7},{20,24},{24,20... | collective-permute-start | bytes 3145736 | tf_op jit(solution)/shard_map/peer_middle/ppermute | solution.py:142
  86.7 6.3 %shard_map.105 = (bf16[256,1024]{1,0:T(8,128)(2,1)}, f32[512,512]{1,0:T(8,128)S(1)}) custom-call(s32[1,2]{1,0:T(1,128)S(1)} %add_bitcast_fusion.count_ref, s32[256,1]{1,0:T(8,128)S(1)} %copy.12.idc_ref, s32[1,512]{1,0:T(1,128)S(1)} %pad.4.idr_ref, bf16[256,1024]{1,0:T(8,128)(2,1)S(1)} %bitcast.49, bf16[512,256]{1,0:T(8,128)(2,1)S(1)} %pad_maximum_fusion.3.k_ref, ...), custom_call_target="tpu_custom_call" | custom-call | flops 1342177280 | bytes 4194304 | tf_op jit(solution)/shard_map/pallas_call | solution.py:95
  93.0 5.8 %collective-permute-done.22 = bf16[256,1024]{1,0:T(8,128)(2,1)S(1)} collective-permute-done((bf16[256,1024]{1,0:T(8,128)(2,1)S(1)}, bf16[256,1024]{1,0:T(8,128)(2,1)S(1)}, u32[]{:S(2)}, u32[]{:S(2)}) %collective-permute-start.22) | collective-permute-done | bytes 524320 | tf_op jit(solution)/shard_map/attn_a_ends/ppermute | solution.py:152
  98.8 1.5 collective-permute-start.16
  100.3 7.5 %collective-permute-done.23 = bf16[256,1024]{1,0:T(8,128)(2,1)S(1)} collective-permute-done((bf16[256,1024]{1,0:T(8,128)(2,1)}, bf16[256,1024]{1,0:T(8,128)(2,1)S(1)}, u32[]{:S(2)}, u32[]{:S(2)}) %collective-permute-start.23) | collective-permute-done | bytes 524320 | tf_op jit(solution)/shard_map/attn_b_ends/ppermute | solution.py:152
  109.6 1.6 %collective-permute-start.25 = (bf16[256,1024]{1,0:T(8,128)(2,1)S(1)}, bf16[256,1024]{1,0:T(8,128)(2,1)S(1)}, u32[]{:S(2)}, u32[]{:S(2)}) collective-permute-start(bf16[256,1024]{1,0:T(8,128)(2,1)S(1)} %get-tuple-element.63), channel_id=1, source_target_pairs={{0,2},{2,0},{1,3},{3,1},{4,6},{6,4},{5,7},{7,5},{8,10},{10,8},{9,1... | collective-permute-start | bytes 1572872 | tf_op jit(solution)/shard_map/attn_xa/ppermute | solution.py:128
  113.8 1.6 %collective-permute-start.17 = (f32[64,512]{1,0:T(8,128)}, f32[64,512]{1,0:T(8,128)S(1)}, u32[]{:S(2)}, u32[]{:S(2)}) collective-permute-start(f32[64,512]{1,0:T(8,128)} %get-tuple-element.71), channel_id=1, source_target_pairs={{4,0},{8,4},{12,8},{5,1},{9,5},{13,9},{6,2},{10,6},{14,10},{7,3},{... | collective-permute-start | bytes 393224 | tf_op jit(solution)/shard_map/grads/ppermute | solution.py:238
  115.4 6.7 %fusion.14 = f32[2048,1024]{1,0:T(8,128)} fusion(bf16[128,2048]{1,0:T(8,128)(2,1)S(1)} %collective-permute-done.15, bf16[128,2048]{1,0:T(8,128)(2,1)} %collective-permute-done.7, bf16[128,2048]{1,0:T(8,128)(2,1)S(1)} %copy-done.6, bf16[128,2048]{1,0:T(8,128)(2,1)S(1)} %collective-permute-done.3, bf16[256,1024]{1,0:T(8,128)(2,1)S(1)} %collective-permute-done.16, ...), kind=kOutput, calls=%fused_computation.13 | convolution fusion | flops 2157969408 | bytes 11534336 | tf_op jit(solution)/shard_map/dot_general | solution.py:22
  122.2 8.8 %fusion.6 = f32[2048,1024]{1,0:T(8,128)S(1)} fusion(f32[2048,1024]{1,0:T(8,128)} %fusion.14, bf16[384,2048]{1,0:T(8,128)(2,1)} %bitcast.60, bf16[384,2048]{1,0:T(8,128)(2,1)S(1)} %bitcast.54, bf16[256,2048]{1,0:T(8,128)(2,1)S(1)} %copy-done.4, bf16[384,1024]{1,0:T(8,128)(2,1)S(1)} %bitcast.56, bf16[384,1024]{1,0:T(8,128)(2,1)S(1)} %bitcast.55, ...), kind=kOutput, calls=%fused_computation.7 | convolution fusion | flops 4315938816 | bytes 23068672 | tf_op jit(solution)/shard_map/dot_general | solution.py:22
  132.3 2.9 %collective-permute-done.26 = bf16[256,1024]{1,0:T(8,128)(2,1)S(1)} collective-permute-done((bf16[256,1024]{1,0:T(8,128)(2,1)S(1)}, bf16[256,1024]{1,0:T(8,128)(2,1)S(1)}, u32[]{:S(2)}, u32[]{:S(2)}) %collective-permute-start.26) | collective-permute-done | bytes 524320 | tf_op jit(solution)/shard_map/attn_xb/ppermute | solution.py:128
  136.5 3.8 %collective-permute-done.20 = bf16[2,128,2048]{2,1,0:T(8,128)(2,1)} collective-permute-done((bf16[2,128,2048]{2,1,0:T(8,128)(2,1)}, bf16[2,128,2048]{2,1,0:T(8,128)(2,1)}, u32[]{:S(2)}, u32[]{:S(2)}) %collective-permute-start.20) | collective-permute-done | bytes 1048608 | tf_op jit(solution)/shard_map/peer_ends/ppermute | solution.py:152
  140.3 1.3 broadcast_select_fusion.1
  143.3 3.4 %add_convert_fusion = bf16[2048,1024]{1,0:T(8,128)(2,1)} fusion(f32[2048,1024]{1,0:T(8,128)S(1)} %fusion.6, f32[2048,1024]{1,0:T(8,128)S(1)} %fusion.28, bf16[256,2048]{1,0:T(8,128)(2,1)S(1)} %bitcast.52, bf16[128,1024]{1,0:T(8,128)(2,1)S(1)} %get-tuple-element.76, bf16[128,1024]{1,0:T(8,128)(2,1)S(1)} %get-tuple-element.74), kind=kOutput, calls=%fused_computation | convolution fusion | flops 1081081856 | bytes 22544384 | tf_op jit(solution)/shard_map/dot_general | solution.py:22
  146.7 1.9 %collective-permute-done.18 = f32[64,512]{1,0:T(8,128)S(1)} collective-permute-done((f32[64,512]{1,0:T(8,128)S(1)}, f32[64,512]{1,0:T(8,128)S(1)}, u32[]{:S(2)}, u32[]{:S(2)}) %collective-permute-start.18) | collective-permute-done | bytes 131104 | tf_op jit(solution)/shard_map/grads/ppermute | solution.py:238
  (84 shorter events, 27.2 us)
Async XLA Ops:
  0.6 21.0 %copy-start = (bf16[1,256,1024]{2,1,0:T(8,128)(2,1)S(1)}, bf16[1,256,1024]{2,1,0:T(8,128)(2,1)}, u32[]{:S(2)}) copy-start(bf16[1,256,1024]{2,1,0:T(8,128)(2,1)} %param.7) | copy-start | bytes 1572868
  1.5 15.2 %collective-permute-start = (bf16[64,512]{1,0:T(8,128)(2,1)S(1)}, bf16[64,512]{1,0:T(8,128)(2,1)S(1)}, u32[]{:S(2)}, u32[]{:S(2)}) collective-permute-start(bf16[64,512]{1,0:T(8,128)(2,1)S(1)} %pad_maximum_fusion.6), channel_id=1, source_target_pairs={{0,4},{4,8},{8,12},{1,5},{5,9},{9,13},{2,6},{6,10},{10,14},{3,7},{... | collective-permute-start | bytes 196616 | tf_op jit(solution)/shard_map/ppermute | solution.py:175
  6.4 11.7 %collective-permute-start.1 = (bf16[64,512]{1,0:T(8,128)(2,1)S(1)}, bf16[64,512]{1,0:T(8,128)(2,1)S(1)}, u32[]{:S(2)}, u32[]{:S(2)}) collective-permute-start(bf16[64,512]{1,0:T(8,128)(2,1)S(1)} %pad_maximum_fusion.6), channel_id=1, source_target_pairs={{0,8},{4,12},{1,9},{5,13},{2,10},{6,14},{3,11},{7,15},{16,24},{20,... | collective-permute-start | bytes 196616 | tf_op jit(solution)/shard_map/ppermute | solution.py:175
  10.9 8.7 %collective-permute-start.2 = (bf16[64,512]{1,0:T(8,128)(2,1)S(1)}, bf16[64,512]{1,0:T(8,128)(2,1)S(1)}, u32[]{:S(2)}, u32[]{:S(2)}) collective-permute-start(bf16[64,512]{1,0:T(8,128)(2,1)S(1)} %pad_maximum_fusion.6), channel_id=1, source_target_pairs={{0,12},{1,13},{2,14},{3,15},{16,28},{17,29},{18,30},{19,31}} | collective-permute-start | bytes 196616 | tf_op jit(solution)/shard_map/ppermute | solution.py:175
  14.3 24.2 %collective-permute-start.4 = (bf16[128,2048]{1,0:T(8,128)(2,1)}, bf16[128,2048]{1,0:T(8,128)(2,1)}, u32[]{:S(2)}, u32[]{:S(2)}) collective-permute-start(bf16[128,2048]{1,0:T(8,128)(2,1)} %get-tuple-element.65), channel_id=1, source_target_pairs={{0,8},{4,12},{8,0},{12,4},{1,9},{5,13},{9,1},{13,5},{2,10},{6,14},... | collective-permute-start | bytes 1572872 | tf_op jit(solution)/shard_map/own_two/ppermute | solution.py:147
  14.3 25.1 %collective-permute-start.5 = (bf16[128,2048]{1,0:T(8,128)(2,1)}, bf16[128,2048]{1,0:T(8,128)(2,1)}, u32[]{:S(2)}, u32[]{:S(2)}) collective-permute-start(bf16[128,2048]{1,0:T(8,128)(2,1)} %get-tuple-element.65), channel_id=1, source_target_pairs={{0,4},{4,0},{8,12},{12,8},{1,5},{5,1},{9,13},{13,9},{2,6},{6,2},{1... | collective-permute-start | bytes 1572872 | tf_op jit(solution)/shard_map/own_pairs/ppermute | solution.py:137
  16.7 22.8 %collective-permute-start.6 = (bf16[128,2048]{1,0:T(8,128)(2,1)}, bf16[128,2048]{1,0:T(8,128)(2,1)}, u32[]{:S(2)}, u32[]{:S(2)}) collective-permute-start(bf16[128,2048]{1,0:T(8,128)(2,1)} %get-tuple-element.65), channel_id=1, source_target_pairs={{4,8},{8,4},{5,9},{9,5},{6,10},{10,6},{7,11},{11,7},{20,24},{24,20... | collective-permute-start | bytes 1572872 | tf_op jit(solution)/shard_map/own_middle/ppermute | solution.py:142
  18.1 13.1 %collective-permute-start.3 = (bf16[128,2048]{1,0:T(8,128)(2,1)S(1)}, bf16[128,2048]{1,0:T(8,128)(2,1)S(1)}, u32[]{:S(2)}, u32[]{:S(2)}) collective-permute-start(bf16[128,2048]{1,0:T(8,128)(2,1)S(1)} %get-tuple-element.66), channel_id=1, source_target_pairs={{0,2},{2,0},{1,3},{3,1},{4,6},{6,4},{5,7},{7,5},{8,10},{10,8},{9,1... | collective-permute-start | bytes 1572872 | tf_op jit(solution)/shard_map/peer_in/ppermute | solution.py:128
  25.8 28.9 %collective-permute-start.8 = (bf16[256,1024]{1,0:T(8,128)(2,1)S(1)}, bf16[256,1024]{1,0:T(8,128)(2,1)}, u32[]{:S(2)}, u32[]{:S(2)}) collective-permute-start(bf16[256,1024]{1,0:T(8,128)(2,1)S(1)} %get-tuple-element.50), channel_id=1, source_target_pairs={{0,4},{4,0},{8,12},{12,8},{1,5},{5,1},{9,13},{13,9},{2,6},{6,2},{1... | collective-permute-start | bytes 1572872 | tf_op jit(solution)/shard_map/attn_pairs/ppermute | solution.py:137
  31.2 24.9 %collective-permute-start.11 = (bf16[128,2048]{1,0:T(8,128)(2,1)S(1)}, bf16[128,2048]{1,0:T(8,128)(2,1)S(1)}, u32[]{:S(2)}, u32[]{:S(2)}) collective-permute-start(bf16[128,2048]{1,0:T(8,128)(2,1)S(1)} %collective-permute-done.3), channel_id=1, source_target_pairs={{0,1},{1,0},{2,3},{3,2},{4,5},{5,4},{6,7},{7,6},{8,9},{9,8},{10,11... | collective-permute-start | bytes 1572872 | tf_op jit(solution)/shard_map/peer_s/ppermute | solution.py:128
  42.6 23.6 %collective-permute-start.7 = (bf16[128,2048]{1,0:T(8,128)(2,1)S(1)}, bf16[128,2048]{1,0:T(8,128)(2,1)}, u32[]{:S(2)}, u32[]{:S(2)}) collective-permute-start(bf16[128,2048]{1,0:T(8,128)(2,1)S(1)} %collective-permute-done.3), channel_id=1, source_target_pairs={{0,4},{4,0},{8,12},{12,8},{1,5},{5,1},{9,13},{13,9},{2,6},{6,2},{1... | collective-permute-start | bytes 1572872 | tf_op jit(solution)/shard_map/peer_pairs/ppermute | solution.py:137
  53.4 23.4 %collective-permute-start.10 = (bf16[128,2048]{1,0:T(8,128)(2,1)}, bf16[128,2048]{1,0:T(8,128)(2,1)}, u32[]{:S(2)}, u32[]{:S(2)}) collective-permute-start(bf16[128,2048]{1,0:T(8,128)(2,1)} %collective-permute-done.4.refs_2_), channel_id=1, source_target_pairs={{4,0},{8,12},{5,1},{9,13},{6,2},{10,14},{7,3},{11,15},{20,16},{24,... | collective-permute-start | bytes 1572872 | tf_op jit(solution)/shard_map/own_ends/ppermute | solution.py:152
  54.7 22.1 %collective-permute-start.9 = (bf16[256,1024]{1,0:T(8,128)(2,1)}, bf16[256,1024]{1,0:T(8,128)(2,1)}, u32[]{:S(2)}, u32[]{:S(2)}) collective-permute-start(bf16[256,1024]{1,0:T(8,128)(2,1)} %collective-permute-done.8), channel_id=1, source_target_pairs={{4,8},{8,4},{5,9},{9,5},{6,10},{10,6},{7,11},{11,7},{20,24},{24,20... | collective-permute-start | bytes 1572872 | tf_op jit(solution)/shard_map/attn_b_middle/ppermute | solution.py:142
  61.2 15.6 %collective-permute-start.12 = (bf16[256,1024]{1,0:T(8,128)(2,1)}, bf16[256,1024]{1,0:T(8,128)(2,1)S(1)}, u32[]{:S(2)}, u32[]{:S(2)}) collective-permute-start(bf16[256,1024]{1,0:T(8,128)(2,1)} %convolution_convert_fusion), channel_id=1, source_target_pairs={{0,2},{2,0},{1,3},{3,1},{4,6},{6,4},{5,7},{7,5},{8,10},{10,8},{9,1... | collective-permute-start | bytes 1572872 | tf_op jit(solution)/shard_map/back/ppermute | solution.py:128
  62.7 16.6 %copy-start.2 = (bf16[1,256,4096]{2,1,0:T(8,128)(2,1)S(1)}, bf16[1,256,4096]{2,1,0:T(8,128)(2,1)}, u32[]{:S(2)}) copy-start(bf16[1,256,4096]{2,1,0:T(8,128)(2,1)} %param.13) | copy-start | bytes 6291460
  62.7 16.8 %collective-permute-start.21 = (bf16[256,1024]{1,0:T(8,128)(2,1)S(1)}, bf16[256,1024]{1,0:T(8,128)(2,1)S(1)}, u32[]{:S(2)}, u32[]{:S(2)}) collective-permute-start(bf16[256,1024]{1,0:T(8,128)(2,1)S(1)} %get-tuple-element.50), channel_id=1, source_target_pairs={{4,8},{8,4},{5,9},{9,5},{6,10},{10,6},{7,11},{11,7},{20,24},{24,20... | collective-permute-start | bytes 1572872 | tf_op jit(solution)/shard_map/attn_a_middle/ppermute | solution.py:142
  66.2 16.0 %copy-start.7 = (bf16[2048,1024]{1,0:T(8,128)(2,1)S(1)}, bf16[2048,1024]{1,0:T(8,128)(2,1)}, u32[]{:S(2)}) copy-start(bf16[2048,1024]{1,0:T(8,128)(2,1)} %param.12) | copy-start | bytes 12582916
  79.3 32.4 %collective-permute-start.14 = (bf16[3,128,2048]{2,1,0:T(8,128)(2,1)S(1)}, bf16[3,128,2048]{2,1,0:T(8,128)(2,1)S(1)}, u32[]{:S(2)}, u32[]{:S(2)}) collective-permute-start(bf16[3,128,2048]{2,1,0:T(8,128)(2,1)S(1)} %pad_maximum_fusion), channel_id=1, source_target_pairs={{0,1},{1,0},{2,3},{3,2},{4,5},{5,4},{6,7},{7,6},{8,9},{9,8},{10,11... | collective-permute-start | bytes 4718600 | tf_op jit(solution)/shard_map/own_s/ppermute | solution.py:128
  79.5 19.3 %collective-permute-start.22 = (bf16[256,1024]{1,0:T(8,128)(2,1)S(1)}, bf16[256,1024]{1,0:T(8,128)(2,1)S(1)}, u32[]{:S(2)}, u32[]{:S(2)}) collective-permute-start(bf16[256,1024]{1,0:T(8,128)(2,1)S(1)} %collective-permute-done.21), channel_id=1, source_target_pairs={{4,0},{8,12},{5,1},{9,13},{6,2},{10,14},{7,3},{11,15},{20,16},{24,... | collective-permute-start | bytes 1572872 | tf_op jit(solution)/shard_map/attn_a_ends/ppermute | solution.py:152
  80.9 26.9 %collective-permute-start.23 = (bf16[256,1024]{1,0:T(8,128)(2,1)}, bf16[256,1024]{1,0:T(8,128)(2,1)S(1)}, u32[]{:S(2)}, u32[]{:S(2)}) collective-permute-start(bf16[256,1024]{1,0:T(8,128)(2,1)} %collective-permute-done.9), channel_id=1, source_target_pairs={{4,0},{8,12},{5,1},{9,13},{6,2},{10,14},{7,3},{11,15},{20,16},{24,... | collective-permute-start | bytes 1572872 | tf_op jit(solution)/shard_map/attn_b_ends/ppermute | solution.py:152
  83.5 30.3 %collective-permute-start.24 = (bf16[256,1024]{1,0:T(8,128)(2,1)S(1)}, bf16[256,1024]{1,0:T(8,128)(2,1)S(1)}, u32[]{:S(2)}, u32[]{:S(2)}) collective-permute-start(bf16[256,1024]{1,0:T(8,128)(2,1)S(1)} %get-tuple-element.50), channel_id=1, source_target_pairs={{0,2},{2,0},{1,3},{3,1},{4,6},{6,4},{5,7},{7,5},{8,10},{10,8},{9,1... | collective-permute-start | bytes 1572872 | tf_op jit(solution)/shard_map/attn_x0/ppermute | solution.py:128
  85.1 26.6 %collective-permute-start.13 = (bf16[2,128,2048]{2,1,0:T(8,128)(2,1)S(1)}, bf16[2,128,2048]{2,1,0:T(8,128)(2,1)}, u32[]{:S(2)}, u32[]{:S(2)}) collective-permute-start(bf16[2,128,2048]{2,1,0:T(8,128)(2,1)S(1)} %pad_maximum_fusion.2), channel_id=1, source_target_pairs={{4,8},{8,4},{5,9},{9,5},{6,10},{10,6},{7,11},{11,7},{20,24},{24,20... | collective-permute-start | bytes 3145736 | tf_op jit(solution)/shard_map/peer_middle/ppermute | solution.py:142
  98.8 10.7 %collective-permute-start.16 = (bf16[256,1024]{1,0:T(8,128)(2,1)}, bf16[256,1024]{1,0:T(8,128)(2,1)S(1)}, u32[]{:S(2)}, u32[]{:S(2)}) collective-permute-start(bf16[256,1024]{1,0:T(8,128)(2,1)} %collective-permute-done.8), channel_id=1, source_target_pairs={{0,2},{2,0},{1,3},{3,1},{4,6},{6,4},{5,7},{7,5},{8,10},{10,8},{9,1... | collective-permute-start | bytes 1572872 | tf_op jit(solution)/shard_map/attn_x1/ppermute | solution.py:128
  107.9 3.3 %collective-permute-start.15 = (bf16[128,2048]{1,0:T(8,128)(2,1)}, bf16[128,2048]{1,0:T(8,128)(2,1)S(1)}, u32[]{:S(2)}, u32[]{:S(2)}) collective-permute-start(bf16[128,2048]{1,0:T(8,128)(2,1)} %collective-permute-done.7), channel_id=1, source_target_pairs={{0,1},{1,0},{2,3},{3,2},{4,5},{5,4},{6,7},{7,6},{8,9},{9,8},{10,11... | collective-permute-start | bytes 1572872 | tf_op jit(solution)/shard_map/peer_1s/ppermute | solution.py:128
  109.6 21.4 %collective-permute-start.25 = (bf16[256,1024]{1,0:T(8,128)(2,1)S(1)}, bf16[256,1024]{1,0:T(8,128)(2,1)S(1)}, u32[]{:S(2)}, u32[]{:S(2)}) collective-permute-start(bf16[256,1024]{1,0:T(8,128)(2,1)S(1)} %get-tuple-element.63), channel_id=1, source_target_pairs={{0,2},{2,0},{1,3},{3,1},{4,6},{6,4},{5,7},{7,5},{8,10},{10,8},{9,1... | collective-permute-start | bytes 1572872 | tf_op jit(solution)/shard_map/attn_xa/ppermute | solution.py:128
  111.1 24.1 %collective-permute-start.26 = (bf16[256,1024]{1,0:T(8,128)(2,1)S(1)}, bf16[256,1024]{1,0:T(8,128)(2,1)S(1)}, u32[]{:S(2)}, u32[]{:S(2)}) collective-permute-start(bf16[256,1024]{1,0:T(8,128)(2,1)S(1)} %get-tuple-element.64), channel_id=1, source_target_pairs={{0,2},{2,0},{1,3},{3,1},{4,6},{6,4},{5,7},{7,5},{8,10},{10,8},{9,1... | collective-permute-start | bytes 1572872 | tf_op jit(solution)/shard_map/attn_xb/ppermute | solution.py:128
  111.7 28.6 %collective-permute-start.20 = (bf16[2,128,2048]{2,1,0:T(8,128)(2,1)}, bf16[2,128,2048]{2,1,0:T(8,128)(2,1)}, u32[]{:S(2)}, u32[]{:S(2)}) collective-permute-start(bf16[2,128,2048]{2,1,0:T(8,128)(2,1)} %collective-permute-done.13), channel_id=1, source_target_pairs={{4,0},{8,12},{5,1},{9,13},{6,2},{10,14},{7,3},{11,15},{20,16},{24,... | collective-permute-start | bytes 3145736 | tf_op jit(solution)/shard_map/peer_ends/ppermute | solution.py:152
  113.0 30.1 %collective-permute-start.28 = (bf16[2,128,2048]{2,1,0:T(8,128)(2,1)}, bf16[2,128,2048]{2,1,0:T(8,128)(2,1)}, u32[]{:S(2)}, u32[]{:S(2)}) collective-permute-start(bf16[2,128,2048]{2,1,0:T(8,128)(2,1)} %collective-permute-done.13), channel_id=1, source_target_pairs={{0,1},{1,0},{2,3},{3,2},{4,5},{5,4},{6,7},{7,6},{8,9},{9,8},{10,11... | collective-permute-start | bytes 3145736 | tf_op jit(solution)/shard_map/peer_mid_s/ppermute | solution.py:128
  113.8 33.0 %collective-permute-start.17 = (f32[64,512]{1,0:T(8,128)}, f32[64,512]{1,0:T(8,128)S(1)}, u32[]{:S(2)}, u32[]{:S(2)}) collective-permute-start(f32[64,512]{1,0:T(8,128)} %get-tuple-element.71), channel_id=1, source_target_pairs={{4,0},{8,4},{12,8},{5,1},{9,5},{13,9},{6,2},{10,6},{14,10},{7,3},{... | collective-permute-start | bytes 393224 | tf_op jit(solution)/shard_map/grads/ppermute | solution.py:238
  131.0 17.6 %collective-permute-start.18 = (f32[64,512]{1,0:T(8,128)S(1)}, f32[64,512]{1,0:T(8,128)S(1)}, u32[]{:S(2)}, u32[]{:S(2)}) collective-permute-start(f32[64,512]{1,0:T(8,128)S(1)} %get-tuple-element.70), channel_id=1, source_target_pairs={{8,0},{12,4},{9,1},{13,5},{10,2},{14,6},{11,3},{15,7},{24,16},{28,... | collective-permute-start | bytes 393224 | tf_op jit(solution)/shard_map/grads/ppermute | solution.py:238
  135.2 13.5 %collective-permute-start.19 = (f32[64,512]{1,0:T(8,128)S(1)}, f32[64,512]{1,0:T(8,128)S(1)}, u32[]{:S(2)}, u32[]{:S(2)}) collective-permute-start(f32[64,512]{1,0:T(8,128)S(1)} %get-tuple-element.69), channel_id=1, source_target_pairs={{12,0},{13,1},{14,2},{15,3},{28,16},{29,17},{30,18},{31,19}} | collective-permute-start | bytes 393224 | tf_op jit(solution)/shard_map/grads/ppermute | solution.py:238
  140.3 2.9 %collective-permute-start.27 = (bf16[2,128,2048]{2,1,0:T(8,128)(2,1)}, bf16[2,128,2048]{2,1,0:T(8,128)(2,1)S(1)}, u32[]{:S(2)}, u32[]{:S(2)}) collective-permute-start(bf16[2,128,2048]{2,1,0:T(8,128)(2,1)} %collective-permute-done.20), channel_id=1, source_target_pairs={{0,1},{1,0},{2,3},{3,2},{4,5},{5,4},{6,7},{7,6},{8,9},{9,8},{10,11... | collective-permute-start | bytes 3145736 | tf_op jit(solution)/shard_map/peer_end_s/ppermute | solution.py:128
  (6 other events, 39.9 us)

commit v3 on v2

--- a/solution.py
+++ b/solution.py
@@ -176,8 +176,6 @@
     far_len = -(-(n_ctx - 1) * SUMMARY_TOKENS // HEAD_SIZE) * HEAD_SIZE
     far.append(jnp.zeros((far_len - (n_ctx - 1) * SUMMARY_TOKENS, 2 * kv_width), keys.dtype))
     far = jnp.concatenate(far, axis=0)
-    all_keys = jnp.concatenate([keys[0], far[:, :kv_width]], axis=0)
-    all_vals = jnp.concatenate([values[0], far[:, kv_width:]], axis=0)
     n_keys = seg_len + far_len
 
     wide = n_ctx != 4
@@ -187,11 +185,14 @@
         return lax.dynamic_slice(grad_out[0], (core * half, dp * part_rows), (half, part_rows))
 
     own = rows_of(me_head, me_dp)
+    (own_late,), (far,) = gate([own], far)
     peer, peer_other = [], []
     for s in range(1, n_dp):
         to = lax.rem(me_dp + s, n_dp)
         peer.append(turn(rows_of(me_head, to), "dp", s, "peer_in"))
 
+    all_keys = jnp.concatenate([keys[0], far[:, :kv_width]], axis=0)
+    all_vals = jnp.concatenate([values[0], far[:, kv_width:]], axis=0)
     count = jnp.stack([place - vis_start[0, 0], me_head]).reshape(1, 2).astype(jnp.int32)
     id_column = tok_ids[0].reshape(seg_len, 1)
     id_row = jnp.pad(tok_ids, ((0, 0), (0, far_len)), constant_values=-1)
@@ -214,6 +215,7 @@
         parts.append(jnp.dot(rows, out_weight, preferred_element_type=jnp.float32).astype(jnp.bfloat16))
     back = [turn(part, "dp", -s, "back") for s, part in zip(range(1, n_dp), parts)]
     own_rows = lax.dynamic_slice(grad_out[0], (0, me_dp * part_rows), (seg_len, part_rows))
+    (own_rows,), back = gate([own_rows], *back)
     d_mine = jnp.dot(own_rows, out_weight, preferred_element_type=jnp.float32)
     d_part = jnp.stack(back)
 
@@ -264,8 +266,8 @@
             return turn(x, "head", 1, name)
 
         own_1 = pairs(own, "own")
-        own_2 = two_away(own, "own")
-        own_mid = middle(own, "own")
+        own_2 = two_away(own_late, "own")
+        own_mid = middle(own_late, "own")
         attn_1 = pairs(turned, "attn")
         attn_x0 = [turn(turned, "dp", s, "attn_x0") for s in steps]
         token = mark(token, own_1, own_2, own_mid)
@@ -279,18 +281,20 @@
         attn_end_a = ends(attn_mid_a, "attn_a")
         attn_x1 = [turn(attn_1, "dp", s, "attn_x1") for s in steps]
         peer_pair = [jnp.stack([a, b]) for a, b in zip(peer, peer_1)]
-        peer_pair, (attn_mid_b, own_end, d_part) = gate(peer_pair, attn_mid_b, own_end, d_part)
+        peer_pair, (attn_mid_b, own_end, *rest) = gate(peer_pair, attn_mid_b, own_end, *parts, *attn_x0)
+        attn_x0 = rest[n_dp - 1 :]
         attn_end_b = ends(attn_mid_b, "attn_b")
         peer_mid = [middle(x, "peer") for x in peer_pair]
         attn_a = jnp.where(at_end, attn_end_a, attn_mid_a)
         attn_b = jnp.where(at_end, attn_end_b, attn_mid_b)
         attn_xa = [turn(attn_a, "dp", s, "attn_xa") for s in steps]
         attn_xb = [turn(attn_b, "dp", s, "attn_xb") for s in steps]
+        peer_1s = [swap(x, "peer_1s") for x in peer_1]
+        grad_q, grad_kv = backward(d_part)
+        (own_1, own_end), (grad_kv,) = gate([own_1, own_end], grad_kv)
         own_all = jnp.stack([own_1, own_2, jnp.where(at_end, own_end, own_mid)])
         own_all_s = swap(own_all, "own_s")
-        peer_1s = [swap(x, "peer_1s") for x in peer_1]
-        grad_q, grad_kv = backward(d_part)
-        peer_send, (own_all_s, grad_kv, *rest) = gate(peer_mid, own_all_s, grad_kv, *peer_1s, *attn_x1)
+        peer_send, (grad_kv, *rest) = gate(peer_mid, grad_kv, *peer_1s, *attn_x1)
         peer_1s, attn_x1 = rest[: n_dp - 1], rest[n_dp - 1 :]
         peer_end = [ends(x, "peer") for x in peer_send]
         peer_mid_s = [swap(x, "peer_mid_s") for x in peer_send]

time: 150 us -> 143 us (0.953)
  waiting for transfers between devices: 43.8 us -> 38.2 us
  starting transfers between devices: 48.7 us -> 46.4 us
    ppermute x4, waiting for transfers between devices: 26.5 us -> 14.1 us  [ends(): return lax.ppermute(x, 'ctx', [(1, 0), (2, 3)])]
    ppermute x3, waiting for transfers between devices: 3.59 us -> 9.03 us  [pairs(): return lax.ppermute(x, 'ctx', [(0, 1), (1, 0), (2, 3), (3, 2)])]
    ppermute x3, waiting for transfers between devices: 1.93 us -> 4.14 us  [send_home(): lax.ppermute(grad_kv[begin:begin + SUMMARY_TOKENS], 'ctx', line_pairs(n_c...]
    ppermute x11, starting transfers between devices: 8.27 us -> 6.43 us  [turn(): return lax.ppermute(x, axis, [(i, (i + step) % n) for i in range(n)])]
  transfers between devices with their start and end apart: 29 -> 29, of which waited for: 11 -> 9; matrix products, arithmetic and copies ran while one was open for 27% -> 29% of each run, Pallas kernels for 9% -> 9%
where the time goes in v3:
time: 143 us; the launch traced here: 142 us
  starting transfers between devices  46.4 us (32%)
  waiting for transfers between devices  38.2 us (27%)
  matrix products  25.4 us (18%)
  Pallas kernels  13 us (9%)
  other arithmetic  9.51 us (7%)
  local copies, waits for them, and re-layouts  7.52 us (5%)
  between operations  1.66 us (1%)
    dot_general x4, matrix products, dot(): lax.dot_general(a, b, (contract, ((), ())), preferred_element_type=jnp.fl...  19.9 us
    ppermute x4, waiting for transfers between devices, ends(): return lax.ppermute(x, 'ctx', [(1, 0), (2, 3)])  14.1 us
    ppermute x3, starting transfers between devices, pairs(): return lax.ppermute(x, 'ctx', [(0, 1), (1, 0), (2, 3), (3, 2)])  13.7 us
    ppermute x3, starting transfers between devices, shards(): lax.ppermute(tail, 'ctx', line_pairs(n_ctx, s))  10.7 us
    pallas_call x2, Pallas kernels, call_attention(): pl.pallas_call(kernel, out_shape=out_shape, in_specs=[pl.BlockSpec(memory...  10.4 us
    ppermute x3, waiting for transfers between devices, pairs(): return lax.ppermute(x, 'ctx', [(0, 1), (1, 0), (2, 3), (3, 2)])  9.03 us
    ppermute x1, waiting for transfers between devices, two_away(): return lax.ppermute(x, 'ctx', [(0, 2), (1, 3), (2, 0), (3, 1)])  7.79 us
    ppermute x11, starting transfers between devices, turn(): return lax.ppermute(x, axis, [(i, (i + step) % n) for i in range(n)])  6.43 us
  transfers between devices with their start and end apart: 29, of which 9 were waited for; matrix products, arithmetic and copies ran while one was open for 29% of the time, Pallas kernels for 9%

profile of v3, /device:TPU:0, one launch (start us, length us, event | category | flops | bytes accessed | tf_op | source)
XLA Modules:
  0.0 141.8 jit_solution(662237870616210077)
XLA Ops:
  1.5 4.9 %collective-permute-start = (bf16[64,512]{1,0:T(8,128)(2,1)S(1)}, bf16[64,512]{1,0:T(8,128)(2,1)S(1)}, u32[]{:S(2)}, u32[]{:S(2)}) collective-permute-start(bf16[64,512]{1,0:T(8,128)(2,1)S(1)} %pad_maximum_fusion.6), channel_id=1, source_target_pairs={{0,4},{4,8},{8,12},{1,5},{5,9},{9,13},{2,6},{6,10},{10,14},{3,7},{... | collective-permute-start | bytes 196616 | tf_op jit(solution)/shard_map/ppermute | solution.py:175
  6.4 4.5 %collective-permute-start.1 = (bf16[64,512]{1,0:T(8,128)(2,1)S(1)}, bf16[64,512]{1,0:T(8,128)(2,1)S(1)}, u32[]{:S(2)}, u32[]{:S(2)}) collective-permute-start(bf16[64,512]{1,0:T(8,128)(2,1)S(1)} %pad_maximum_fusion.6), channel_id=1, source_target_pairs={{0,8},{4,12},{1,9},{5,13},{2,10},{6,14},{3,11},{7,15},{16,24},{20,... | collective-permute-start | bytes 196616 | tf_op jit(solution)/shard_map/ppermute | solution.py:175
  10.9 1.3 collective-permute-start.2
  12.2 2.1 %dynamic-slice_bitcast_fusion.1 = (bf16[128,2048]{1,0:T(8,128)(2,1)S(1)}, bf16[128,2048]{1,0:T(8,128)(2,1)}) fusion(bf16[1,256,4096]{2,1,0:T(8,128)(2,1)} %param.13, s32[]{:T(128)S(6)} %select_n.61, s32[]{:T(128)S(6)} %select_n.63, s32[]{:T(128)S(6)} %select_n.62), kind=kLoop, calls=%fused_computation.45 | loop fusion | bytes 2097164 | tf_op jit(solution)/shard_map/dynamic_slice | solution.py:185
  14.3 1.5 %collective-permute-start.3 = (bf16[128,2048]{1,0:T(8,128)(2,1)S(1)}, bf16[128,2048]{1,0:T(8,128)(2,1)S(1)}, u32[]{:S(2)}, u32[]{:S(2)}) collective-permute-start(bf16[128,2048]{1,0:T(8,128)(2,1)S(1)} %get-tuple-element.77), channel_id=1, source_target_pairs={{0,2},{2,0},{1,3},{3,1},{4,6},{6,4},{5,7},{7,5},{8,10},{10,8},{9,1... | collective-permute-start | bytes 1572872 | tf_op jit(solution)/shard_map/peer_in/ppermute | solution.py:128
  16.8 1.5 %collective-permute-start.9 = (bf16[128,2048]{1,0:T(8,128)(2,1)}, bf16[128,2048]{1,0:T(8,128)(2,1)}, u32[]{:S(2)}, u32[]{:S(2)}) collective-permute-start(bf16[128,2048]{1,0:T(8,128)(2,1)} %get-tuple-element.46), channel_id=1, source_target_pairs={{4,8},{8,4},{5,9},{9,5},{6,10},{10,6},{7,11},{11,7},{20,24},{24,20... | collective-permute-start | bytes 1572872 | tf_op jit(solution)/shard_map/own_middle/ppermute | solution.py:142
  21.8 4.1 %shard_map.102 = (bf16[256,1024]{1,0:T(8,128)(2,1)S(1)}, bf16[256,1024]{1,0:T(8,128)(2,1)S(1)}) custom-call(s32[1,2]{1,0:T(1,128)S(1)} %add_bitcast_fusion.count_ref, s32[256,1]{1,0:T(8,128)S(1)} %copy.12.idc_ref, s32[1,512]{1,0:T(1,128)S(1)} %pad.4.idr_ref, bf16[256,1024]{1,0:T(8,128)(2,1)S(1)} %bitcast.48, bf16[512,256]{1,0:T(8,128)(2,1)S(1)} %pad_maximum_fusion.3.k_ref, ...), custom_call_target="tpu_custom_call" | custom-call | flops 536870912 | bytes 4194304 | tf_op jit(solution)/shard_map/pallas_call | solution.py:95
  25.9 3.9 %collective-permute-start.6 = (bf16[256,1024]{1,0:T(8,128)(2,1)S(1)}, bf16[256,1024]{1,0:T(8,128)(2,1)}, u32[]{:S(2)}, u32[]{:S(2)}) collective-permute-start(bf16[256,1024]{1,0:T(8,128)(2,1)S(1)} %get-tuple-element.61), channel_id=1, source_target_pairs={{0,4},{4,0},{8,12},{12,8},{1,5},{5,1},{9,13},{13,9},{2,6},{6,2},{1... | collective-permute-start | bytes 1572872 | tf_op jit(solution)/shard_map/attn_pairs/ppermute | solution.py:137
  30.4 6.0 %collective-permute-done.8.refs_1_ = bf16[128,2048]{1,0:T(8,128)(2,1)} collective-permute-done((bf16[128,2048]{1,0:T(8,128)(2,1)}, bf16[128,2048]{1,0:T(8,128)(2,1)}, u32[]{:S(2)}, u32[]{:S(2)}) %collective-permute-start.8) | collective-permute-done | bytes 524320 | tf_op jit(solution)/shard_map/own_pairs/ppermute | solution.py:137
  36.3 7.8 %collective-permute-done.7.refs_2_ = bf16[128,2048]{1,0:T(8,128)(2,1)} collective-permute-done((bf16[128,2048]{1,0:T(8,128)(2,1)}, bf16[128,2048]{1,0:T(8,128)(2,1)}, u32[]{:S(2)}, u32[]{:S(2)}) %collective-permute-start.7) | collective-permute-done | bytes 524320 | tf_op jit(solution)/shard_map/own_two/ppermute | solution.py:147
  46.0 9.8 %collective-permute-start.10 = (bf16[128,2048]{1,0:T(8,128)(2,1)S(1)}, bf16[128,2048]{1,0:T(8,128)(2,1)}, u32[]{:S(2)}, u32[]{:S(2)}) collective-permute-start(bf16[128,2048]{1,0:T(8,128)(2,1)S(1)} %collective-permute-done.3), channel_id=1, source_target_pairs={{0,4},{4,0},{8,12},{12,8},{1,5},{5,1},{9,13},{13,9},{2,6},{6,2},{1... | collective-permute-start | bytes 1572872 | tf_op jit(solution)/shard_map/peer_pairs/ppermute | solution.py:137
  57.1 1.5 %collective-permute-start.11 = (bf16[256,1024]{1,0:T(8,128)(2,1)}, bf16[256,1024]{1,0:T(8,128)(2,1)}, u32[]{:S(2)}, u32[]{:S(2)}) collective-permute-start(bf16[256,1024]{1,0:T(8,128)(2,1)} %collective-permute-done.6), channel_id=1, source_target_pairs={{4,8},{8,4},{5,9},{9,5},{6,10},{10,6},{7,11},{11,7},{20,24},{24,20... | collective-permute-start | bytes 1572872 | tf_op jit(solution)/shard_map/attn_b_middle/ppermute | solution.py:142
  59.9 1.5 %collective-permute-start.22 = (bf16[256,1024]{1,0:T(8,128)(2,1)S(1)}, bf16[256,1024]{1,0:T(8,128)(2,1)}, u32[]{:S(2)}, u32[]{:S(2)}) collective-permute-start(bf16[256,1024]{1,0:T(8,128)(2,1)S(1)} %get-tuple-element.61), channel_id=1, source_target_pairs={{4,8},{8,4},{5,9},{9,5},{6,10},{10,6},{7,11},{11,7},{20,24},{24,20... | collective-permute-start | bytes 1572872 | tf_op jit(solution)/shard_map/attn_a_middle/ppermute | solution.py:142
  61.4 4.3 %convolution_convert_fusion = bf16[256,1024]{1,0:T(8,128)(2,1)} fusion(bf16[2048,1024]{1,0:T(8,128)(2,1)} %param.12, bf16[128,2048]{1,0:T(8,128)(2,1)S(1)} %get-tuple-element.85, bf16[128,2048]{1,0:T(8,128)(2,1)S(1)} %get-tuple-element.84), kind=kOutput, calls=%fused_computation.23 | convolution fusion | flops 1076101120 | bytes 5767168 | tf_op jit(solution)/shard_map/dot_general | solution.py:215
  65.7 3.1 %collective-permute-done.10 = bf16[128,2048]{1,0:T(8,128)(2,1)} collective-permute-done((bf16[128,2048]{1,0:T(8,128)(2,1)S(1)}, bf16[128,2048]{1,0:T(8,128)(2,1)}, u32[]{:S(2)}, u32[]{:S(2)}) %collective-permute-start.10) | collective-permute-done | bytes 524320 | tf_op jit(solution)/shard_map/peer_pairs/ppermute | solution.py:137
  69.2 1.5 %dynamic-slice_bitcast_fusion = bf16[256,2048]{1,0:T(8,128)(2,1)S(1)} fusion(bf16[1,256,4096]{2,1,0:T(8,128)(2,1)} %param.13, s32[]{:T(128)S(6)} %select_n.62), kind=kLoop, calls=%fused_computation.31 | loop fusion | bytes 2097156 | tf_op jit(solution)/shard_map/dynamic_slice | solution.py:217
  72.0 1.6 %collective-permute-start.16 = (bf16[256,1024]{1,0:T(8,128)(2,1)}, bf16[256,1024]{1,0:T(8,128)(2,1)S(1)}, u32[]{:S(2)}, u32[]{:S(2)}) collective-permute-start(bf16[256,1024]{1,0:T(8,128)(2,1)} %collective-permute-done.6), channel_id=1, source_target_pairs={{0,2},{2,0},{1,3},{3,1},{4,6},{6,4},{5,7},{7,5},{8,10},{10,8},{9,1... | collective-permute-start | bytes 1572872 | tf_op jit(solution)/shard_map/attn_x1/ppermute | solution.py:128
  73.6 3.8 %collective-permute-done.12 = bf16[128,2048]{1,0:T(8,128)(2,1)} collective-permute-done((bf16[128,2048]{1,0:T(8,128)(2,1)}, bf16[128,2048]{1,0:T(8,128)(2,1)}, u32[]{:S(2)}, u32[]{:S(2)}) %collective-permute-start.12) | collective-permute-done | bytes 524320 | tf_op jit(solution)/shard_map/own_ends/ppermute | solution.py:152
  78.6 1.6 %collective-permute-start.14 = (bf16[2,128,2048]{2,1,0:T(8,128)(2,1)S(1)}, bf16[2,128,2048]{2,1,0:T(8,128)(2,1)}, u32[]{:S(2)}, u32[]{:S(2)}) collective-permute-start(bf16[2,128,2048]{2,1,0:T(8,128)(2,1)S(1)} %pad_maximum_fusion.2), channel_id=1, source_target_pairs={{4,8},{8,4},{5,9},{9,5},{6,10},{10,6},{7,11},{11,7},{20,24},{24,20... | collective-permute-start | bytes 3145736 | tf_op jit(solution)/shard_map/peer_middle/ppermute | solution.py:142
  80.3 3.0 %collective-permute-done.5 = bf16[256,1024]{1,0:T(8,128)(2,1)S(1)} collective-permute-done((bf16[256,1024]{1,0:T(8,128)(2,1)}, bf16[256,1024]{1,0:T(8,128)(2,1)S(1)}, u32[]{:S(2)}, u32[]{:S(2)}) %collective-permute-start.5) | collective-permute-done | bytes 524320 | tf_op jit(solution)/shard_map/back/ppermute | solution.py:128
  83.2 1.5 %collective-permute-start.23 = (bf16[256,1024]{1,0:T(8,128)(2,1)}, bf16[256,1024]{1,0:T(8,128)(2,1)S(1)}, u32[]{:S(2)}, u32[]{:S(2)}) collective-permute-start(bf16[256,1024]{1,0:T(8,128)(2,1)} %collective-permute-done.22), channel_id=1, source_target_pairs={{4,0},{8,12},{5,1},{9,13},{6,2},{10,14},{7,3},{11,15},{20,16},{24,... | collective-permute-start | bytes 1572872 | tf_op jit(solution)/shard_map/attn_a_ends/ppermute | solution.py:152
  86.0 6.3 %shard_map.105 = (bf16[256,1024]{1,0:T(8,128)(2,1)}, f32[512,512]{1,0:T(8,128)S(1)}) custom-call(s32[1,2]{1,0:T(1,128)S(1)} %add_bitcast_fusion.count_ref, s32[256,1]{1,0:T(8,128)S(1)} %copy.12.idc_ref, s32[1,512]{1,0:T(1,128)S(1)} %pad.4.idr_ref, bf16[256,1024]{1,0:T(8,128)(2,1)S(1)} %bitcast.49, bf16[512,256]{1,0:T(8,128)(2,1)S(1)} %pad_maximum_fusion.3.k_ref, ...), custom_call_target="tpu_custom_call" | custom-call | flops 1342177280 | bytes 4194304 | tf_op jit(solution)/shard_map/pallas_call | solution.py:95
  93.4 1.4 pad_maximum_fusion
  94.9 7.1 %collective-permute-done.23 = bf16[256,1024]{1,0:T(8,128)(2,1)S(1)} collective-permute-done((bf16[256,1024]{1,0:T(8,128)(2,1)}, bf16[256,1024]{1,0:T(8,128)(2,1)S(1)}, u32[]{:S(2)}, u32[]{:S(2)}) %collective-permute-start.23) | collective-permute-done | bytes 524320 | tf_op jit(solution)/shard_map/attn_a_ends/ppermute | solution.py:152
  104.2 1.6 %collective-permute-start.26 = (bf16[256,1024]{1,0:T(8,128)(2,1)S(1)}, bf16[256,1024]{1,0:T(8,128)(2,1)S(1)}, u32[]{:S(2)}, u32[]{:S(2)}) collective-permute-start(bf16[256,1024]{1,0:T(8,128)(2,1)S(1)} %get-tuple-element.76), channel_id=1, source_target_pairs={{0,2},{2,0},{1,3},{3,1},{4,6},{6,4},{5,7},{7,5},{8,10},{10,8},{9,1... | collective-permute-start | bytes 1572872 | tf_op jit(solution)/shard_map/attn_xb/ppermute | solution.py:128
  107.9 6.9 %fusion.14 = f32[2048,1024]{1,0:T(8,128)} fusion(bf16[128,2048]{1,0:T(8,128)(2,1)S(1)} %collective-permute-done.15, bf16[128,2048]{1,0:T(8,128)(2,1)} %collective-permute-done.10, bf16[128,2048]{1,0:T(8,128)(2,1)S(1)} %copy-done.3, bf16[128,2048]{1,0:T(8,128)(2,1)S(1)} %collective-permute-done.3, bf16[256,1024]{1,0:T(8,128)(2,1)S(1)} %collective-permute-done.16, ...), kind=kOutput, calls=%fused_computation.13 | convolution fusion | flops 2157969408 | bytes 11534336 | tf_op jit(solution)/shard_map/dot_general | solution.py:22
  114.8 1.5 %collective-permute-start.17 = (f32[64,512]{1,0:T(8,128)}, f32[64,512]{1,0:T(8,128)S(1)}, u32[]{:S(2)}, u32[]{:S(2)}) collective-permute-start(f32[64,512]{1,0:T(8,128)} %get-tuple-element.83), channel_id=1, source_target_pairs={{4,0},{8,4},{12,8},{5,1},{9,5},{13,9},{6,2},{10,6},{14,10},{7,3},{... | collective-permute-start | bytes 393224 | tf_op jit(solution)/shard_map/grads/ppermute | solution.py:240
  116.3 8.3 %fusion.6 = f32[2048,1024]{1,0:T(8,128)S(1)} fusion(f32[2048,1024]{1,0:T(8,128)} %fusion.14, bf16[384,2048]{1,0:T(8,128)(2,1)S(1)} %bitcast.60, bf16[384,2048]{1,0:T(8,128)(2,1)S(1)} %bitcast.54, bf16[256,2048]{1,0:T(8,128)(2,1)S(1)} %dynamic-slice_bitcast_fusion, bf16[384,1024]{1,0:T(8,128)(2,1)S(1)} %bitcast.56, bf16[384,1024]{1,0:T(8,128)(2,1)S(1)} %bitcast.55, ...), kind=kOutput, calls=%fused_computation.7 | convolution fusion | flops 4315938816 | bytes 23068672 | tf_op jit(solution)/shard_map/dot_general | solution.py:22
  127.2 3.3 %collective-permute-done.20 = bf16[2,128,2048]{2,1,0:T(8,128)(2,1)} collective-permute-done((bf16[2,128,2048]{2,1,0:T(8,128)(2,1)}, bf16[2,128,2048]{2,1,0:T(8,128)(2,1)}, u32[]{:S(2)}, u32[]{:S(2)}) %collective-permute-start.20) | collective-permute-done | bytes 1048608 | tf_op jit(solution)/shard_map/peer_ends/ppermute | solution.py:152
  130.5 1.3 broadcast_select_fusion.1
  133.4 3.4 %add_convert_fusion = bf16[2048,1024]{1,0:T(8,128)(2,1)} fusion(f32[2048,1024]{1,0:T(8,128)S(1)} %fusion.6, f32[2048,1024]{1,0:T(8,128)S(1)} %fusion.28, bf16[256,2048]{1,0:T(8,128)(2,1)S(1)} %bitcast.52, bf16[128,1024]{1,0:T(8,128)(2,1)S(1)} %get-tuple-element.88, bf16[128,1024]{1,0:T(8,128)(2,1)S(1)} %get-tuple-element.86), kind=kOutput, calls=%fused_computation | convolution fusion | flops 1081081856 | bytes 22544384 | tf_op jit(solution)/shard_map/dot_general | solution.py:22
  136.9 4.1 %collective-permute-done.18 = f32[64,512]{1,0:T(8,128)S(1)} collective-permute-done((f32[64,512]{1,0:T(8,128)S(1)}, f32[64,512]{1,0:T(8,128)S(1)}, u32[]{:S(2)}, u32[]{:S(2)}) %collective-permute-start.18) | collective-permute-done | bytes 131104 | tf_op jit(solution)/shard_map/grads/ppermute | solution.py:240
  (76 shorter events, 24.4 us)
Async XLA Ops:
  0.6 21.2 %copy-start = (bf16[1,256,1024]{2,1,0:T(8,128)(2,1)S(1)}, bf16[1,256,1024]{2,1,0:T(8,128)(2,1)}, u32[]{:S(2)}) copy-start(bf16[1,256,1024]{2,1,0:T(8,128)(2,1)} %param.7) | copy-start | bytes 1572868
  1.5 15.1 %collective-permute-start = (bf16[64,512]{1,0:T(8,128)(2,1)S(1)}, bf16[64,512]{1,0:T(8,128)(2,1)S(1)}, u32[]{:S(2)}, u32[]{:S(2)}) collective-permute-start(bf16[64,512]{1,0:T(8,128)(2,1)S(1)} %pad_maximum_fusion.6), channel_id=1, source_target_pairs={{0,4},{4,8},{8,12},{1,5},{5,9},{9,13},{2,6},{6,10},{10,14},{3,7},{... | collective-permute-start | bytes 196616 | tf_op jit(solution)/shard_map/ppermute | solution.py:175
  6.4 10.2 %collective-permute-start.1 = (bf16[64,512]{1,0:T(8,128)(2,1)S(1)}, bf16[64,512]{1,0:T(8,128)(2,1)S(1)}, u32[]{:S(2)}, u32[]{:S(2)}) collective-permute-start(bf16[64,512]{1,0:T(8,128)(2,1)S(1)} %pad_maximum_fusion.6), channel_id=1, source_target_pairs={{0,8},{4,12},{1,9},{5,13},{2,10},{6,14},{3,11},{7,15},{16,24},{20,... | collective-permute-start | bytes 196616 | tf_op jit(solution)/shard_map/ppermute | solution.py:175
  10.9 5.7 %collective-permute-start.2 = (bf16[64,512]{1,0:T(8,128)(2,1)S(1)}, bf16[64,512]{1,0:T(8,128)(2,1)S(1)}, u32[]{:S(2)}, u32[]{:S(2)}) collective-permute-start(bf16[64,512]{1,0:T(8,128)(2,1)S(1)} %pad_maximum_fusion.6), channel_id=1, source_target_pairs={{0,12},{1,13},{2,14},{3,15},{16,28},{17,29},{18,30},{19,31}} | collective-permute-start | bytes 196616 | tf_op jit(solution)/shard_map/ppermute | solution.py:175
  14.3 22.0 %collective-permute-start.8 = (bf16[128,2048]{1,0:T(8,128)(2,1)}, bf16[128,2048]{1,0:T(8,128)(2,1)}, u32[]{:S(2)}, u32[]{:S(2)}) collective-permute-start(bf16[128,2048]{1,0:T(8,128)(2,1)} %get-tuple-element.46), channel_id=1, source_target_pairs={{0,4},{4,0},{8,12},{12,8},{1,5},{5,1},{9,13},{13,9},{2,6},{6,2},{1... | collective-permute-start | bytes 1572872 | tf_op jit(solution)/shard_map/own_pairs/ppermute | solution.py:137
  14.3 15.5 %collective-permute-start.3 = (bf16[128,2048]{1,0:T(8,128)(2,1)S(1)}, bf16[128,2048]{1,0:T(8,128)(2,1)S(1)}, u32[]{:S(2)}, u32[]{:S(2)}) collective-permute-start(bf16[128,2048]{1,0:T(8,128)(2,1)S(1)} %get-tuple-element.77), channel_id=1, source_target_pairs={{0,2},{2,0},{1,3},{3,1},{4,6},{6,4},{5,7},{7,5},{8,10},{10,8},{9,1... | collective-permute-start | bytes 1572872 | tf_op jit(solution)/shard_map/peer_in/ppermute | solution.py:128
  16.7 27.4 %collective-permute-start.7 = (bf16[128,2048]{1,0:T(8,128)(2,1)}, bf16[128,2048]{1,0:T(8,128)(2,1)}, u32[]{:S(2)}, u32[]{:S(2)}) collective-permute-start(bf16[128,2048]{1,0:T(8,128)(2,1)} %get-tuple-element.46), channel_id=1, source_target_pairs={{0,8},{4,12},{8,0},{12,4},{1,9},{5,13},{9,1},{13,5},{2,10},{6,14},... | collective-permute-start | bytes 1572872 | tf_op jit(solution)/shard_map/own_two/ppermute | solution.py:147
  16.8 27.3 %collective-permute-start.9 = (bf16[128,2048]{1,0:T(8,128)(2,1)}, bf16[128,2048]{1,0:T(8,128)(2,1)}, u32[]{:S(2)}, u32[]{:S(2)}) collective-permute-start(bf16[128,2048]{1,0:T(8,128)(2,1)} %get-tuple-element.46), channel_id=1, source_target_pairs={{4,8},{8,4},{5,9},{9,5},{6,10},{10,6},{7,11},{11,7},{20,24},{24,20... | collective-permute-start | bytes 1572872 | tf_op jit(solution)/shard_map/own_middle/ppermute | solution.py:142
  25.9 31.2 %collective-permute-start.6 = (bf16[256,1024]{1,0:T(8,128)(2,1)S(1)}, bf16[256,1024]{1,0:T(8,128)(2,1)}, u32[]{:S(2)}, u32[]{:S(2)}) collective-permute-start(bf16[256,1024]{1,0:T(8,128)(2,1)S(1)} %get-tuple-element.61), channel_id=1, source_target_pairs={{0,4},{4,0},{8,12},{12,8},{1,5},{5,1},{9,13},{13,9},{2,6},{6,2},{1... | collective-permute-start | bytes 1572872 | tf_op jit(solution)/shard_map/attn_pairs/ppermute | solution.py:137
  29.8 42.1 %collective-permute-start.13 = (bf16[256,1024]{1,0:T(8,128)(2,1)S(1)}, bf16[256,1024]{1,0:T(8,128)(2,1)}, u32[]{:S(2)}, u32[]{:S(2)}) collective-permute-start(bf16[256,1024]{1,0:T(8,128)(2,1)S(1)} %get-tuple-element.61), channel_id=1, source_target_pairs={{0,2},{2,0},{1,3},{3,1},{4,6},{6,4},{5,7},{7,5},{8,10},{10,8},{9,1... | collective-permute-start | bytes 1572872 | tf_op jit(solution)/shard_map/attn_x0/ppermute | solution.py:128
  36.3 23.5 %collective-permute-start.4 = (bf16[128,2048]{1,0:T(8,128)(2,1)S(1)}, bf16[128,2048]{1,0:T(8,128)(2,1)S(1)}, u32[]{:S(2)}, u32[]{:S(2)}) collective-permute-start(bf16[128,2048]{1,0:T(8,128)(2,1)S(1)} %collective-permute-done.3), channel_id=1, source_target_pairs={{0,1},{1,0},{2,3},{3,2},{4,5},{5,4},{6,7},{7,6},{8,9},{9,8},{10,11... | collective-permute-start | bytes 1572872 | tf_op jit(solution)/shard_map/peer_s/ppermute | solution.py:128
  46.0 22.7 %collective-permute-start.10 = (bf16[128,2048]{1,0:T(8,128)(2,1)S(1)}, bf16[128,2048]{1,0:T(8,128)(2,1)}, u32[]{:S(2)}, u32[]{:S(2)}) collective-permute-start(bf16[128,2048]{1,0:T(8,128)(2,1)S(1)} %collective-permute-done.3), channel_id=1, source_target_pairs={{0,4},{4,0},{8,12},{12,8},{1,5},{5,1},{9,13},{13,9},{2,6},{6,2},{1... | collective-permute-start | bytes 1572872 | tf_op jit(solution)/shard_map/peer_pairs/ppermute | solution.py:137
  57.1 16.5 %collective-permute-start.11 = (bf16[256,1024]{1,0:T(8,128)(2,1)}, bf16[256,1024]{1,0:T(8,128)(2,1)}, u32[]{:S(2)}, u32[]{:S(2)}) collective-permute-start(bf16[256,1024]{1,0:T(8,128)(2,1)} %collective-permute-done.6), channel_id=1, source_target_pairs={{4,8},{8,4},{5,9},{9,5},{6,10},{10,6},{7,11},{11,7},{20,24},{24,20... | collective-permute-start | bytes 1572872 | tf_op jit(solution)/shard_map/attn_b_middle/ppermute | solution.py:142
  58.5 18.8 %collective-permute-start.12 = (bf16[128,2048]{1,0:T(8,128)(2,1)}, bf16[128,2048]{1,0:T(8,128)(2,1)}, u32[]{:S(2)}, u32[]{:S(2)}) collective-permute-start(bf16[128,2048]{1,0:T(8,128)(2,1)} %collective-permute-done.7.refs_2_), channel_id=1, source_target_pairs={{4,0},{8,12},{5,1},{9,13},{6,2},{10,14},{7,3},{11,15},{20,16},{24,... | collective-permute-start | bytes 1572872 | tf_op jit(solution)/shard_map/own_ends/ppermute | solution.py:152
  59.9 20.4 %collective-permute-start.22 = (bf16[256,1024]{1,0:T(8,128)(2,1)S(1)}, bf16[256,1024]{1,0:T(8,128)(2,1)}, u32[]{:S(2)}, u32[]{:S(2)}) collective-permute-start(bf16[256,1024]{1,0:T(8,128)(2,1)S(1)} %get-tuple-element.61), channel_id=1, source_target_pairs={{4,8},{8,4},{5,9},{9,5},{6,10},{10,6},{7,11},{11,7},{20,24},{24,20... | collective-permute-start | bytes 1572872 | tf_op jit(solution)/shard_map/attn_a_middle/ppermute | solution.py:142
  68.7 14.5 %collective-permute-start.5 = (bf16[256,1024]{1,0:T(8,128)(2,1)}, bf16[256,1024]{1,0:T(8,128)(2,1)S(1)}, u32[]{:S(2)}, u32[]{:S(2)}) collective-permute-start(bf16[256,1024]{1,0:T(8,128)(2,1)} %convolution_convert_fusion), channel_id=1, source_target_pairs={{0,2},{2,0},{1,3},{3,1},{4,6},{6,4},{5,7},{7,5},{8,10},{10,8},{9,1... | collective-permute-start | bytes 1572872 | tf_op jit(solution)/shard_map/back/ppermute | solution.py:128
  69.2 15.5 %copy-start.4 = (bf16[2048,1024]{1,0:T(8,128)(2,1)S(1)}, bf16[2048,1024]{1,0:T(8,128)(2,1)}, u32[]{:S(2)}) copy-start(bf16[2048,1024]{1,0:T(8,128)(2,1)} %param.12) | copy-start | bytes 12582916
  71.9 14.1 %copy-start.1 = (f32[8,128]{1,0:T(8,128)S(1)}, f32[8,128]{1,0:T(8,128)}, u32[]{:S(2)}) copy-start(f32[8,128]{1,0:T(8,128)} %shard_map.104.token_ref) | copy-start | bytes 12292
  72.0 32.2 %collective-permute-start.16 = (bf16[256,1024]{1,0:T(8,128)(2,1)}, bf16[256,1024]{1,0:T(8,128)(2,1)S(1)}, u32[]{:S(2)}, u32[]{:S(2)}) collective-permute-start(bf16[256,1024]{1,0:T(8,128)(2,1)} %collective-permute-done.6), channel_id=1, source_target_pairs={{0,2},{2,0},{1,3},{3,1},{4,6},{6,4},{5,7},{7,5},{8,10},{10,8},{9,1... | collective-permute-start | bytes 1572872 | tf_op jit(solution)/shard_map/attn_x1/ppermute | solution.py:128
  77.3 17.4 %collective-permute-start.24 = (bf16[256,1024]{1,0:T(8,128)(2,1)}, bf16[256,1024]{1,0:T(8,128)(2,1)S(1)}, u32[]{:S(2)}, u32[]{:S(2)}) collective-permute-start(bf16[256,1024]{1,0:T(8,128)(2,1)} %collective-permute-done.11), channel_id=1, source_target_pairs={{4,0},{8,12},{5,1},{9,13},{6,2},{10,14},{7,3},{11,15},{20,16},{24,... | collective-permute-start | bytes 1572872 | tf_op jit(solution)/shard_map/attn_b_ends/ppermute | solution.py:152
  78.6 27.2 %collective-permute-start.14 = (bf16[2,128,2048]{2,1,0:T(8,128)(2,1)S(1)}, bf16[2,128,2048]{2,1,0:T(8,128)(2,1)}, u32[]{:S(2)}, u32[]{:S(2)}) collective-permute-start(bf16[2,128,2048]{2,1,0:T(8,128)(2,1)S(1)} %pad_maximum_fusion.2), channel_id=1, source_target_pairs={{4,8},{8,4},{5,9},{9,5},{6,10},{10,6},{7,11},{11,7},{20,24},{24,20... | collective-permute-start | bytes 3145736 | tf_op jit(solution)/shard_map/peer_middle/ppermute | solution.py:142
  80.3 25.5 %collective-permute-start.15 = (bf16[128,2048]{1,0:T(8,128)(2,1)}, bf16[128,2048]{1,0:T(8,128)(2,1)S(1)}, u32[]{:S(2)}, u32[]{:S(2)}) collective-permute-start(bf16[128,2048]{1,0:T(8,128)(2,1)} %collective-permute-done.10), channel_id=1, source_target_pairs={{0,1},{1,0},{2,3},{3,2},{4,5},{5,4},{6,7},{7,6},{8,9},{9,8},{10,11... | collective-permute-start | bytes 1572872 | tf_op jit(solution)/shard_map/peer_1s/ppermute | solution.py:128
  83.2 18.7 %collective-permute-start.23 = (bf16[256,1024]{1,0:T(8,128)(2,1)}, bf16[256,1024]{1,0:T(8,128)(2,1)S(1)}, u32[]{:S(2)}, u32[]{:S(2)}) collective-permute-start(bf16[256,1024]{1,0:T(8,128)(2,1)} %collective-permute-done.22), channel_id=1, source_target_pairs={{4,0},{8,12},{5,1},{9,13},{6,2},{10,14},{7,3},{11,15},{20,16},{24,... | collective-permute-start | bytes 1572872 | tf_op jit(solution)/shard_map/attn_a_ends/ppermute | solution.py:152
  94.8 20.0 %collective-permute-start.21 = (bf16[3,128,2048]{2,1,0:T(8,128)(2,1)S(1)}, bf16[3,128,2048]{2,1,0:T(8,128)(2,1)S(1)}, u32[]{:S(2)}, u32[]{:S(2)}) collective-permute-start(bf16[3,128,2048]{2,1,0:T(8,128)(2,1)S(1)} %pad_maximum_fusion), channel_id=1, source_target_pairs={{0,1},{1,0},{2,3},{3,2},{4,5},{5,4},{6,7},{7,6},{8,9},{9,8},{10,11... | collective-permute-start | bytes 4718600 | tf_op jit(solution)/shard_map/own_s/ppermute | solution.py:128
  102.2 22.4 %collective-permute-start.25 = (bf16[256,1024]{1,0:T(8,128)(2,1)S(1)}, bf16[256,1024]{1,0:T(8,128)(2,1)S(1)}, u32[]{:S(2)}, u32[]{:S(2)}) collective-permute-start(bf16[256,1024]{1,0:T(8,128)(2,1)S(1)} %get-tuple-element.75), channel_id=1, source_target_pairs={{0,2},{2,0},{1,3},{3,1},{4,6},{6,4},{5,7},{7,5},{8,10},{10,8},{9,1... | collective-permute-start | bytes 1572872 | tf_op jit(solution)/shard_map/attn_xa/ppermute | solution.py:128
  104.2 21.7 %collective-permute-start.26 = (bf16[256,1024]{1,0:T(8,128)(2,1)S(1)}, bf16[256,1024]{1,0:T(8,128)(2,1)S(1)}, u32[]{:S(2)}, u32[]{:S(2)}) collective-permute-start(bf16[256,1024]{1,0:T(8,128)(2,1)S(1)} %get-tuple-element.76), channel_id=1, source_target_pairs={{0,2},{2,0},{1,3},{3,1},{4,6},{6,4},{5,7},{7,5},{8,10},{10,8},{9,1... | collective-permute-start | bytes 1572872 | tf_op jit(solution)/shard_map/attn_xb/ppermute | solution.py:128
  105.8 24.7 %collective-permute-start.20 = (bf16[2,128,2048]{2,1,0:T(8,128)(2,1)}, bf16[2,128,2048]{2,1,0:T(8,128)(2,1)}, u32[]{:S(2)}, u32[]{:S(2)}) collective-permute-start(bf16[2,128,2048]{2,1,0:T(8,128)(2,1)} %collective-permute-done.14), channel_id=1, source_target_pairs={{4,0},{8,12},{5,1},{9,13},{6,2},{10,14},{7,3},{11,15},{20,16},{24,... | collective-permute-start | bytes 3145736 | tf_op jit(solution)/shard_map/peer_ends/ppermute | solution.py:152
  107.1 26.1 %collective-permute-start.28 = (bf16[2,128,2048]{2,1,0:T(8,128)(2,1)}, bf16[2,128,2048]{2,1,0:T(8,128)(2,1)S(1)}, u32[]{:S(2)}, u32[]{:S(2)}) collective-permute-start(bf16[2,128,2048]{2,1,0:T(8,128)(2,1)} %collective-permute-done.14), channel_id=1, source_target_pairs={{0,1},{1,0},{2,3},{3,2},{4,5},{5,4},{6,7},{7,6},{8,9},{9,8},{10,11... | collective-permute-start | bytes 3145736 | tf_op jit(solution)/shard_map/peer_mid_s/ppermute | solution.py:128
  114.8 22.1 %collective-permute-start.17 = (f32[64,512]{1,0:T(8,128)}, f32[64,512]{1,0:T(8,128)S(1)}, u32[]{:S(2)}, u32[]{:S(2)}) collective-permute-start(f32[64,512]{1,0:T(8,128)} %get-tuple-element.83), channel_id=1, source_target_pairs={{4,0},{8,4},{12,8},{5,1},{9,5},{13,9},{6,2},{10,6},{14,10},{7,3},{... | collective-permute-start | bytes 393224 | tf_op jit(solution)/shard_map/grads/ppermute | solution.py:240
  124.6 16.4 %collective-permute-start.18 = (f32[64,512]{1,0:T(8,128)S(1)}, f32[64,512]{1,0:T(8,128)S(1)}, u32[]{:S(2)}, u32[]{:S(2)}) collective-permute-start(f32[64,512]{1,0:T(8,128)S(1)} %get-tuple-element.82), channel_id=1, source_target_pairs={{8,0},{12,4},{9,1},{13,5},{10,2},{14,6},{11,3},{15,7},{24,16},{28,... | collective-permute-start | bytes 393224 | tf_op jit(solution)/shard_map/grads/ppermute | solution.py:240
  125.9 15.1 %collective-permute-start.19 = (f32[64,512]{1,0:T(8,128)S(1)}, f32[64,512]{1,0:T(8,128)S(1)}, u32[]{:S(2)}, u32[]{:S(2)}) collective-permute-start(f32[64,512]{1,0:T(8,128)S(1)} %get-tuple-element.81), channel_id=1, source_target_pairs={{12,0},{13,1},{14,2},{15,3},{28,16},{29,17},{30,18},{31,19}} | collective-permute-start | bytes 393224 | tf_op jit(solution)/shard_map/grads/ppermute | solution.py:240
  130.5 2.9 %collective-permute-start.27 = (bf16[2,128,2048]{2,1,0:T(8,128)(2,1)}, bf16[2,128,2048]{2,1,0:T(8,128)(2,1)S(1)}, u32[]{:S(2)}, u32[]{:S(2)}) collective-permute-start(bf16[2,128,2048]{2,1,0:T(8,128)(2,1)} %collective-permute-done.20), channel_id=1, source_target_pairs={{0,1},{1,0},{2,3},{3,2},{4,5},{5,4},{6,7},{7,6},{8,9},{9,8},{10,11... | collective-permute-start | bytes 3145736 | tf_op jit(solution)/shard_map/peer_end_s/ppermute | solution.py:128
  (2 other events, 11.0 us)

commit v4 on v3

--- a/solution.py
+++ b/solution.py
@@ -236,12 +236,13 @@
         sent = []
         for s in range(1, n_ctx):
             begin = seg_len + (s - 1) * SUMMARY_TOKENS
+            part = grad_kv[begin : begin + SUMMARY_TOKENS].astype(jnp.bfloat16)
             with jax.named_scope("grads"):
-                sent.append(lax.ppermute(grad_kv[begin : begin + SUMMARY_TOKENS], "ctx", line_pairs(n_ctx, -s)))
+                sent.append(lax.ppermute(part, "ctx", line_pairs(n_ctx, -s)))
         return sent
 
     def add_home(grad_kv, sent):
-        home = sum(sent, grad_kv[cut:seg_len])
+        home = sum([x.astype(jnp.float32) for x in sent], grad_kv[cut:seg_len])
         return jnp.concatenate([grad_kv[:cut], home], 0).astype(jnp.bfloat16)
 
     if wide:

time: 143 us -> 138 us (0.965)
  waiting for transfers between devices: 38.2 us -> 34.1 us
    ppermute x3, waiting for transfers between devices: 4.14 us -> 0.32 us  [send_home(): sent.append(lax.ppermute(part, 'ctx', line_pairs(n_ctx, -s)))]
where the time goes in v4:
time: 138 us; the launch traced here: 137 us
  starting transfers between devices  46.5 us (34%)
  waiting for transfers between devices  34.1 us (25%)
  matrix products  25.6 us (19%)
  Pallas kernels  13 us (9%)
  other arithmetic  9.59 us (7%)
  local copies, waits for them, and re-layouts  6.86 us (5%)
  between operations  1.7 us (1%)
    dot_general x4, matrix products, dot(): lax.dot_general(a, b, (contract, ((), ())), preferred_element_type=jnp.fl...  20.1 us
    ppermute x4, waiting for transfers between devices, ends(): return lax.ppermute(x, 'ctx', [(1, 0), (2, 3)])  13.8 us
    ppermute x3, starting transfers between devices, pairs(): return lax.ppermute(x, 'ctx', [(0, 1), (1, 0), (2, 3), (3, 2)])  13.7 us
    ppermute x3, starting transfers between devices, shards(): lax.ppermute(tail, 'ctx', line_pairs(n_ctx, s))  10.7 us
    pallas_call x2, Pallas kernels, call_attention(): pl.pallas_call(kernel, out_shape=out_shape, in_specs=[pl.BlockSpec(memory...  10.4 us
    ppermute x3, waiting for transfers between devices, pairs(): return lax.ppermute(x, 'ctx', [(0, 1), (1, 0), (2, 3), (3, 2)])  8.99 us
    ppermute x1, waiting for transfers between devices, two_away(): return lax.ppermute(x, 'ctx', [(0, 2), (1, 3), (2, 0), (3, 1)])  7.79 us
    ppermute x11, starting transfers between devices, turn(): return lax.ppermute(x, axis, [(i, (i + step) % n) for i in range(n)])  6.43 us
  transfers between devices with their start and end apart: 29, of which 9 were waited for; matrix products, arithmetic and copies ran while one was open for 29% of the time, Pallas kernels for 9%

profile of v4, /device:TPU:0, one launch (start us, length us, event | category | flops | bytes accessed | tf_op | source)
XLA Modules:
  0.0 137.3 jit_solution(3799176667977288140)
XLA Ops:
  1.5 4.9 %collective-permute-start = (bf16[64,512]{1,0:T(8,128)(2,1)S(1)}, bf16[64,512]{1,0:T(8,128)(2,1)S(1)}, u32[]{:S(2)}, u32[]{:S(2)}) collective-permute-start(bf16[64,512]{1,0:T(8,128)(2,1)S(1)} %pad_maximum_fusion.6), channel_id=1, source_target_pairs={{0,4},{4,8},{8,12},{1,5},{5,9},{9,13},{2,6},{6,10},{10,14},{3,7},{... | collective-permute-start | bytes 196616 | tf_op jit(solution)/shard_map/ppermute | solution.py:175
  6.4 4.5 %collective-permute-start.1 = (bf16[64,512]{1,0:T(8,128)(2,1)S(1)}, bf16[64,512]{1,0:T(8,128)(2,1)S(1)}, u32[]{:S(2)}, u32[]{:S(2)}) collective-permute-start(bf16[64,512]{1,0:T(8,128)(2,1)S(1)} %pad_maximum_fusion.6), channel_id=1, source_target_pairs={{0,8},{4,12},{1,9},{5,13},{2,10},{6,14},{3,11},{7,15},{16,24},{20,... | collective-permute-start | bytes 196616 | tf_op jit(solution)/shard_map/ppermute | solution.py:175
  10.9 1.3 collective-permute-start.2
  12.2 2.1 %dynamic-slice_bitcast_fusion.1 = (bf16[128,2048]{1,0:T(8,128)(2,1)S(1)}, bf16[128,2048]{1,0:T(8,128)(2,1)}) fusion(bf16[1,256,4096]{2,1,0:T(8,128)(2,1)} %param.13, s32[]{:T(128)S(6)} %select_n.61, s32[]{:T(128)S(6)} %select_n.63, s32[]{:T(128)S(6)} %select_n.62), kind=kLoop, calls=%fused_computation.45 | loop fusion | bytes 2097164 | tf_op jit(solution)/shard_map/dynamic_slice | solution.py:185
  14.3 1.5 %collective-permute-start.3 = (bf16[128,2048]{1,0:T(8,128)(2,1)S(1)}, bf16[128,2048]{1,0:T(8,128)(2,1)S(1)}, u32[]{:S(2)}, u32[]{:S(2)}) collective-permute-start(bf16[128,2048]{1,0:T(8,128)(2,1)S(1)} %get-tuple-element.77), channel_id=1, source_target_pairs={{0,2},{2,0},{1,3},{3,1},{4,6},{6,4},{5,7},{7,5},{8,10},{10,8},{9,1... | collective-permute-start | bytes 1572872 | tf_op jit(solution)/shard_map/peer_in/ppermute | solution.py:128
  16.8 1.5 %collective-permute-start.9 = (bf16[128,2048]{1,0:T(8,128)(2,1)}, bf16[128,2048]{1,0:T(8,128)(2,1)}, u32[]{:S(2)}, u32[]{:S(2)}) collective-permute-start(bf16[128,2048]{1,0:T(8,128)(2,1)} %get-tuple-element.46), channel_id=1, source_target_pairs={{4,8},{8,4},{5,9},{9,5},{6,10},{10,6},{7,11},{11,7},{20,24},{24,20... | collective-permute-start | bytes 1572872 | tf_op jit(solution)/shard_map/own_middle/ppermute | solution.py:142
  21.8 4.1 %shard_map.102 = (bf16[256,1024]{1,0:T(8,128)(2,1)S(1)}, bf16[256,1024]{1,0:T(8,128)(2,1)S(1)}) custom-call(s32[1,2]{1,0:T(1,128)S(1)} %add_bitcast_fusion.count_ref, s32[256,1]{1,0:T(8,128)S(1)} %copy.12.idc_ref, s32[1,512]{1,0:T(1,128)S(1)} %pad.4.idr_ref, bf16[256,1024]{1,0:T(8,128)(2,1)S(1)} %bitcast.48, bf16[512,256]{1,0:T(8,128)(2,1)S(1)} %pad_maximum_fusion.3.k_ref, ...), custom_call_target="tpu_custom_call" | custom-call | flops 536870912 | bytes 4194304 | tf_op jit(solution)/shard_map/pallas_call | solution.py:95
  25.9 3.9 %collective-permute-start.6 = (bf16[256,1024]{1,0:T(8,128)(2,1)S(1)}, bf16[256,1024]{1,0:T(8,128)(2,1)}, u32[]{:S(2)}, u32[]{:S(2)}) collective-permute-start(bf16[256,1024]{1,0:T(8,128)(2,1)S(1)} %get-tuple-element.61), channel_id=1, source_target_pairs={{0,4},{4,0},{8,12},{12,8},{1,5},{5,1},{9,13},{13,9},{2,6},{6,2},{1... | collective-permute-start | bytes 1572872 | tf_op jit(solution)/shard_map/attn_pairs/ppermute | solution.py:137
  30.4 6.0 %collective-permute-done.8.refs_1_ = bf16[128,2048]{1,0:T(8,128)(2,1)} collective-permute-done((bf16[128,2048]{1,0:T(8,128)(2,1)}, bf16[128,2048]{1,0:T(8,128)(2,1)}, u32[]{:S(2)}, u32[]{:S(2)}) %collective-permute-start.8) | collective-permute-done | bytes 524320 | tf_op jit(solution)/shard_map/own_pairs/ppermute | solution.py:137
  36.3 7.8 %collective-permute-done.7.refs_2_ = bf16[128,2048]{1,0:T(8,128)(2,1)} collective-permute-done((bf16[128,2048]{1,0:T(8,128)(2,1)}, bf16[128,2048]{1,0:T(8,128)(2,1)}, u32[]{:S(2)}, u32[]{:S(2)}) %collective-permute-start.7) | collective-permute-done | bytes 524320 | tf_op jit(solution)/shard_map/own_two/ppermute | solution.py:147
  46.0 9.8 %collective-permute-start.10 = (bf16[128,2048]{1,0:T(8,128)(2,1)S(1)}, bf16[128,2048]{1,0:T(8,128)(2,1)}, u32[]{:S(2)}, u32[]{:S(2)}) collective-permute-start(bf16[128,2048]{1,0:T(8,128)(2,1)S(1)} %collective-permute-done.3), channel_id=1, source_target_pairs={{0,4},{4,0},{8,12},{12,8},{1,5},{5,1},{9,13},{13,9},{2,6},{6,2},{1... | collective-permute-start | bytes 1572872 | tf_op jit(solution)/shard_map/peer_pairs/ppermute | solution.py:137
  57.1 1.5 %collective-permute-start.11 = (bf16[256,1024]{1,0:T(8,128)(2,1)}, bf16[256,1024]{1,0:T(8,128)(2,1)}, u32[]{:S(2)}, u32[]{:S(2)}) collective-permute-start(bf16[256,1024]{1,0:T(8,128)(2,1)} %collective-permute-done.6), channel_id=1, source_target_pairs={{4,8},{8,4},{5,9},{9,5},{6,10},{10,6},{7,11},{11,7},{20,24},{24,20... | collective-permute-start | bytes 1572872 | tf_op jit(solution)/shard_map/attn_b_middle/ppermute | solution.py:142
  59.9 1.5 %collective-permute-start.22 = (bf16[256,1024]{1,0:T(8,128)(2,1)S(1)}, bf16[256,1024]{1,0:T(8,128)(2,1)}, u32[]{:S(2)}, u32[]{:S(2)}) collective-permute-start(bf16[256,1024]{1,0:T(8,128)(2,1)S(1)} %get-tuple-element.61), channel_id=1, source_target_pairs={{4,8},{8,4},{5,9},{9,5},{6,10},{10,6},{7,11},{11,7},{20,24},{24,20... | collective-permute-start | bytes 1572872 | tf_op jit(solution)/shard_map/attn_a_middle/ppermute | solution.py:142
  61.4 4.3 %convolution_convert_fusion = bf16[256,1024]{1,0:T(8,128)(2,1)} fusion(bf16[2048,1024]{1,0:T(8,128)(2,1)} %param.12, bf16[128,2048]{1,0:T(8,128)(2,1)S(1)} %get-tuple-element.82, bf16[128,2048]{1,0:T(8,128)(2,1)S(1)} %get-tuple-element.81), kind=kOutput, calls=%fused_computation.23 | convolution fusion | flops 1076101120 | bytes 5767168 | tf_op jit(solution)/shard_map/dot_general | solution.py:215
  65.7 3.0 %collective-permute-done.10 = bf16[128,2048]{1,0:T(8,128)(2,1)} collective-permute-done((bf16[128,2048]{1,0:T(8,128)(2,1)S(1)}, bf16[128,2048]{1,0:T(8,128)(2,1)}, u32[]{:S(2)}, u32[]{:S(2)}) %collective-permute-start.10) | collective-permute-done | bytes 524320 | tf_op jit(solution)/shard_map/peer_pairs/ppermute | solution.py:137
  69.2 1.5 %dynamic-slice_bitcast_fusion = bf16[256,2048]{1,0:T(8,128)(2,1)S(1)} fusion(bf16[1,256,4096]{2,1,0:T(8,128)(2,1)} %param.13, s32[]{:T(128)S(6)} %select_n.62), kind=kLoop, calls=%fused_computation.31 | loop fusion | bytes 2097156 | tf_op jit(solution)/shard_map/dynamic_slice | solution.py:217
  72.0 1.6 %collective-permute-start.16 = (bf16[256,1024]{1,0:T(8,128)(2,1)}, bf16[256,1024]{1,0:T(8,128)(2,1)S(1)}, u32[]{:S(2)}, u32[]{:S(2)}) collective-permute-start(bf16[256,1024]{1,0:T(8,128)(2,1)} %collective-permute-done.6), channel_id=1, source_target_pairs={{0,2},{2,0},{1,3},{3,1},{4,6},{6,4},{5,7},{7,5},{8,10},{10,8},{9,1... | collective-permute-start | bytes 1572872 | tf_op jit(solution)/shard_map/attn_x1/ppermute | solution.py:128
  73.6 3.8 %collective-permute-done.12 = bf16[128,2048]{1,0:T(8,128)(2,1)} collective-permute-done((bf16[128,2048]{1,0:T(8,128)(2,1)}, bf16[128,2048]{1,0:T(8,128)(2,1)}, u32[]{:S(2)}, u32[]{:S(2)}) %collective-permute-start.12) | collective-permute-done | bytes 524320 | tf_op jit(solution)/shard_map/own_ends/ppermute | solution.py:152
  78.6 1.6 %collective-permute-start.14 = (bf16[2,128,2048]{2,1,0:T(8,128)(2,1)S(1)}, bf16[2,128,2048]{2,1,0:T(8,128)(2,1)}, u32[]{:S(2)}, u32[]{:S(2)}) collective-permute-start(bf16[2,128,2048]{2,1,0:T(8,128)(2,1)S(1)} %pad_maximum_fusion.2), channel_id=1, source_target_pairs={{4,8},{8,4},{5,9},{9,5},{6,10},{10,6},{7,11},{11,7},{20,24},{24,20... | collective-permute-start | bytes 3145736 | tf_op jit(solution)/shard_map/peer_middle/ppermute | solution.py:142
  80.3 3.0 %collective-permute-done.5 = bf16[256,1024]{1,0:T(8,128)(2,1)S(1)} collective-permute-done((bf16[256,1024]{1,0:T(8,128)(2,1)}, bf16[256,1024]{1,0:T(8,128)(2,1)S(1)}, u32[]{:S(2)}, u32[]{:S(2)}) %collective-permute-start.5) | collective-permute-done | bytes 524320 | tf_op jit(solution)/shard_map/back/ppermute | solution.py:128
  83.2 1.5 %collective-permute-start.23 = (bf16[256,1024]{1,0:T(8,128)(2,1)}, bf16[256,1024]{1,0:T(8,128)(2,1)S(1)}, u32[]{:S(2)}, u32[]{:S(2)}) collective-permute-start(bf16[256,1024]{1,0:T(8,128)(2,1)} %collective-permute-done.22), channel_id=1, source_target_pairs={{4,0},{8,12},{5,1},{9,13},{6,2},{10,14},{7,3},{11,15},{20,16},{24,... | collective-permute-start | bytes 1572872 | tf_op jit(solution)/shard_map/attn_a_ends/ppermute | solution.py:152
  86.0 6.3 %shard_map.105 = (bf16[256,1024]{1,0:T(8,128)(2,1)}, f32[512,512]{1,0:T(8,128)S(1)}) custom-call(s32[1,2]{1,0:T(1,128)S(1)} %add_bitcast_fusion.count_ref, s32[256,1]{1,0:T(8,128)S(1)} %copy.12.idc_ref, s32[1,512]{1,0:T(1,128)S(1)} %pad.4.idr_ref, bf16[256,1024]{1,0:T(8,128)(2,1)S(1)} %bitcast.49, bf16[512,256]{1,0:T(8,128)(2,1)S(1)} %pad_maximum_fusion.3.k_ref, ...), custom_call_target="tpu_custom_call" | custom-call | flops 1342177280 | bytes 4194304 | tf_op jit(solution)/shard_map/pallas_call | solution.py:95
  93.4 1.4 %pad_maximum_fusion = bf16[3,128,2048]{2,1,0:T(8,128)(2,1)S(1)} fusion(bf16[1,128,2048]{2,1,0:T(8,128)(2,1)S(1)} %select_bitcast_fusion.2, bf16[1,128,2048]{2,1,0:T(8,128)(2,1)} %bitcast.18, bf16[1,128,2048]{2,1,0:T(8,128)(2,1)} %bitcast.17), kind=kLoop, calls=%fused_computation.21 | loop fusion | flops 1572864 | bytes 3145728 | tf_op jit(solution)/shard_map/stack | solution.py:296
  94.9 7.1 %collective-permute-done.23 = bf16[256,1024]{1,0:T(8,128)(2,1)S(1)} collective-permute-done((bf16[256,1024]{1,0:T(8,128)(2,1)}, bf16[256,1024]{1,0:T(8,128)(2,1)S(1)}, u32[]{:S(2)}, u32[]{:S(2)}) %collective-permute-start.23) | collective-permute-done | bytes 524320 | tf_op jit(solution)/shard_map/attn_a_ends/ppermute | solution.py:152
  104.2 1.6 %collective-permute-start.26 = (bf16[256,1024]{1,0:T(8,128)(2,1)S(1)}, bf16[256,1024]{1,0:T(8,128)(2,1)S(1)}, u32[]{:S(2)}, u32[]{:S(2)}) collective-permute-start(bf16[256,1024]{1,0:T(8,128)(2,1)S(1)} %get-tuple-element.76), channel_id=1, source_target_pairs={{0,2},{2,0},{1,3},{3,1},{4,6},{6,4},{5,7},{7,5},{8,10},{10,8},{9,1... | collective-permute-start | bytes 1572872 | tf_op jit(solution)/shard_map/attn_xb/ppermute | solution.py:128
  107.3 7.1 %fusion.14 = f32[2048,1024]{1,0:T(8,128)} fusion(bf16[128,2048]{1,0:T(8,128)(2,1)S(1)} %collective-permute-done.15, bf16[128,2048]{1,0:T(8,128)(2,1)} %collective-permute-done.10, bf16[128,2048]{1,0:T(8,128)(2,1)S(1)} %copy-done.4, bf16[128,2048]{1,0:T(8,128)(2,1)S(1)} %collective-permute-done.3, bf16[256,1024]{1,0:T(8,128)(2,1)S(1)} %collective-permute-done.16, ...), kind=kOutput, calls=%fused_computation.13 | convolution fusion | flops 2157969408 | bytes 11534336 | tf_op jit(solution)/shard_map/dot_general | solution.py:22
  114.4 1.5 %collective-permute-start.17 = (bf16[64,512]{1,0:T(8,128)(2,1)S(1)}, bf16[64,512]{1,0:T(8,128)(2,1)S(1)}, u32[]{:S(2)}, u32[]{:S(2)}) collective-permute-start(bf16[64,512]{1,0:T(8,128)(2,1)S(1)} %get-tuple-element.89), channel_id=1, source_target_pairs={{4,0},{8,4},{12,8},{5,1},{9,5},{13,9},{6,2},{10,6},{14,10},{7,3},{... | collective-permute-start | bytes 196616 | tf_op jit(solution)/shard_map/grads/ppermute | solution.py:241
  115.9 8.3 %fusion.6 = f32[2048,1024]{1,0:T(8,128)S(1)} fusion(f32[2048,1024]{1,0:T(8,128)} %fusion.14, bf16[384,2048]{1,0:T(8,128)(2,1)S(1)} %bitcast.60, bf16[384,2048]{1,0:T(8,128)(2,1)S(1)} %bitcast.54, bf16[256,2048]{1,0:T(8,128)(2,1)S(1)} %dynamic-slice_bitcast_fusion, bf16[384,1024]{1,0:T(8,128)(2,1)S(1)} %bitcast.56, bf16[384,1024]{1,0:T(8,128)(2,1)S(1)} %bitcast.55, ...), kind=kOutput, calls=%fused_computation.7 | convolution fusion | flops 4315938816 | bytes 23068672 | tf_op jit(solution)/shard_map/dot_general | solution.py:22
  124.2 1.3 collective-permute-start.18
  126.8 3.0 %collective-permute-done.20 = bf16[2,128,2048]{2,1,0:T(8,128)(2,1)} collective-permute-done((bf16[2,128,2048]{2,1,0:T(8,128)(2,1)}, bf16[2,128,2048]{2,1,0:T(8,128)(2,1)}, u32[]{:S(2)}, u32[]{:S(2)}) %collective-permute-start.20) | collective-permute-done | bytes 1048608 | tf_op jit(solution)/shard_map/peer_ends/ppermute | solution.py:152
  129.8 1.3 broadcast_select_fusion.1
  132.8 3.4 %add_convert_fusion = bf16[2048,1024]{1,0:T(8,128)(2,1)} fusion(f32[2048,1024]{1,0:T(8,128)S(1)} %fusion.6, f32[2048,1024]{1,0:T(8,128)S(1)} %fusion.28, bf16[256,2048]{1,0:T(8,128)(2,1)S(1)} %bitcast.52, bf16[128,1024]{1,0:T(8,128)(2,1)S(1)} %get-tuple-element.85, bf16[128,1024]{1,0:T(8,128)(2,1)S(1)} %get-tuple-element.83), kind=kOutput, calls=%fused_computation | convolution fusion | flops 1081081856 | bytes 22544384 | tf_op jit(solution)/shard_map/dot_general | solution.py:22
  (80 shorter events, 22.8 us)
Async XLA Ops:
  0.6 21.1 %copy-start = (bf16[1,256,1024]{2,1,0:T(8,128)(2,1)S(1)}, bf16[1,256,1024]{2,1,0:T(8,128)(2,1)}, u32[]{:S(2)}) copy-start(bf16[1,256,1024]{2,1,0:T(8,128)(2,1)} %param.7) | copy-start | bytes 1572868
  1.5 15.1 %collective-permute-start = (bf16[64,512]{1,0:T(8,128)(2,1)S(1)}, bf16[64,512]{1,0:T(8,128)(2,1)S(1)}, u32[]{:S(2)}, u32[]{:S(2)}) collective-permute-start(bf16[64,512]{1,0:T(8,128)(2,1)S(1)} %pad_maximum_fusion.6), channel_id=1, source_target_pairs={{0,4},{4,8},{8,12},{1,5},{5,9},{9,13},{2,6},{6,10},{10,14},{3,7},{... | collective-permute-start | bytes 196616 | tf_op jit(solution)/shard_map/ppermute | solution.py:175
  6.4 10.2 %collective-permute-start.1 = (bf16[64,512]{1,0:T(8,128)(2,1)S(1)}, bf16[64,512]{1,0:T(8,128)(2,1)S(1)}, u32[]{:S(2)}, u32[]{:S(2)}) collective-permute-start(bf16[64,512]{1,0:T(8,128)(2,1)S(1)} %pad_maximum_fusion.6), channel_id=1, source_target_pairs={{0,8},{4,12},{1,9},{5,13},{2,10},{6,14},{3,11},{7,15},{16,24},{20,... | collective-permute-start | bytes 196616 | tf_op jit(solution)/shard_map/ppermute | solution.py:175
  10.9 5.7 %collective-permute-start.2 = (bf16[64,512]{1,0:T(8,128)(2,1)S(1)}, bf16[64,512]{1,0:T(8,128)(2,1)S(1)}, u32[]{:S(2)}, u32[]{:S(2)}) collective-permute-start(bf16[64,512]{1,0:T(8,128)(2,1)S(1)} %pad_maximum_fusion.6), channel_id=1, source_target_pairs={{0,12},{1,13},{2,14},{3,15},{16,28},{17,29},{18,30},{19,31}} | collective-permute-start | bytes 196616 | tf_op jit(solution)/shard_map/ppermute | solution.py:175
  14.3 22.0 %collective-permute-start.8 = (bf16[128,2048]{1,0:T(8,128)(2,1)}, bf16[128,2048]{1,0:T(8,128)(2,1)}, u32[]{:S(2)}, u32[]{:S(2)}) collective-permute-start(bf16[128,2048]{1,0:T(8,128)(2,1)} %get-tuple-element.46), channel_id=1, source_target_pairs={{0,4},{4,0},{8,12},{12,8},{1,5},{5,1},{9,13},{13,9},{2,6},{6,2},{1... | collective-permute-start | bytes 1572872 | tf_op jit(solution)/shard_map/own_pairs/ppermute | solution.py:137
  14.3 15.5 %collective-permute-start.3 = (bf16[128,2048]{1,0:T(8,128)(2,1)S(1)}, bf16[128,2048]{1,0:T(8,128)(2,1)S(1)}, u32[]{:S(2)}, u32[]{:S(2)}) collective-permute-start(bf16[128,2048]{1,0:T(8,128)(2,1)S(1)} %get-tuple-element.77), channel_id=1, source_target_pairs={{0,2},{2,0},{1,3},{3,1},{4,6},{6,4},{5,7},{7,5},{8,10},{10,8},{9,1... | collective-permute-start | bytes 1572872 | tf_op jit(solution)/shard_map/peer_in/ppermute | solution.py:128
  16.7 27.4 %collective-permute-start.7 = (bf16[128,2048]{1,0:T(8,128)(2,1)}, bf16[128,2048]{1,0:T(8,128)(2,1)}, u32[]{:S(2)}, u32[]{:S(2)}) collective-permute-start(bf16[128,2048]{1,0:T(8,128)(2,1)} %get-tuple-element.46), channel_id=1, source_target_pairs={{0,8},{4,12},{8,0},{12,4},{1,9},{5,13},{9,1},{13,5},{2,10},{6,14},... | collective-permute-start | bytes 1572872 | tf_op jit(solution)/shard_map/own_two/ppermute | solution.py:147
  16.8 27.3 %collective-permute-start.9 = (bf16[128,2048]{1,0:T(8,128)(2,1)}, bf16[128,2048]{1,0:T(8,128)(2,1)}, u32[]{:S(2)}, u32[]{:S(2)}) collective-permute-start(bf16[128,2048]{1,0:T(8,128)(2,1)} %get-tuple-element.46), channel_id=1, source_target_pairs={{4,8},{8,4},{5,9},{9,5},{6,10},{10,6},{7,11},{11,7},{20,24},{24,20... | collective-permute-start | bytes 1572872 | tf_op jit(solution)/shard_map/own_middle/ppermute | solution.py:142
  25.9 31.2 %collective-permute-start.6 = (bf16[256,1024]{1,0:T(8,128)(2,1)S(1)}, bf16[256,1024]{1,0:T(8,128)(2,1)}, u32[]{:S(2)}, u32[]{:S(2)}) collective-permute-start(bf16[256,1024]{1,0:T(8,128)(2,1)S(1)} %get-tuple-element.61), channel_id=1, source_target_pairs={{0,4},{4,0},{8,12},{12,8},{1,5},{5,1},{9,13},{13,9},{2,6},{6,2},{1... | collective-permute-start | bytes 1572872 | tf_op jit(solution)/shard_map/attn_pairs/ppermute | solution.py:137
  29.8 42.1 %collective-permute-start.13 = (bf16[256,1024]{1,0:T(8,128)(2,1)S(1)}, bf16[256,1024]{1,0:T(8,128)(2,1)}, u32[]{:S(2)}, u32[]{:S(2)}) collective-permute-start(bf16[256,1024]{1,0:T(8,128)(2,1)S(1)} %get-tuple-element.61), channel_id=1, source_target_pairs={{0,2},{2,0},{1,3},{3,1},{4,6},{6,4},{5,7},{7,5},{8,10},{10,8},{9,1... | collective-permute-start | bytes 1572872 | tf_op jit(solution)/shard_map/attn_x0/ppermute | solution.py:128
  36.3 23.5 %collective-permute-start.4 = (bf16[128,2048]{1,0:T(8,128)(2,1)S(1)}, bf16[128,2048]{1,0:T(8,128)(2,1)S(1)}, u32[]{:S(2)}, u32[]{:S(2)}) collective-permute-start(bf16[128,2048]{1,0:T(8,128)(2,1)S(1)} %collective-permute-done.3), channel_id=1, source_target_pairs={{0,1},{1,0},{2,3},{3,2},{4,5},{5,4},{6,7},{7,6},{8,9},{9,8},{10,11... | collective-permute-start | bytes 1572872 | tf_op jit(solution)/shard_map/peer_s/ppermute | solution.py:128
  46.0 22.7 %collective-permute-start.10 = (bf16[128,2048]{1,0:T(8,128)(2,1)S(1)}, bf16[128,2048]{1,0:T(8,128)(2,1)}, u32[]{:S(2)}, u32[]{:S(2)}) collective-permute-start(bf16[128,2048]{1,0:T(8,128)(2,1)S(1)} %collective-permute-done.3), channel_id=1, source_target_pairs={{0,4},{4,0},{8,12},{12,8},{1,5},{5,1},{9,13},{13,9},{2,6},{6,2},{1... | collective-permute-start | bytes 1572872 | tf_op jit(solution)/shard_map/peer_pairs/ppermute | solution.py:137
  57.1 16.5 %collective-permute-start.11 = (bf16[256,1024]{1,0:T(8,128)(2,1)}, bf16[256,1024]{1,0:T(8,128)(2,1)}, u32[]{:S(2)}, u32[]{:S(2)}) collective-permute-start(bf16[256,1024]{1,0:T(8,128)(2,1)} %collective-permute-done.6), channel_id=1, source_target_pairs={{4,8},{8,4},{5,9},{9,5},{6,10},{10,6},{7,11},{11,7},{20,24},{24,20... | collective-permute-start | bytes 1572872 | tf_op jit(solution)/shard_map/attn_b_middle/ppermute | solution.py:142
  58.6 18.8 %collective-permute-start.12 = (bf16[128,2048]{1,0:T(8,128)(2,1)}, bf16[128,2048]{1,0:T(8,128)(2,1)}, u32[]{:S(2)}, u32[]{:S(2)}) collective-permute-start(bf16[128,2048]{1,0:T(8,128)(2,1)} %collective-permute-done.7.refs_2_), channel_id=1, source_target_pairs={{4,0},{8,12},{5,1},{9,13},{6,2},{10,14},{7,3},{11,15},{20,16},{24,... | collective-permute-start | bytes 1572872 | tf_op jit(solution)/shard_map/own_ends/ppermute | solution.py:152
  59.9 20.4 %collective-permute-start.22 = (bf16[256,1024]{1,0:T(8,128)(2,1)S(1)}, bf16[256,1024]{1,0:T(8,128)(2,1)}, u32[]{:S(2)}, u32[]{:S(2)}) collective-permute-start(bf16[256,1024]{1,0:T(8,128)(2,1)S(1)} %get-tuple-element.61), channel_id=1, source_target_pairs={{4,8},{8,4},{5,9},{9,5},{6,10},{10,6},{7,11},{11,7},{20,24},{24,20... | collective-permute-start | bytes 1572872 | tf_op jit(solution)/shard_map/attn_a_middle/ppermute | solution.py:142
  68.7 14.5 %collective-permute-start.5 = (bf16[256,1024]{1,0:T(8,128)(2,1)}, bf16[256,1024]{1,0:T(8,128)(2,1)S(1)}, u32[]{:S(2)}, u32[]{:S(2)}) collective-permute-start(bf16[256,1024]{1,0:T(8,128)(2,1)} %convolution_convert_fusion), channel_id=1, source_target_pairs={{0,2},{2,0},{1,3},{3,1},{4,6},{6,4},{5,7},{7,5},{8,10},{10,8},{9,1... | collective-permute-start | bytes 1572872 | tf_op jit(solution)/shard_map/back/ppermute | solution.py:128
  69.2 15.5 %copy-start.5 = (bf16[2048,1024]{1,0:T(8,128)(2,1)S(1)}, bf16[2048,1024]{1,0:T(8,128)(2,1)}, u32[]{:S(2)}) copy-start(bf16[2048,1024]{1,0:T(8,128)(2,1)} %param.12) | copy-start | bytes 12582916
  71.9 14.1 %copy-start.1 = (f32[8,128]{1,0:T(8,128)S(1)}, f32[8,128]{1,0:T(8,128)}, u32[]{:S(2)}) copy-start(f32[8,128]{1,0:T(8,128)} %shard_map.104.token_ref) | copy-start | bytes 12292
  72.0 32.2 %collective-permute-start.16 = (bf16[256,1024]{1,0:T(8,128)(2,1)}, bf16[256,1024]{1,0:T(8,128)(2,1)S(1)}, u32[]{:S(2)}, u32[]{:S(2)}) collective-permute-start(bf16[256,1024]{1,0:T(8,128)(2,1)} %collective-permute-done.6), channel_id=1, source_target_pairs={{0,2},{2,0},{1,3},{3,1},{4,6},{6,4},{5,7},{7,5},{8,10},{10,8},{9,1... | collective-permute-start | bytes 1572872 | tf_op jit(solution)/shard_map/attn_x1/ppermute | solution.py:128
  77.3 17.4 %collective-permute-start.24 = (bf16[256,1024]{1,0:T(8,128)(2,1)}, bf16[256,1024]{1,0:T(8,128)(2,1)S(1)}, u32[]{:S(2)}, u32[]{:S(2)}) collective-permute-start(bf16[256,1024]{1,0:T(8,128)(2,1)} %collective-permute-done.11), channel_id=1, source_target_pairs={{4,0},{8,12},{5,1},{9,13},{6,2},{10,14},{7,3},{11,15},{20,16},{24,... | collective-permute-start | bytes 1572872 | tf_op jit(solution)/shard_map/attn_b_ends/ppermute | solution.py:152
  78.6 27.2 %collective-permute-start.14 = (bf16[2,128,2048]{2,1,0:T(8,128)(2,1)S(1)}, bf16[2,128,2048]{2,1,0:T(8,128)(2,1)}, u32[]{:S(2)}, u32[]{:S(2)}) collective-permute-start(bf16[2,128,2048]{2,1,0:T(8,128)(2,1)S(1)} %pad_maximum_fusion.2), channel_id=1, source_target_pairs={{4,8},{8,4},{5,9},{9,5},{6,10},{10,6},{7,11},{11,7},{20,24},{24,20... | collective-permute-start | bytes 3145736 | tf_op jit(solution)/shard_map/peer_middle/ppermute | solution.py:142
  80.3 25.5 %collective-permute-start.15 = (bf16[128,2048]{1,0:T(8,128)(2,1)}, bf16[128,2048]{1,0:T(8,128)(2,1)S(1)}, u32[]{:S(2)}, u32[]{:S(2)}) collective-permute-start(bf16[128,2048]{1,0:T(8,128)(2,1)} %collective-permute-done.10), channel_id=1, source_target_pairs={{0,1},{1,0},{2,3},{3,2},{4,5},{5,4},{6,7},{7,6},{8,9},{9,8},{10,11... | collective-permute-start | bytes 1572872 | tf_op jit(solution)/shard_map/peer_1s/ppermute | solution.py:128
  83.2 18.7 %collective-permute-start.23 = (bf16[256,1024]{1,0:T(8,128)(2,1)}, bf16[256,1024]{1,0:T(8,128)(2,1)S(1)}, u32[]{:S(2)}, u32[]{:S(2)}) collective-permute-start(bf16[256,1024]{1,0:T(8,128)(2,1)} %collective-permute-done.22), channel_id=1, source_target_pairs={{4,0},{8,12},{5,1},{9,13},{6,2},{10,14},{7,3},{11,15},{20,16},{24,... | collective-permute-start | bytes 1572872 | tf_op jit(solution)/shard_map/attn_a_ends/ppermute | solution.py:152
  94.8 19.6 %collective-permute-start.21 = (bf16[3,128,2048]{2,1,0:T(8,128)(2,1)S(1)}, bf16[3,128,2048]{2,1,0:T(8,128)(2,1)S(1)}, u32[]{:S(2)}, u32[]{:S(2)}) collective-permute-start(bf16[3,128,2048]{2,1,0:T(8,128)(2,1)S(1)} %pad_maximum_fusion), channel_id=1, source_target_pairs={{0,1},{1,0},{2,3},{3,2},{4,5},{5,4},{6,7},{7,6},{8,9},{9,8},{10,11... | collective-permute-start | bytes 4718600 | tf_op jit(solution)/shard_map/own_s/ppermute | solution.py:128
  102.2 22.1 %collective-permute-start.25 = (bf16[256,1024]{1,0:T(8,128)(2,1)S(1)}, bf16[256,1024]{1,0:T(8,128)(2,1)S(1)}, u32[]{:S(2)}, u32[]{:S(2)}) collective-permute-start(bf16[256,1024]{1,0:T(8,128)(2,1)S(1)} %get-tuple-element.75), channel_id=1, source_target_pairs={{0,2},{2,0},{1,3},{3,1},{4,6},{6,4},{5,7},{7,5},{8,10},{10,8},{9,1... | collective-permute-start | bytes 1572872 | tf_op jit(solution)/shard_map/attn_xa/ppermute | solution.py:128
  104.2 21.3 %collective-permute-start.26 = (bf16[256,1024]{1,0:T(8,128)(2,1)S(1)}, bf16[256,1024]{1,0:T(8,128)(2,1)S(1)}, u32[]{:S(2)}, u32[]{:S(2)}) collective-permute-start(bf16[256,1024]{1,0:T(8,128)(2,1)S(1)} %get-tuple-element.76), channel_id=1, source_target_pairs={{0,2},{2,0},{1,3},{3,1},{4,6},{6,4},{5,7},{7,5},{8,10},{10,8},{9,1... | collective-permute-start | bytes 1572872 | tf_op jit(solution)/shard_map/attn_xb/ppermute | solution.py:128
  105.8 24.0 %collective-permute-start.20 = (bf16[2,128,2048]{2,1,0:T(8,128)(2,1)}, bf16[2,128,2048]{2,1,0:T(8,128)(2,1)}, u32[]{:S(2)}, u32[]{:S(2)}) collective-permute-start(bf16[2,128,2048]{2,1,0:T(8,128)(2,1)} %collective-permute-done.14), channel_id=1, source_target_pairs={{4,0},{8,12},{5,1},{9,13},{6,2},{10,14},{7,3},{11,15},{20,16},{24,... | collective-permute-start | bytes 3145736 | tf_op jit(solution)/shard_map/peer_ends/ppermute | solution.py:152
  107.1 25.4 %collective-permute-start.28 = (bf16[2,128,2048]{2,1,0:T(8,128)(2,1)}, bf16[2,128,2048]{2,1,0:T(8,128)(2,1)S(1)}, u32[]{:S(2)}, u32[]{:S(2)}) collective-permute-start(bf16[2,128,2048]{2,1,0:T(8,128)(2,1)} %collective-permute-done.14), channel_id=1, source_target_pairs={{0,1},{1,0},{2,3},{3,2},{4,5},{5,4},{6,7},{7,6},{8,9},{9,8},{10,11... | collective-permute-start | bytes 3145736 | tf_op jit(solution)/shard_map/peer_mid_s/ppermute | solution.py:128
  114.4 21.8 %collective-permute-start.17 = (bf16[64,512]{1,0:T(8,128)(2,1)S(1)}, bf16[64,512]{1,0:T(8,128)(2,1)S(1)}, u32[]{:S(2)}, u32[]{:S(2)}) collective-permute-start(bf16[64,512]{1,0:T(8,128)(2,1)S(1)} %get-tuple-element.89), channel_id=1, source_target_pairs={{4,0},{8,4},{12,8},{5,1},{9,5},{13,9},{6,2},{10,6},{14,10},{7,3},{... | collective-permute-start | bytes 196616 | tf_op jit(solution)/shard_map/grads/ppermute | solution.py:241
  124.2 12.0 %collective-permute-start.18 = (bf16[64,512]{1,0:T(8,128)(2,1)S(1)}, bf16[64,512]{1,0:T(8,128)(2,1)S(1)}, u32[]{:S(2)}, u32[]{:S(2)}) collective-permute-start(bf16[64,512]{1,0:T(8,128)(2,1)S(1)} %get-tuple-element.88), channel_id=1, source_target_pairs={{8,0},{12,4},{9,1},{13,5},{10,2},{14,6},{11,3},{15,7},{24,16},{28,... | collective-permute-start | bytes 196616 | tf_op jit(solution)/shard_map/grads/ppermute | solution.py:241
  125.5 11.0 %collective-permute-start.19 = (bf16[64,512]{1,0:T(8,128)(2,1)S(1)}, bf16[64,512]{1,0:T(8,128)(2,1)S(1)}, u32[]{:S(2)}, u32[]{:S(2)}) collective-permute-start(bf16[64,512]{1,0:T(8,128)(2,1)S(1)} %get-tuple-element.87), channel_id=1, source_target_pairs={{12,0},{13,1},{14,2},{15,3},{28,16},{29,17},{30,18},{31,19}} | collective-permute-start | bytes 196616 | tf_op jit(solution)/shard_map/grads/ppermute | solution.py:241
  129.8 2.9 %collective-permute-start.27 = (bf16[2,128,2048]{2,1,0:T(8,128)(2,1)}, bf16[2,128,2048]{2,1,0:T(8,128)(2,1)S(1)}, u32[]{:S(2)}, u32[]{:S(2)}) collective-permute-start(bf16[2,128,2048]{2,1,0:T(8,128)(2,1)} %collective-permute-done.20), channel_id=1, source_target_pairs={{0,1},{1,0},{2,3},{3,2},{4,5},{5,4},{6,7},{7,6},{8,9},{9,8},{10,11... | collective-permute-start | bytes 3145736 | tf_op jit(solution)/shard_map/peer_end_s/ppermute | solution.py:128
  (4 other events, 21.3 us)

commit v5 on v4

--- a/solution.py
+++ b/solution.py
@@ -267,16 +267,18 @@
             return turn(x, "head", 1, name)
 
         own_1 = pairs(own, "own")
-        own_2 = two_away(own_late, "own")
-        own_mid = middle(own_late, "own")
+        own_ma = middle(own_late, "own_a")
         attn_1 = pairs(turned, "attn")
         attn_x0 = [turn(turned, "dp", s, "attn_x0") for s in steps]
-        token = mark(token, own_1, own_2, own_mid)
-        (attn_0, own_2, *peer), (token,) = gate([turned, own_2, *peer], token)
-        own_end = ends(own_2, "own")
+        token = mark(token, own_1, own_ma)
+        (own_1, own_ma), (token,) = gate([own_1, own_ma], token)
+        own_mb = middle(own_1, "own_b")
+        own_ea = ends(own_ma, "own_a")
+        token = mark(token, own_mb, own_ea)
+        (own_mb, attn_0, *peer), (token,) = gate([own_mb, turned, *peer], token)
+        own_end = ends(own_mb, "own_b")
         peer_1 = [pairs(x, "peer") for x in peer]
         attn_mid_a = middle(attn_0, "attn_a")
-        token = mark(token)
         (attn_1,), (token,) = gate([attn_1], token)
         attn_mid_b = middle(attn_1, "attn_b")
         attn_end_a = ends(attn_mid_a, "attn_a")
@@ -293,13 +295,13 @@
         peer_1s = [swap(x, "peer_1s") for x in peer_1]
         grad_q, grad_kv = backward(d_part)
         (own_1, own_end), (grad_kv,) = gate([own_1, own_end], grad_kv)
-        own_all = jnp.stack([own_1, own_2, jnp.where(at_end, own_end, own_mid)])
+        own_all = jnp.stack([own_1, jnp.where(at_end, own_ea, own_ma), jnp.where(at_end, own_end, own_mb)])
         own_all_s = swap(own_all, "own_s")
-        peer_send, (grad_kv, *rest) = gate(peer_mid, grad_kv, *peer_1s, *attn_x1)
+        peer_send, (grad_kv, attn_1, *rest) = gate(peer_mid, grad_kv, attn_1, *peer_1s, *attn_x1)
         peer_1s, attn_x1 = rest[: n_dp - 1], rest[n_dp - 1 :]
         peer_end = [ends(x, "peer") for x in peer_send]
         peer_mid_s = [swap(x, "peer_mid_s") for x in peer_send]
-        attn_all = jnp.stack([attn_1, jnp.where(at_end, attn_a, attn_b), jnp.where(at_end, attn_b, attn_a)])
+        attn_all = jnp.stack([attn_1, attn_a, attn_b])
         share = own_all.shape[0] * half
         rows = jnp.concatenate([own_rows, own_all.reshape(share, -1), own_all_s.reshape(share, -1)], 0)
         cols = [attn, attn_all[:, :half].reshape(share, -1), attn_all[:, half:].reshape(share, -1)]

time: 138 us -> 135 us (0.978)
  starting transfers between devices: 46.5 us -> 41.2 us
  other arithmetic: 9.59 us -> 6.62 us
  matrix products: 25.6 us -> 27.9 us
  waiting for transfers between devices: 34.1 us -> 36.4 us
    ppermute x4 -> x5, waiting for transfers between devices: 13.8 us -> 34.7 us  [ends(): return lax.ppermute(x, 'ctx', [(1, 0), (2, 3)])]
    ppermute x3, waiting for transfers between devices: 8.99 us -> 0.22 us  [pairs(): return lax.ppermute(x, 'ctx', [(0, 1), (1, 0), (2, 3), (3, 2)])]
    ppermute x3, starting transfers between devices: 13.7 us -> 5.88 us  [pairs(): return lax.ppermute(x, 'ctx', [(0, 1), (1, 0), (2, 3), (3, 2)])]
    ppermute x1 -> x0, waiting for transfers between devices: 7.79 us -> none  [two_away(): return lax.ppermute(x, 'ctx', [(0, 2), (1, 3), (2, 0), (3, 1)])]
    ppermute x11, waiting for transfers between devices: 3.12 us -> 0.17 us  [turn(): return lax.ppermute(x, axis, [(i, (i + step) % n) for i in range(n)])]
    dot_general x1, matrix products: 1.29 us -> 3.76 us  [shards(): d_mine = jnp.dot(own_rows, out_weight, preferred_element_type=jnp.float32)]
    ppermute x11, starting transfers between devices: 6.43 us -> 8.11 us  [turn(): return lax.ppermute(x, axis, [(i, (i + step) % n) for i in range(n)])]
    ppermute x4 -> x5, starting transfers between devices: 5.3 us -> 6.74 us  [ends(): return lax.ppermute(x, 'ctx', [(1, 0), (2, 3)])]
  transfers between devices with their start and end apart: 29 -> 30, of which waited for: 9 -> 8; matrix products, arithmetic and copies ran while one was open for 29% -> 29% of each run, Pallas kernels for 9% -> 10%
where the time goes in v5:
time: 135 us; the launch traced here: 134 us
  starting transfers between devices  41.2 us (31%)
  waiting for transfers between devices  36.4 us (27%)
  matrix products  27.9 us (21%)
  Pallas kernels  12.9 us (10%)
  local copies, waits for them, and re-layouts  7.12 us (5%)
  other arithmetic  6.62 us (5%)
  between operations  1.81 us (1%)
    ppermute x5, waiting for transfers between devices, ends(): return lax.ppermute(x, 'ctx', [(1, 0), (2, 3)])  34.7 us
    dot_general x4, matrix products, dot(): lax.dot_general(a, b, (contract, ((), ())), preferred_element_type=jnp.fl...  19.9 us
    ppermute x3, starting transfers between devices, shards(): lax.ppermute(tail, 'ctx', line_pairs(n_ctx, s))  10.7 us
    pallas_call x2, Pallas kernels, call_attention(): pl.pallas_call(kernel, out_shape=out_shape, in_specs=[pl.BlockSpec(memory...  10.4 us
    ppermute x11, starting transfers between devices, turn(): return lax.ppermute(x, axis, [(i, (i + step) % n) for i in range(n)])  8.11 us
    ppermute x5, starting transfers between devices, ends(): return lax.ppermute(x, 'ctx', [(1, 0), (2, 3)])  6.74 us
    ppermute x5, starting transfers between devices, middle(): return lax.ppermute(x, 'ctx', [(1, 2), (2, 1)])  5.92 us
    ppermute x3, starting transfers between devices, pairs(): return lax.ppermute(x, 'ctx', [(0, 1), (1, 0), (2, 3), (3, 2)])  5.88 us
  transfers between devices with their start and end apart: 30, of which 8 were waited for; matrix products, arithmetic and copies ran while one was open for 29% of the time, Pallas kernels for 10%

profile of v5, /device:TPU:0, one launch (start us, length us, event | category | flops | bytes accessed | tf_op | source)
XLA Modules:
  0.0 134.0 jit_solution(12886816379693461212)
XLA Ops:
  1.5 4.9 %collective-permute-start = (bf16[64,512]{1,0:T(8,128)(2,1)S(1)}, bf16[64,512]{1,0:T(8,128)(2,1)S(1)}, u32[]{:S(2)}, u32[]{:S(2)}) collective-permute-start(bf16[64,512]{1,0:T(8,128)(2,1)S(1)} %pad_maximum_fusion.6), channel_id=1, source_target_pairs={{0,4},{4,8},{8,12},{1,5},{5,9},{9,13},{2,6},{6,10},{10,14},{3,7},{... | collective-permute-start | bytes 196616 | tf_op jit(solution)/shard_map/ppermute | solution.py:175
  6.5 4.5 %collective-permute-start.1 = (bf16[64,512]{1,0:T(8,128)(2,1)S(1)}, bf16[64,512]{1,0:T(8,128)(2,1)S(1)}, u32[]{:S(2)}, u32[]{:S(2)}) collective-permute-start(bf16[64,512]{1,0:T(8,128)(2,1)S(1)} %pad_maximum_fusion.6), channel_id=1, source_target_pairs={{0,8},{4,12},{1,9},{5,13},{2,10},{6,14},{3,11},{7,15},{16,24},{20,... | collective-permute-start | bytes 196616 | tf_op jit(solution)/shard_map/ppermute | solution.py:175
  11.0 1.3 collective-permute-start.2
  12.3 2.1 %dynamic-slice_bitcast_fusion.1 = (bf16[128,2048]{1,0:T(8,128)(2,1)S(1)}, bf16[128,2048]{1,0:T(8,128)(2,1)}) fusion(bf16[1,256,4096]{2,1,0:T(8,128)(2,1)} %param.13, s32[]{:T(128)S(6)} %select_n.57, s32[]{:T(128)S(6)} %select_n.59, s32[]{:T(128)S(6)} %select_n.58), kind=kLoop, calls=%fused_computation.44 | loop fusion | bytes 2097164 | tf_op jit(solution)/shard_map/dynamic_slice | solution.py:185
  14.4 1.5 %collective-permute-start.3 = (bf16[128,2048]{1,0:T(8,128)(2,1)S(1)}, bf16[128,2048]{1,0:T(8,128)(2,1)S(1)}, u32[]{:S(2)}, u32[]{:S(2)}) collective-permute-start(bf16[128,2048]{1,0:T(8,128)(2,1)S(1)} %get-tuple-element.82), channel_id=1, source_target_pairs={{0,2},{2,0},{1,3},{3,1},{4,6},{6,4},{5,7},{7,5},{8,10},{10,8},{9,1... | collective-permute-start | bytes 1572872 | tf_op jit(solution)/shard_map/peer_in/ppermute | solution.py:128
  15.9 2.3 %dynamic-slice_bitcast_fusion = bf16[256,2048]{1,0:T(8,128)(2,1)} fusion(bf16[1,256,4096]{2,1,0:T(8,128)(2,1)} %param.13, s32[]{:T(128)S(6)} %select_n.58), kind=kLoop, calls=%fused_computation.31 | loop fusion | bytes 2097156 | tf_op jit(solution)/shard_map/dynamic_slice | solution.py:217
  19.0 1.5 %collective-permute-start.8 = (bf16[128,2048]{1,0:T(8,128)(2,1)}, bf16[128,2048]{1,0:T(8,128)(2,1)}, u32[]{:S(2)}, u32[]{:S(2)}) collective-permute-start(bf16[128,2048]{1,0:T(8,128)(2,1)} %get-tuple-element.50), channel_id=1, source_target_pairs={{4,8},{8,4},{5,9},{9,5},{6,10},{10,6},{7,11},{11,7},{20,24},{24,20... | collective-permute-start | bytes 1572872 | tf_op jit(solution)/shard_map/own_a_middle/ppermute | solution.py:142
  20.9 4.1 %shard_map.102 = (bf16[256,1024]{1,0:T(8,128)(2,1)S(1)}, bf16[256,1024]{1,0:T(8,128)(2,1)S(1)}) custom-call(s32[1,2]{1,0:T(1,128)S(1)} %add_bitcast_fusion.count_ref, s32[256,1]{1,0:T(8,128)S(1)} %copy.12.idc_ref, s32[1,512]{1,0:T(1,128)S(1)} %pad.4.idr_ref, bf16[256,1024]{1,0:T(8,128)(2,1)S(1)} %bitcast.47, bf16[512,256]{1,0:T(8,128)(2,1)S(1)} %pad_maximum_fusion.3.k_ref, ...), custom_call_target="tpu_custom_call" | custom-call | flops 536870912 | bytes 4194304 | tf_op jit(solution)/shard_map/pallas_call | solution.py:95
  25.0 2.6 %collective-permute-start.6 = (bf16[256,1024]{1,0:T(8,128)(2,1)S(1)}, bf16[256,1024]{1,0:T(8,128)(2,1)}, u32[]{:S(2)}, u32[]{:S(2)}) collective-permute-start(bf16[256,1024]{1,0:T(8,128)(2,1)S(1)} %get-tuple-element.69), channel_id=1, source_target_pairs={{0,4},{4,0},{8,12},{12,8},{1,5},{5,1},{9,13},{13,9},{2,6},{6,2},{1... | collective-permute-start | bytes 1572872 | tf_op jit(solution)/shard_map/attn_pairs/ppermute | solution.py:137
  31.5 1.5 %collective-permute-start.9 = (bf16[128,2048]{1,0:T(8,128)(2,1)}, bf16[128,2048]{1,0:T(8,128)(2,1)}, u32[]{:S(2)}, u32[]{:S(2)}) collective-permute-start(bf16[128,2048]{1,0:T(8,128)(2,1)} %collective-permute-done.7.refs_1_), channel_id=1, source_target_pairs={{4,8},{8,4},{5,9},{9,5},{6,10},{10,6},{7,11},{11,7},{20,24},{24,20... | collective-permute-start | bytes 1572872 | tf_op jit(solution)/shard_map/own_b_middle/ppermute | solution.py:142
  33.7 4.3 %convolution_convert_fusion = bf16[256,1024]{1,0:T(8,128)(2,1)} fusion(bf16[2048,1024]{1,0:T(8,128)(2,1)} %param.12, bf16[128,2048]{1,0:T(8,128)(2,1)S(1)} %get-tuple-element.87, bf16[128,2048]{1,0:T(8,128)(2,1)S(1)} %get-tuple-element.86), kind=kOutput, calls=%fused_computation.23 | convolution fusion | flops 1076101120 | bytes 5767168 | tf_op jit(solution)/shard_map/dot_general | solution.py:215
  38.0 2.5 %collective-permute-start.5 = (bf16[256,1024]{1,0:T(8,128)(2,1)}, bf16[256,1024]{1,0:T(8,128)(2,1)S(1)}, u32[]{:S(2)}, u32[]{:S(2)}) collective-permute-start(bf16[256,1024]{1,0:T(8,128)(2,1)} %convolution_convert_fusion), channel_id=1, source_target_pairs={{0,2},{2,0},{1,3},{3,1},{4,6},{6,4},{5,7},{7,5},{8,10},{10,8},{9,1... | collective-permute-start | bytes 1572872 | tf_op jit(solution)/shard_map/back/ppermute | solution.py:128
  40.5 9.8 %collective-permute-done.10.refs_2_ = bf16[128,2048]{1,0:T(8,128)(2,1)} collective-permute-done((bf16[128,2048]{1,0:T(8,128)(2,1)}, bf16[128,2048]{1,0:T(8,128)(2,1)}, u32[]{:S(2)}, u32[]{:S(2)}) %collective-permute-start.10) | collective-permute-done | bytes 524320 | tf_op jit(solution)/shard_map/own_a_ends/ppermute | solution.py:152
  51.6 3.3 %collective-permute-start.11 = (bf16[128,2048]{1,0:T(8,128)(2,1)S(1)}, bf16[128,2048]{1,0:T(8,128)(2,1)S(1)}, u32[]{:S(2)}, u32[]{:S(2)}) collective-permute-start(bf16[128,2048]{1,0:T(8,128)(2,1)S(1)} %collective-permute-done.3), channel_id=1, source_target_pairs={{0,4},{4,0},{8,12},{12,8},{1,5},{5,1},{9,13},{13,9},{2,6},{6,2},{1... | collective-permute-start | bytes 1572872 | tf_op jit(solution)/shard_map/peer_pairs/ppermute | solution.py:137
  55.6 1.3 collective-permute-start.13
  58.7 3.8 %fusion.51.d_mine_ref = f32[256,1024]{1,0:T(8,128)S(1)} fusion(bf16[256,2048]{1,0:T(8,128)(2,1)} %dynamic-slice_bitcast_fusion, bf16[2048,1024]{1,0:T(8,128)(2,1)} %param.12), kind=kOutput, calls=%fused_computation.74 | convolution fusion | flops 1073741824 | bytes 6291456 | tf_op jit(solution)/shard_map/dot_general | solution.py:219
  62.5 6.3 %shard_map.105 = (bf16[256,1024]{1,0:T(8,128)(2,1)}, f32[512,512]{1,0:T(8,128)S(1)}) custom-call(s32[1,2]{1,0:T(1,128)S(1)} %add_bitcast_fusion.count_ref, s32[256,1]{1,0:T(8,128)S(1)} %copy.12.idc_ref, s32[1,512]{1,0:T(1,128)S(1)} %pad.4.idr_ref, bf16[256,1024]{1,0:T(8,128)(2,1)S(1)} %bitcast.48, bf16[512,256]{1,0:T(8,128)(2,1)S(1)} %pad_maximum_fusion.3.k_ref, ...), custom_call_target="tpu_custom_call" | custom-call | flops 1342177280 | bytes 4194304 | tf_op jit(solution)/shard_map/pallas_call | solution.py:95
  69.4 5.6 %collective-permute-done.13 = bf16[128,2048]{1,0:T(8,128)(2,1)S(1)} collective-permute-done((bf16[128,2048]{1,0:T(8,128)(2,1)}, bf16[128,2048]{1,0:T(8,128)(2,1)S(1)}, u32[]{:S(2)}, u32[]{:S(2)}) %collective-permute-start.13) | collective-permute-done | bytes 524320 | tf_op jit(solution)/shard_map/own_b_ends/ppermute | solution.py:152
  76.4 1.6 %collective-permute-start.15 = (bf16[2,128,2048]{2,1,0:T(8,128)(2,1)S(1)}, bf16[2,128,2048]{2,1,0:T(8,128)(2,1)}, u32[]{:S(2)}, u32[]{:S(2)}) collective-permute-start(bf16[2,128,2048]{2,1,0:T(8,128)(2,1)S(1)} %pad_maximum_fusion.2), channel_id=1, source_target_pairs={{4,8},{8,4},{5,9},{9,5},{6,10},{10,6},{7,11},{11,7},{20,24},{24,20... | collective-permute-start | bytes 3145736 | tf_op jit(solution)/shard_map/peer_middle/ppermute | solution.py:142
  78.0 1.5 %collective-permute-start.24 = (bf16[256,1024]{1,0:T(8,128)(2,1)S(1)}, bf16[256,1024]{1,0:T(8,128)(2,1)S(1)}, u32[]{:S(2)}, u32[]{:S(2)}) collective-permute-start(bf16[256,1024]{1,0:T(8,128)(2,1)S(1)} %collective-permute-done.23), channel_id=1, source_target_pairs={{4,0},{8,12},{5,1},{9,13},{6,2},{10,14},{7,3},{11,15},{20,16},{24,... | collective-permute-start | bytes 1572872 | tf_op jit(solution)/shard_map/attn_a_ends/ppermute | solution.py:152
  80.8 11.0 %collective-permute-done.25 = bf16[256,1024]{1,0:T(8,128)(2,1)S(1)} collective-permute-done((bf16[256,1024]{1,0:T(8,128)(2,1)S(1)}, bf16[256,1024]{1,0:T(8,128)(2,1)S(1)}, u32[]{:S(2)}, u32[]{:S(2)}) %collective-permute-start.25) | collective-permute-done | bytes 524320 | tf_op jit(solution)/shard_map/attn_b_ends/ppermute | solution.py:152
  91.9 6.4 %collective-permute-done.24 = bf16[256,1024]{1,0:T(8,128)(2,1)S(1)} collective-permute-done((bf16[256,1024]{1,0:T(8,128)(2,1)S(1)}, bf16[256,1024]{1,0:T(8,128)(2,1)S(1)}, u32[]{:S(2)}, u32[]{:S(2)}) %collective-permute-start.24) | collective-permute-done | bytes 524320 | tf_op jit(solution)/shard_map/attn_a_ends/ppermute | solution.py:152
  98.2 2.8 %collective-permute-start.27 = (bf16[256,1024]{1,0:T(8,128)(2,1)S(1)}, bf16[256,1024]{1,0:T(8,128)(2,1)S(1)}, u32[]{:S(2)}, u32[]{:S(2)}) collective-permute-start(bf16[256,1024]{1,0:T(8,128)(2,1)S(1)} %broadcast_select_fusion.2), channel_id=1, source_target_pairs={{0,2},{2,0},{1,3},{3,1},{4,6},{6,4},{5,7},{7,5},{8,10},{10,8},{9,1... | collective-permute-start | bytes 1572872 | tf_op jit(solution)/shard_map/attn_xb/ppermute | solution.py:128
  101.3 1.4 %collective-permute-start.21 = (bf16[2,128,2048]{2,1,0:T(8,128)(2,1)}, bf16[2,128,2048]{2,1,0:T(8,128)(2,1)}, u32[]{:S(2)}, u32[]{:S(2)}) collective-permute-start(bf16[2,128,2048]{2,1,0:T(8,128)(2,1)} %collective-permute-done.15), channel_id=1, source_target_pairs={{4,0},{8,12},{5,1},{9,13},{6,2},{10,14},{7,3},{11,15},{20,16},{24,... | collective-permute-start | bytes 3145736 | tf_op jit(solution)/shard_map/peer_ends/ppermute | solution.py:152
  102.9 1.4 %pad_maximum_fusion.1 = bf16[3,256,1024]{2,1,0:T(8,128)(2,1)S(1)} fusion(bf16[1,256,1024]{2,1,0:T(8,128)(2,1)S(1)} %bitcast.53, bf16[1,256,1024]{2,1,0:T(8,128)(2,1)S(1)} %bitcast.54, bf16[1,256,1024]{2,1,0:T(8,128)(2,1)} %bitcast.22), kind=kLoop, calls=%fused_computation.22 | loop fusion | flops 1572864 | bytes 3145728 | tf_op jit(solution)/shard_map/stack | solution.py:304
  104.5 6.8 %fusion.14 = f32[2048,1024]{1,0:T(8,128)} fusion(bf16[128,2048]{1,0:T(8,128)(2,1)S(1)} %collective-permute-done.16, bf16[128,2048]{1,0:T(8,128)(2,1)S(1)} %collective-permute-done.11, bf16[128,2048]{1,0:T(8,128)(2,1)S(1)} %copy-done.5, bf16[128,2048]{1,0:T(8,128)(2,1)S(1)} %collective-permute-done.3, bf16[256,1024]{1,0:T(8,128)(2,1)S(1)} %collective-permute-done.17, ...), kind=kOutput, calls=%fused_computation.13 | convolution fusion | flops 2157969408 | bytes 11534336 | tf_op jit(solution)/shard_map/dot_general | solution.py:22
  112.6 8.3 %fusion.6 = f32[2048,1024]{1,0:T(8,128)S(1)} fusion(f32[2048,1024]{1,0:T(8,128)} %fusion.14, bf16[384,2048]{1,0:T(8,128)(2,1)S(1)} %bitcast.62, bf16[384,2048]{1,0:T(8,128)(2,1)S(1)} %bitcast.55, bf16[256,2048]{1,0:T(8,128)(2,1)S(1)} %copy-done.3, bf16[384,1024]{1,0:T(8,128)(2,1)S(1)} %bitcast.57, bf16[384,1024]{1,0:T(8,128)(2,1)S(1)} %bitcast.56, ...), kind=kOutput, calls=%fused_computation.7 | convolution fusion | flops 4315938816 | bytes 23068672 | tf_op jit(solution)/shard_map/dot_general | solution.py:22
  121.0 1.3 collective-permute-start.19
  122.3 1.3 collective-permute-start.20
  123.6 2.0 %collective-permute-done.21 = bf16[2,128,2048]{2,1,0:T(8,128)(2,1)} collective-permute-done((bf16[2,128,2048]{2,1,0:T(8,128)(2,1)}, bf16[2,128,2048]{2,1,0:T(8,128)(2,1)}, u32[]{:S(2)}, u32[]{:S(2)}) %collective-permute-start.21) | collective-permute-done | bytes 1048608 | tf_op jit(solution)/shard_map/peer_ends/ppermute | solution.py:152
  125.5 1.3 broadcast_select_fusion.1
  128.6 3.4 %add_convert_fusion = bf16[2048,1024]{1,0:T(8,128)(2,1)} fusion(f32[2048,1024]{1,0:T(8,128)S(1)} %fusion.6, f32[2048,1024]{1,0:T(8,128)S(1)} %fusion.28, bf16[256,2048]{1,0:T(8,128)(2,1)S(1)} %bitcast.51, bf16[128,1024]{1,0:T(8,128)(2,1)S(1)} %get-tuple-element.90, bf16[128,1024]{1,0:T(8,128)(2,1)S(1)} %get-tuple-element.88), kind=kOutput, calls=%fused_computation | convolution fusion | flops 1081081856 | bytes 22544384 | tf_op jit(solution)/shard_map/dot_general | solution.py:22
  (89 shorter events, 18.7 us)
Async XLA Ops:
  0.6 20.2 %copy-start.7 = (bf16[1,256,256]{2,1,0:T(8,128)(2,1)S(1)}, bf16[1,256,256]{2,1,0:T(8,128)(2,1)}, u32[]{:S(2)}) copy-start(bf16[1,256,256]{2,1,0:T(8,128)(2,1)} %param.9) | copy-start | bytes 393220
  0.7 20.2 %copy-start = (bf16[1,256,1024]{2,1,0:T(8,128)(2,1)S(1)}, bf16[1,256,1024]{2,1,0:T(8,128)(2,1)}, u32[]{:S(2)}) copy-start(bf16[1,256,1024]{2,1,0:T(8,128)(2,1)} %param.7) | copy-start | bytes 1572868
  1.5 17.4 %collective-permute-start = (bf16[64,512]{1,0:T(8,128)(2,1)S(1)}, bf16[64,512]{1,0:T(8,128)(2,1)S(1)}, u32[]{:S(2)}, u32[]{:S(2)}) collective-permute-start(bf16[64,512]{1,0:T(8,128)(2,1)S(1)} %pad_maximum_fusion.6), channel_id=1, source_target_pairs={{0,4},{4,8},{8,12},{1,5},{5,9},{9,13},{2,6},{6,10},{10,14},{3,7},{... | collective-permute-start | bytes 196616 | tf_op jit(solution)/shard_map/ppermute | solution.py:175
  6.5 12.5 %collective-permute-start.1 = (bf16[64,512]{1,0:T(8,128)(2,1)S(1)}, bf16[64,512]{1,0:T(8,128)(2,1)S(1)}, u32[]{:S(2)}, u32[]{:S(2)}) collective-permute-start(bf16[64,512]{1,0:T(8,128)(2,1)S(1)} %pad_maximum_fusion.6), channel_id=1, source_target_pairs={{0,8},{4,12},{1,9},{5,13},{2,10},{6,14},{3,11},{7,15},{16,24},{20,... | collective-permute-start | bytes 196616 | tf_op jit(solution)/shard_map/ppermute | solution.py:175
  11.0 8.0 %collective-permute-start.2 = (bf16[64,512]{1,0:T(8,128)(2,1)S(1)}, bf16[64,512]{1,0:T(8,128)(2,1)S(1)}, u32[]{:S(2)}, u32[]{:S(2)}) collective-permute-start(bf16[64,512]{1,0:T(8,128)(2,1)S(1)} %pad_maximum_fusion.6), channel_id=1, source_target_pairs={{0,12},{1,13},{2,14},{3,15},{16,28},{17,29},{18,30},{19,31}} | collective-permute-start | bytes 196616 | tf_op jit(solution)/shard_map/ppermute | solution.py:175
  14.4 13.9 %collective-permute-start.7 = (bf16[128,2048]{1,0:T(8,128)(2,1)}, bf16[128,2048]{1,0:T(8,128)(2,1)}, u32[]{:S(2)}, u32[]{:S(2)}) collective-permute-start(bf16[128,2048]{1,0:T(8,128)(2,1)} %get-tuple-element.50), channel_id=1, source_target_pairs={{0,4},{4,0},{8,12},{12,8},{1,5},{5,1},{9,13},{13,9},{2,6},{6,2},{1... | collective-permute-start | bytes 1572872 | tf_op jit(solution)/shard_map/own_pairs/ppermute | solution.py:137
  14.4 13.7 %collective-permute-start.3 = (bf16[128,2048]{1,0:T(8,128)(2,1)S(1)}, bf16[128,2048]{1,0:T(8,128)(2,1)S(1)}, u32[]{:S(2)}, u32[]{:S(2)}) collective-permute-start(bf16[128,2048]{1,0:T(8,128)(2,1)S(1)} %get-tuple-element.82), channel_id=1, source_target_pairs={{0,2},{2,0},{1,3},{3,1},{4,6},{6,4},{5,7},{7,5},{8,10},{10,8},{9,1... | collective-permute-start | bytes 1572872 | tf_op jit(solution)/shard_map/peer_in/ppermute | solution.py:128
  19.0 9.3 %collective-permute-start.8 = (bf16[128,2048]{1,0:T(8,128)(2,1)}, bf16[128,2048]{1,0:T(8,128)(2,1)}, u32[]{:S(2)}, u32[]{:S(2)}) collective-permute-start(bf16[128,2048]{1,0:T(8,128)(2,1)} %get-tuple-element.50), channel_id=1, source_target_pairs={{4,8},{8,4},{5,9},{9,5},{6,10},{10,6},{7,11},{11,7},{20,24},{24,20... | collective-permute-start | bytes 1572872 | tf_op jit(solution)/shard_map/own_a_middle/ppermute | solution.py:142
  25.0 29.9 %collective-permute-start.6 = (bf16[256,1024]{1,0:T(8,128)(2,1)S(1)}, bf16[256,1024]{1,0:T(8,128)(2,1)}, u32[]{:S(2)}, u32[]{:S(2)}) collective-permute-start(bf16[256,1024]{1,0:T(8,128)(2,1)S(1)} %get-tuple-element.69), channel_id=1, source_target_pairs={{0,4},{4,0},{8,12},{12,8},{1,5},{5,1},{9,13},{13,9},{2,6},{6,2},{1... | collective-permute-start | bytes 1572872 | tf_op jit(solution)/shard_map/attn_pairs/ppermute | solution.py:137
  27.6 41.8 %collective-permute-start.14 = (bf16[256,1024]{1,0:T(8,128)(2,1)S(1)}, bf16[256,1024]{1,0:T(8,128)(2,1)}, u32[]{:S(2)}, u32[]{:S(2)}) collective-permute-start(bf16[256,1024]{1,0:T(8,128)(2,1)S(1)} %get-tuple-element.69), channel_id=1, source_target_pairs={{0,2},{2,0},{1,3},{3,1},{4,6},{6,4},{5,7},{7,5},{8,10},{10,8},{9,1... | collective-permute-start | bytes 1572872 | tf_op jit(solution)/shard_map/attn_x0/ppermute | solution.py:128
  28.1 4.8 %collective-permute-start.4 = (bf16[128,2048]{1,0:T(8,128)(2,1)S(1)}, bf16[128,2048]{1,0:T(8,128)(2,1)S(1)}, u32[]{:S(2)}, u32[]{:S(2)}) collective-permute-start(bf16[128,2048]{1,0:T(8,128)(2,1)S(1)} %collective-permute-done.3), channel_id=1, source_target_pairs={{0,1},{1,0},{2,3},{3,2},{4,5},{5,4},{6,7},{7,6},{8,9},{9,8},{10,11... | collective-permute-start | bytes 1572872 | tf_op jit(solution)/shard_map/peer_s/ppermute | solution.py:128
  30.2 20.1 %collective-permute-start.10 = (bf16[128,2048]{1,0:T(8,128)(2,1)}, bf16[128,2048]{1,0:T(8,128)(2,1)}, u32[]{:S(2)}, u32[]{:S(2)}) collective-permute-start(bf16[128,2048]{1,0:T(8,128)(2,1)} %collective-permute-done.8.refs_2_), channel_id=1, source_target_pairs={{4,0},{8,12},{5,1},{9,13},{6,2},{10,14},{7,3},{11,15},{20,16},{24,... | collective-permute-start | bytes 1572872 | tf_op jit(solution)/shard_map/own_a_ends/ppermute | solution.py:152
  31.5 18.8 %collective-permute-start.9 = (bf16[128,2048]{1,0:T(8,128)(2,1)}, bf16[128,2048]{1,0:T(8,128)(2,1)}, u32[]{:S(2)}, u32[]{:S(2)}) collective-permute-start(bf16[128,2048]{1,0:T(8,128)(2,1)} %collective-permute-done.7.refs_1_), channel_id=1, source_target_pairs={{4,8},{8,4},{5,9},{9,5},{6,10},{10,6},{7,11},{11,7},{20,24},{24,20... | collective-permute-start | bytes 1572872 | tf_op jit(solution)/shard_map/own_b_middle/ppermute | solution.py:142
  38.0 20.0 %collective-permute-start.5 = (bf16[256,1024]{1,0:T(8,128)(2,1)}, bf16[256,1024]{1,0:T(8,128)(2,1)S(1)}, u32[]{:S(2)}, u32[]{:S(2)}) collective-permute-start(bf16[256,1024]{1,0:T(8,128)(2,1)} %convolution_convert_fusion), channel_id=1, source_target_pairs={{0,2},{2,0},{1,3},{3,1},{4,6},{6,4},{5,7},{7,5},{8,10},{10,8},{9,1... | collective-permute-start | bytes 1572872 | tf_op jit(solution)/shard_map/back/ppermute | solution.py:128
  51.6 17.2 %collective-permute-start.11 = (bf16[128,2048]{1,0:T(8,128)(2,1)S(1)}, bf16[128,2048]{1,0:T(8,128)(2,1)S(1)}, u32[]{:S(2)}, u32[]{:S(2)}) collective-permute-start(bf16[128,2048]{1,0:T(8,128)(2,1)S(1)} %collective-permute-done.3), channel_id=1, source_target_pairs={{0,4},{4,0},{8,12},{12,8},{1,5},{5,1},{9,13},{13,9},{2,6},{6,2},{1... | collective-permute-start | bytes 1572872 | tf_op jit(solution)/shard_map/peer_pairs/ppermute | solution.py:137
  54.9 14.5 %collective-permute-start.12 = (bf16[256,1024]{1,0:T(8,128)(2,1)}, bf16[256,1024]{1,0:T(8,128)(2,1)S(1)}, u32[]{:S(2)}, u32[]{:S(2)}) collective-permute-start(bf16[256,1024]{1,0:T(8,128)(2,1)} %collective-permute-done.6), channel_id=1, source_target_pairs={{4,8},{8,4},{5,9},{9,5},{6,10},{10,6},{7,11},{11,7},{20,24},{24,20... | collective-permute-start | bytes 1572872 | tf_op jit(solution)/shard_map/attn_b_middle/ppermute | solution.py:142
  55.6 19.5 %collective-permute-start.13 = (bf16[128,2048]{1,0:T(8,128)(2,1)}, bf16[128,2048]{1,0:T(8,128)(2,1)S(1)}, u32[]{:S(2)}, u32[]{:S(2)}) collective-permute-start(bf16[128,2048]{1,0:T(8,128)(2,1)} %collective-permute-done.9.refs_1_), channel_id=1, source_target_pairs={{4,0},{8,12},{5,1},{9,13},{6,2},{10,14},{7,3},{11,15},{20,16},{24,... | collective-permute-start | bytes 1572872 | tf_op jit(solution)/shard_map/own_b_ends/ppermute | solution.py:152
  58.0 20.0 %collective-permute-start.23 = (bf16[256,1024]{1,0:T(8,128)(2,1)S(1)}, bf16[256,1024]{1,0:T(8,128)(2,1)S(1)}, u32[]{:S(2)}, u32[]{:S(2)}) collective-permute-start(bf16[256,1024]{1,0:T(8,128)(2,1)S(1)} %get-tuple-element.69), channel_id=1, source_target_pairs={{4,8},{8,4},{5,9},{9,5},{6,10},{10,6},{7,11},{11,7},{20,24},{24,20... | collective-permute-start | bytes 1572872 | tf_op jit(solution)/shard_map/attn_a_middle/ppermute | solution.py:142
  68.7 32.4 %collective-permute-start.17 = (bf16[256,1024]{1,0:T(8,128)(2,1)}, bf16[256,1024]{1,0:T(8,128)(2,1)S(1)}, u32[]{:S(2)}, u32[]{:S(2)}) collective-permute-start(bf16[256,1024]{1,0:T(8,128)(2,1)} %collective-permute-done.6), channel_id=1, source_target_pairs={{0,2},{2,0},{1,3},{3,1},{4,6},{6,4},{5,7},{7,5},{8,10},{10,8},{9,1... | collective-permute-start | bytes 1572872 | tf_op jit(solution)/shard_map/attn_x1/ppermute | solution.py:128
  75.1 16.7 %collective-permute-start.25 = (bf16[256,1024]{1,0:T(8,128)(2,1)S(1)}, bf16[256,1024]{1,0:T(8,128)(2,1)S(1)}, u32[]{:S(2)}, u32[]{:S(2)}) collective-permute-start(bf16[256,1024]{1,0:T(8,128)(2,1)S(1)} %collective-permute-done.12), channel_id=1, source_target_pairs={{4,0},{8,12},{5,1},{9,13},{6,2},{10,14},{7,3},{11,15},{20,16},{24,... | collective-permute-start | bytes 1572872 | tf_op jit(solution)/shard_map/attn_b_ends/ppermute | solution.py:152
  76.4 24.9 %collective-permute-start.15 = (bf16[2,128,2048]{2,1,0:T(8,128)(2,1)S(1)}, bf16[2,128,2048]{2,1,0:T(8,128)(2,1)}, u32[]{:S(2)}, u32[]{:S(2)}) collective-permute-start(bf16[2,128,2048]{2,1,0:T(8,128)(2,1)S(1)} %pad_maximum_fusion.2), channel_id=1, source_target_pairs={{4,8},{8,4},{5,9},{9,5},{6,10},{10,6},{7,11},{11,7},{20,24},{24,20... | collective-permute-start | bytes 3145736 | tf_op jit(solution)/shard_map/peer_middle/ppermute | solution.py:142
  78.0 20.2 %collective-permute-start.24 = (bf16[256,1024]{1,0:T(8,128)(2,1)S(1)}, bf16[256,1024]{1,0:T(8,128)(2,1)S(1)}, u32[]{:S(2)}, u32[]{:S(2)}) collective-permute-start(bf16[256,1024]{1,0:T(8,128)(2,1)S(1)} %collective-permute-done.23), channel_id=1, source_target_pairs={{4,0},{8,12},{5,1},{9,13},{6,2},{10,14},{7,3},{11,15},{20,16},{24,... | collective-permute-start | bytes 1572872 | tf_op jit(solution)/shard_map/attn_a_ends/ppermute | solution.py:152
  80.8 30.6 %collective-permute-start.22 = (bf16[3,128,2048]{2,1,0:T(8,128)(2,1)S(1)}, bf16[3,128,2048]{2,1,0:T(8,128)(2,1)S(1)}, u32[]{:S(2)}, u32[]{:S(2)}) collective-permute-start(bf16[3,128,2048]{2,1,0:T(8,128)(2,1)S(1)} %pad_maximum_fusion), channel_id=1, source_target_pairs={{0,1},{1,0},{2,3},{3,2},{4,5},{5,4},{6,7},{7,6},{8,9},{9,8},{10,11... | collective-permute-start | bytes 4718600 | tf_op jit(solution)/shard_map/own_s/ppermute | solution.py:128
  91.8 9.4 %collective-permute-start.16 = (bf16[128,2048]{1,0:T(8,128)(2,1)S(1)}, bf16[128,2048]{1,0:T(8,128)(2,1)S(1)}, u32[]{:S(2)}, u32[]{:S(2)}) collective-permute-start(bf16[128,2048]{1,0:T(8,128)(2,1)S(1)} %collective-permute-done.11), channel_id=1, source_target_pairs={{0,1},{1,0},{2,3},{3,2},{4,5},{5,4},{6,7},{7,6},{8,9},{9,8},{10,11... | collective-permute-start | bytes 1572872 | tf_op jit(solution)/shard_map/peer_1s/ppermute | solution.py:128
  98.2 22.7 %collective-permute-start.27 = (bf16[256,1024]{1,0:T(8,128)(2,1)S(1)}, bf16[256,1024]{1,0:T(8,128)(2,1)S(1)}, u32[]{:S(2)}, u32[]{:S(2)}) collective-permute-start(bf16[256,1024]{1,0:T(8,128)(2,1)S(1)} %broadcast_select_fusion.2), channel_id=1, source_target_pairs={{0,2},{2,0},{1,3},{3,1},{4,6},{6,4},{5,7},{7,5},{8,10},{10,8},{9,1... | collective-permute-start | bytes 1572872 | tf_op jit(solution)/shard_map/attn_xb/ppermute | solution.py:128
  101.2 21.1 %collective-permute-start.26 = (bf16[256,1024]{1,0:T(8,128)(2,1)S(1)}, bf16[256,1024]{1,0:T(8,128)(2,1)S(1)}, u32[]{:S(2)}, u32[]{:S(2)}) collective-permute-start(bf16[256,1024]{1,0:T(8,128)(2,1)S(1)} %broadcast_select_fusion.3), channel_id=1, source_target_pairs={{0,2},{2,0},{1,3},{3,1},{4,6},{6,4},{5,7},{7,5},{8,10},{10,8},{9,1... | collective-permute-start | bytes 1572872 | tf_op jit(solution)/shard_map/attn_xa/ppermute | solution.py:128
  101.3 24.3 %collective-permute-start.21 = (bf16[2,128,2048]{2,1,0:T(8,128)(2,1)}, bf16[2,128,2048]{2,1,0:T(8,128)(2,1)}, u32[]{:S(2)}, u32[]{:S(2)}) collective-permute-start(bf16[2,128,2048]{2,1,0:T(8,128)(2,1)} %collective-permute-done.15), channel_id=1, source_target_pairs={{4,0},{8,12},{5,1},{9,13},{6,2},{10,14},{7,3},{11,15},{20,16},{24,... | collective-permute-start | bytes 3145736 | tf_op jit(solution)/shard_map/peer_ends/ppermute | solution.py:152
  102.7 25.6 %collective-permute-start.29 = (bf16[2,128,2048]{2,1,0:T(8,128)(2,1)}, bf16[2,128,2048]{2,1,0:T(8,128)(2,1)}, u32[]{:S(2)}, u32[]{:S(2)}) collective-permute-start(bf16[2,128,2048]{2,1,0:T(8,128)(2,1)} %collective-permute-done.15), channel_id=1, source_target_pairs={{0,1},{1,0},{2,3},{3,2},{4,5},{5,4},{6,7},{7,6},{8,9},{9,8},{10,11... | collective-permute-start | bytes 3145736 | tf_op jit(solution)/shard_map/peer_mid_s/ppermute | solution.py:128
  111.3 20.6 %collective-permute-start.18 = (bf16[64,512]{1,0:T(8,128)(2,1)S(1)}, bf16[64,512]{1,0:T(8,128)(2,1)S(1)}, u32[]{:S(2)}, u32[]{:S(2)}) collective-permute-start(bf16[64,512]{1,0:T(8,128)(2,1)S(1)} %get-tuple-element.94), channel_id=1, source_target_pairs={{4,0},{8,4},{12,8},{5,1},{9,5},{13,9},{6,2},{10,6},{14,10},{7,3},{... | collective-permute-start | bytes 196616 | tf_op jit(solution)/shard_map/grads/ppermute | solution.py:241
  121.0 11.0 %collective-permute-start.19 = (bf16[64,512]{1,0:T(8,128)(2,1)S(1)}, bf16[64,512]{1,0:T(8,128)(2,1)S(1)}, u32[]{:S(2)}, u32[]{:S(2)}) collective-permute-start(bf16[64,512]{1,0:T(8,128)(2,1)S(1)} %get-tuple-element.93), channel_id=1, source_target_pairs={{8,0},{12,4},{9,1},{13,5},{10,2},{14,6},{11,3},{15,7},{24,16},{28,... | collective-permute-start | bytes 196616 | tf_op jit(solution)/shard_map/grads/ppermute | solution.py:241
  122.3 11.0 %collective-permute-start.20 = (bf16[64,512]{1,0:T(8,128)(2,1)S(1)}, bf16[64,512]{1,0:T(8,128)(2,1)S(1)}, u32[]{:S(2)}, u32[]{:S(2)}) collective-permute-start(bf16[64,512]{1,0:T(8,128)(2,1)S(1)} %get-tuple-element.92), channel_id=1, source_target_pairs={{12,0},{13,1},{14,2},{15,3},{28,16},{29,17},{30,18},{31,19}} | collective-permute-start | bytes 196616 | tf_op jit(solution)/shard_map/grads/ppermute | solution.py:241
  125.5 2.9 %collective-permute-start.28 = (bf16[2,128,2048]{2,1,0:T(8,128)(2,1)}, bf16[2,128,2048]{2,1,0:T(8,128)(2,1)S(1)}, u32[]{:S(2)}, u32[]{:S(2)}) collective-permute-start(bf16[2,128,2048]{2,1,0:T(8,128)(2,1)} %collective-permute-done.21), channel_id=1, source_target_pairs={{0,1},{1,0},{2,3},{3,2},{4,5},{5,4},{6,7},{7,6},{8,9},{9,8},{10,11... | collective-permute-start | bytes 3145736 | tf_op jit(solution)/shard_map/peer_end_s/ppermute | solution.py:128
  (8 other events, 76.5 us)
